TPU v7x, 32 devices: a whole 2x2x4 slice. The times are simulated.
32 devices in a mesh: wide: 8 (over z, core), ctx: 4 (over y, x).
Axes of the slice: x: 2, y: 2, z: 4, core: 2. Of those that a mesh axis runs over, the one named last changes fastest.
Arguments:
- residual: float32 [256, 4096], P('wide', 'ctx'), may hold values from -40 to 40
- grad_out: float32 [256, 4096], P('wide', 'ctx'), may hold values from -6 to 6
- norm_gain: float32 [4096], P('ctx'), may hold values from 0.5 to 1.5
- w_gate: float32 [4096, 14336], P('ctx', 'wide'), may hold values from -0.09375 to 0.09375
- w_up: float32 [4096, 14336], P('ctx', 'wide'), may hold values from -0.09375 to 0.09375
- w_down: float32 [14336, 4096], P('wide', 'ctx'), may hold values from -0.046875 to 0.046875
- w_out: float32 [4096, 4096], P('wide', 'ctx'), may hold values from -0.09375 to 0.09375
- queries: float32 [256, 4096], P('ctx', 'wide'), may hold values from -12 to 12
- attn_out: float32 [256, 4096], P('ctx', 'wide'), may hold values from -3 to 3
- log_sum_exp: float32 [32, 256], P('wide', 'ctx')
- key_cache: float32 [8, 4096, 128], P('wide', 'ctx'), may hold values from -16 to 16
- value_cache: float32 [8, 4096, 128], P('wide', 'ctx'), may hold values from -6 to 6
Outputs:
- grad_w_gate: float32 [4096, 14336], P('ctx', 'wide')
- grad_w_up: float32 [4096, 14336], P('ctx', 'wide')
- grad_w_down: float32 [14336, 4096], P('wide', 'ctx')
- grad_w_out: float32 [4096, 4096], P('wide', 'ctx')
- grad_resid: float32 [256, 4096], P('wide', 'ctx')
- grad_queries: float32 [256, 4096], P('ctx', 'wide')
All inputs are finite; a program needn't handle non-finite values.
Results may differ from a plain program's by a relative error of at most 0.0003.
Values sent between devices are 32-bit elements; how exact they have to be, the bound alone decides.
No kernel may reach another device: no remote copies, remote signals or barrier semaphores. Data moves between devices by JAX's collectives and lax.ppermute only.
A program may use at most 128 MiB of HBM per device.

v0:
```python
import math

import jax
import jax.numpy as jnp
from jax import lax
from jax.sharding import PartitionSpec as P

KVH = 8
HD = 128


epsilon = 1e-05
highest = lax.Precision.HIGHEST


def swapped(block, axis, bit):
    count = lax.axis_size(axis)
    route = []
    for low in range(count):
        high = low | 1 << bit
        if high != low and high < count:
            route += [(low, high), (high, low)]
    return lax.ppermute(block, axis, route)


def matmul(left, right):
    return jnp.dot(left, right, precision=highest, preferred_element_type=jnp.float32)


def matmul_tn(left, right):
    return lax.dot_general(
        left, right, (((0,), (0,)), ((), ())), precision=highest, preferred_element_type=jnp.float32
    )


def matmul_nt(left, right):
    return lax.dot_general(
        left, right, (((1,), (1,)), ((), ())), precision=highest, preferred_element_type=jnp.float32
    )


def join_group(own_part, far_part, upper):
    joined = []
    for own_item, far_item, join_dim in zip(own_part, far_part, (1, 1, 0, 0)):
        lower_first = jnp.concatenate((own_item, far_item), axis=join_dim)
        upper_first = jnp.concatenate((far_item, own_item), axis=join_dim)
        joined.append(jnp.where(upper, upper_first, lower_first))
    return tuple(joined)


def halve_group(partial_sums, member, split):
    for bit_index in reversed(range(split.bit_length() - 1)):
        half_width = partial_sums.shape[1] // 2
        upper = member // (1 << bit_index) % 2 == 1
        lower_half = partial_sums[:, :half_width]
        upper_half = partial_sums[:, half_width:]
        kept_half = jnp.where(upper, upper_half, lower_half)
        sent_half = jnp.where(upper, lower_half, upper_half)
        partial_sums = kept_half + swapped(sent_half, "wide", bit_index)
    return partial_sums


def shards(
    residual,
    grad_out,
    norm_gain,
    w_gate,
    w_up,
    w_down,
    w_out,
    queries,
    attn_out,
    log_sum_exp,
    key_cache,
    value_cache,
):
    width = residual.shape[1] * lax.axis_size("ctx")
    all_resid, all_grad = (
        lax.all_gather(residual, "wide", axis=0, tiled=True),
        lax.all_gather(grad_out, "wide", axis=0, tiled=True),
    )
    gained = all_resid * norm_gain[None, :]
    gate_raw, up_raw, d_hidden, squares = lax.psum(
        (
            matmul(gained, w_gate),
            matmul(gained, w_up),
            matmul_nt(all_grad, w_down),
            jnp.sum(all_resid * all_resid, axis=1),
        ),
        "ctx",
    )
    inv_rms = lax.rsqrt(squares / width + epsilon)
    normed = gained * inv_rms[:, None]
    gate_out = gate_raw * inv_rms[:, None]
    up_out = up_raw * inv_rms[:, None]
    sigmoid_gate = jax.nn.sigmoid(gate_out)
    activated = gate_out * sigmoid_gate
    hidden = activated * up_out
    grad_w_down = matmul_tn(hidden, all_grad)
    d_up = d_hidden * activated
    d_gate = d_hidden * up_out * sigmoid_gate * (1.0 + gate_out * (1.0 - sigmoid_gate))
    grad_w_gate = matmul_tn(normed, d_gate)
    grad_w_up = matmul_tn(normed, d_up)
    own_rows = residual.shape[0]
    d_normed = lax.psum_scatter(
        matmul_nt(d_gate, w_gate) + matmul_nt(d_up, w_up), "wide", scatter_dimension=0, tiled=True
    )
    scaled = d_normed * norm_gain[None, :]
    row_dot = lax.psum(jnp.sum(residual * scaled, axis=1), "ctx")
    own_inv = lax.dynamic_slice_in_dim(inv_rms, lax.axis_index("wide") * own_rows, own_rows, 0)
    cubed = own_inv * own_inv * own_inv
    grad_resid = (
        grad_out + own_inv[:, None] * scaled - residual * (cubed * row_dot / width)[:, None]
    )
    gathered_resid = lax.all_gather(grad_resid, "wide", axis=0, tiled=True)
    d_attn = lax.psum_scatter(
        matmul_nt(gathered_resid, w_out), "ctx", scatter_dimension=0, tiled=True
    )
    all_queries, all_outputs, all_dattn, all_lse = (
        lax.all_gather(queries, "ctx", axis=0, tiled=True),
        lax.all_gather(attn_out, "ctx", axis=0, tiled=True),
        lax.all_gather(d_attn, "ctx", axis=0, tiled=True),
        lax.all_gather(log_sum_exp, "ctx", axis=1, tiled=True),
    )
    grad_w_out = matmul_tn(all_outputs, gathered_resid)
    rows_total = all_queries.shape[0]
    head_dim = HD
    local_heads = all_queries.shape[1] // head_dim
    delta = jnp.sum((all_dattn * all_outputs).reshape(rows_total, local_heads, head_dim), axis=2).T
    split = lax.axis_size("wide") // KVH
    member = lax.axis_index("wide") % split
    group = (all_queries, all_dattn, all_lse, delta)
    for bit_index in range(split.bit_length() - 1):
        partner = swapped(group, "wide", bit_index)
        upper = member // (1 << bit_index) % 2 == 1
        group = join_group(group, partner, upper)
    group_queries, group_dattn, group_lse, group_delta = group
    group_count = group_queries.shape[1] // head_dim
    query_rows = (
        group_queries.reshape(rows_total, group_count, head_dim)
        .transpose(1, 0, 2)
        .reshape(group_count * rows_total, head_dim)
    )
    dout_rows = (
        group_dattn.reshape(rows_total, group_count, head_dim)
        .transpose(1, 0, 2)
        .reshape(group_count * rows_total, head_dim)
    )
    lse_rows = group_lse.reshape(group_count * rows_total)
    delta_rows = group_delta.reshape(group_count * rows_total)
    keys_local = key_cache[0]
    values_local = value_cache[0]
    key_count = keys_local.shape[0]
    ctx_count = lax.axis_size("ctx")
    context = key_count * ctx_count * split
    key_base = member * (key_count * ctx_count) + lax.axis_index("ctx") * key_count
    query_pos = jnp.tile(jnp.arange(rows_total, dtype=jnp.int32), group_count) + (
        context - rows_total
    )
    scale = 1.0 / math.sqrt(head_dim)
    block = min(512, key_count)
    accum = jnp.zeros((group_count * rows_total, head_dim), jnp.float32)
    for block_index in range(key_count // block):
        key_block = keys_local[block_index * block : (block_index + 1) * block]
        value_block = values_local[block_index * block : (block_index + 1) * block]
        key_pos = key_base + block_index * block + jnp.arange(block, dtype=jnp.int32)
        scores = matmul_nt(query_rows, key_block) * scale
        probs = jnp.where(
            key_pos[None, :] <= query_pos[:, None], jnp.exp(scores - lse_rows[:, None]), 0.0
        )
        dprobs = matmul_nt(dout_rows, value_block)
        accum = accum + matmul(probs * (dprobs - delta_rows[:, None]), key_block)
    dq_group = (
        (accum * scale)
        .reshape(group_count, rows_total, head_dim)
        .transpose(1, 0, 2)
        .reshape(rows_total, group_count * head_dim)
    )
    summed = lax.psum_scatter(dq_group, "ctx", scatter_dimension=0, tiled=True)
    grad_queries = halve_group(summed, member, split)
    return (grad_w_gate, grad_w_up, grad_w_down, grad_w_out, grad_resid, grad_queries)


def solution(mesh):
    placed = (
        P("wide", "ctx"),
        P("wide", "ctx"),
        P("ctx"),
        P("ctx", "wide"),
        P("ctx", "wide"),
        P("wide", "ctx"),
        P("wide", "ctx"),
        P("ctx", "wide"),
        P("ctx", "wide"),
        P("wide", "ctx"),
        P("wide", "ctx", None),
        P("wide", "ctx", None),
    )
    return jax.shard_map(
        shards,
        mesh=mesh,
        in_specs=placed,
        out_specs=(
            P("ctx", "wide"),
            P("ctx", "wide"),
            P("wide", "ctx"),
            P("wide", "ctx"),
            P("wide", "ctx"),
            P("ctx", "wide"),
        ),
        check_vma=False,
    )
```

profile of v0, /device:TPU:0, one launch (start us, length us, event | category | flops | bytes accessed | tf_op | source)
XLA Modules:
  0.0 382.4 jit_solution(8386128014454703732)
XLA Ops:
  7.2 0.7 all-gather.5.cloned.1.call-update
  7.9 0.0 all-gather.7.cloned.1.call-start
  8.0 0.7 all-gather.7.cloned.1.call-update
  8.7 0.0 all-reduce.3.cloned.1.call-start
  8.7 25.7 %all-gather.5.cloned.1.call-done = f32[256,1024]{1,0:T(8,128)} async-done(((f32[32,1024]{1,0:T(8,128)}), f32[256,1024]{1,0:T(8,128)}) %all-gather.5.cloned.1.call-update) | async-done | bytes 1048592 | tf_op jit(solution)/shard_map/all_gather | solution.py:79
  34.5 10.0 %fusion.46 = f32[256,1792]{1,0:T(8,128)} fusion(f32[1024,1792]{1,0:T(8,128)} %param.16, f32[256,1024]{1,0:T(8,128)} %all-gather.5.cloned.1.call-done, f32[1024]{0:T(1024)} %param.14), kind=kOutput, calls=%fused_computation.47 | convolution fusion | flops 5637406720 | bytes 10227712 | tf_op jit(solution)/shard_map/dot_general | solution.py:27
  44.5 7.6 %fusion.44 = f32[256,1792]{1,0:T(8,128)} fusion(f32[1024,1792]{1,0:T(8,128)S(1)} %copy-done.11, f32[256,1024]{1,0:T(8,128)S(1)} %copy-done.4, f32[1024]{0:T(1024)S(1)} %copy-done.17), kind=kOutput, calls=%fused_computation.45 | convolution fusion | flops 5637406720 | bytes 10227712 | tf_op jit(solution)/shard_map/dot_general | solution.py:27
  52.1 5.7 %all-gather.7.cloned.1.call-done = f32[256,1024]{1,0:T(8,128)} async-done(((f32[32,1024]{1,0:T(8,128)}), f32[256,1024]{1,0:T(8,128)}) %all-gather.7.cloned.1.call-update) | async-done | bytes 1048592 | tf_op jit(solution)/shard_map/all_gather | solution.py:80
  57.8 10.1 %fusion.83 = f32[256,1792]{1,0:T(8,128)} fusion(f32[256,1024]{1,0:T(8,128)} %all-gather.7.cloned.1.call-done, f32[1792,1024]{1,0:T(8,128)} %param.17), kind=kOutput, calls=%fused_computation.90 | convolution fusion | flops 5637144576 | bytes 10223616 | tf_op jit(solution)/shard_map/dot_general | solution.py:37
  67.9 0.0 reduce-scatter.4.cloned.1.call-start
  68.0 0.1 multiply_reduce_fusion
  68.1 10.0 %psum.35 = f32[256]{0:T(256)S(1)} all-reduce(f32[256]{0:T(256)S(1)} %multiply_reduce_fusion), channel_id=1, replica_groups=mesh['wide'=8,'ctx'=4] {'ctx'}, use_global_device_ids=true, to_apply=%region_1.0 | all-reduce | flops 256 | bytes 2048 | tf_op jit(solution)/shard_map/psum | solution.py:83
  78.1 115.8 %all-reduce.3.cloned.1.call-done = (f32[256,1792]{1,0:T(8,128)}, f32[256,1792]{1,0:T(8,128)}, f32[256,1792]{1,0:T(8,128)}) async-done(((f32[256,1792]{1,0:T(8,128)}, f32[256,1792]{1,0:T(8,128)}, f32[256,1792]{1,0:T(8,128)}), (f32[256,1792]{1,0:T(8,128)}, f32[256,1792]{1,0:T(8,128)}, f32[256,1792]{1,0:T(8,128)})) %all-reduce.3.cloned.1.call-update) | async-done | bytes 5505040 | tf_op jit(solution)/shard_map/psum | solution.py:83
  193.9 11.9 %fusion.82 = f32[256,1024]{1,0:T(8,128)S(1)} fusion(f32[1024,1792]{1,0:T(8,128)} %param.15, f32[256,1792]{1,0:T(8,128)} %get-tuple-element.30, f32[256,1792]{1,0:T(8,128)} %get-tuple-element.31, f32[256,1792]{1,0:T(8,128)} %get-tuple-element.32, f32[256]{0:T(256)S(1)} %add_rsqrt_fusion), kind=kOutput, calls=%fused_computation.89 | convolution fusion | flops 5642190848 | bytes 13894656 | tf_op jit(solution)/shard_map/dot_general | solution.py:37
  205.9 10.3 %convolution_add_fusion = f32[256,1024]{1,0:T(8,128)} fusion(f32[256,1024]{1,0:T(8,128)S(1)} %fusion.82, f32[1024,1792]{1,0:T(8,128)} %param.16, f32[256,1792]{1,0:T(8,128)S(1)} %copy-done.5, f32[256,1792]{1,0:T(8,128)S(1)} %copy-done.2, f32[256]{0:T(256)S(1)} %add_rsqrt_fusion), kind=kOutput, calls=%fused_computation.23 | convolution fusion | flops 5640159232 | bytes 13108224 | tf_op jit(solution)/shard_map/dot_general | solution.py:37
  216.2 0.0 all-gather.9.cloned.1.call-start
  216.3 32.4 %reduce-scatter.4.cloned.1.call-done = f32[32,1024]{1,0:T(8,128)} async-done(((f32[256,1024]{1,0:T(8,128)}), f32[32,1024]{1,0:T(8,128)}) %reduce-scatter.4.cloned.1.call-update) | async-done | bytes 131088 | tf_op jit(solution)/shard_map/reduce_scatter | solution.py:105
  248.7 1.0 multiply_reduce_fusion.1
  249.8 10.3 %psum.39 = f32[32]{0:T(128)} all-reduce(f32[32]{0:T(128)S(1)} %multiply_reduce_fusion.1), channel_id=1, replica_groups=mesh['wide'=8,'ctx'=4] {'ctx'}, use_global_device_ids=true, to_apply=%region_7.0 | all-reduce | flops 32 | bytes 256 | tf_op jit(solution)/shard_map/psum | solution.py:109
  260.1 0.7 fusion.74
  260.8 1.6 multiply_subtract_fusion
  262.5 0.0 reduce-scatter.6.cloned.1.call-start
  262.6 7.3 %all-gather = f32[4,64,4]{1,2,0:T(4,128)S(1)} all-gather(f32[1,64,4]{1,2,0:T(4,128)S(1)} %bitcast.82), channel_id=1, replica_groups=mesh['wide'=8,'ctx'=4] {'ctx'}, dimensions={0}, use_global_device_ids=true | all-gather | bytes 5120 | tf_op jit(solution)/shard_map/all_gather | solution.py:123
  269.9 0.1 reshape.66
  270.0 10.6 %all_gather.25 = f32[256,512]{1,0:T(8,128)} all-gather(f32[64,512]{1,0:T(8,128)S(1)} %copy-done.20), channel_id=1, replica_groups=mesh['wide'=8,'ctx'=4] {'ctx'}, dimensions={0}, use_global_device_ids=true | all-gather | bytes 655360 | tf_op jit(solution)/shard_map/all_gather | solution.py:120
  280.6 2.0 copy.30
  282.6 2.0 copy.31
  284.7 10.2 %all_gather.24 = f32[256,512]{1,0:T(8,128)} all-gather(f32[64,512]{1,0:T(8,128)S(1)} %copy-done.21), channel_id=1, replica_groups=mesh['wide'=8,'ctx'=4] {'ctx'}, dimensions={0}, use_global_device_ids=true | all-gather | bytes 655360 | tf_op jit(solution)/shard_map/all_gather | solution.py:121
  295.0 4.0 %fusion.84 = f32[256,512]{1,0:T(8,128)} fusion(f32[256,1024]{1,0:T(8,128)} %all-gather.9.cloned.1.call-done, f32[512,1024]{1,0:T(8,128)S(1)} %copy-done), kind=kOutput, calls=%fused_computation.91 | convolution fusion | flops 1610612736 | bytes 3670016 | tf_op jit(solution)/shard_map/dot_general | solution.py:37
  298.9 0.0 reduce-scatter.8.cloned.1.call-start
  299.0 4.4 %fusion.60 = f32[1024,512]{1,0:T(8,128)} fusion(f32[1024,128]{1,0:T(8,128)} %bitcast.66, f32[1,1024,128]{2,1,0:T(8,128)} %param.22), kind=kOutput, calls=%fused_computation.63 | convolution fusion | flops 805306368 | bytes 2883584 | tf_op jit(solution)/shard_map/dot_general | solution.py:37
  303.4 4.4 %fusion.65 = f32[1024,512]{1,0:T(8,128)} fusion(f32[1024,128]{1,0:T(8,128)} %bitcast.67, f32[1,1024,128]{2,1,0:T(8,128)} %param.22), kind=kOutput, calls=%fused_computation.68 | convolution fusion | flops 805306368 | bytes 2883584 | tf_op jit(solution)/shard_map/dot_general | solution.py:37
  307.8 9.0 %fusion.38 = f32[1024,1792]{1,0:T(8,128)} fusion(f32[256,1024]{1,0:T(8,128)S(1)} %copy-done.4, f32[256,1792]{1,0:T(8,128)S(1)} %copy-done.6, f32[256]{0:T(256)S(1)} %add_rsqrt_fusion, f32[1024]{0:T(1024)S(1)} %copy-done.17, f32[256,1792]{1,0:T(8,128)S(1)} %copy-done.3), kind=kOutput, calls=%fused_computation.39 | convolution fusion | flops 5640421376 | bytes 12063744 | tf_op jit(solution)/shard_map/dot_general | solution.py:31
  316.8 4.3 %reduce-scatter.6.cloned.1.call-done = f32[64,512]{1,0:T(8,128)} async-done(((f32[256,512]{1,0:T(8,128)}), f32[64,512]{1,0:T(8,128)}) %reduce-scatter.6.cloned.1.call-update) | async-done | bytes 131088 | tf_op jit(solution)/shard_map/reduce_scatter | solution.py:116
  321.1 10.1 %all_gather.27 = f32[256,512]{1,0:T(8,128)S(1)} all-gather(f32[64,512]{1,0:T(8,128)} %reduce-scatter.6.cloned.1.call-done), channel_id=1, replica_groups=mesh['wide'=8,'ctx'=4] {'ctx'}, dimensions={0}, use_global_device_ids=true | all-gather | bytes 655360 | tf_op jit(solution)/shard_map/all_gather | solution.py:122
  331.3 3.1 fusion.57
  334.4 3.1 fusion.62
  337.5 0.9 mul.146
  338.4 2.0 reshape.62
  340.4 1.4 reduce_sum.29
  341.8 0.1 copy.34
  341.9 4.5 %fusion = f32[1024,128]{1,0:T(8,128)S(1)} fusion(f32[1024,512]{1,0:T(8,128)} %fusion.57, f32[1024,512]{1,0:T(8,128)} %fusion.60, s32[512]{0:T(512)S(1)} %iota_add_fusion, f32[1024]{0:T(1024)S(1)} %bitcast.78, f32[1024]{0:T(1024)S(1)} %bitcast.76, s32[1024]{0:T(1024)S(1)} %bitcast.74, f32[1,1024,128]{2,1,0:T(8,128)} %param.22), kind=kOutput, calls=%fused_computation | convolution fusion | flops 808452096 | bytes 4995072 | tf_op jit(solution)/shard_map/dot_general | solution.py:27
  346.4 2.2 fusion.23
  348.6 0.9 copy.44
  349.6 10.2 %fusion.16 = f32[1792,1024]{1,0:T(8,128)} fusion(f32[256,1024]{1,0:T(8,128)} %all-gather.7.cloned.1.call-done, f32[256,1792]{1,0:T(8,128)} %get-tuple-element.32, f32[256]{0:T(256)S(1)} %add_rsqrt_fusion, f32[256,1792]{1,0:T(8,128)S(1)} %copy-done.3), kind=kOutput, calls=%fused_computation.16 | convolution fusion | flops 5640355840 | bytes 12059648 | tf_op jit(solution)/shard_map/dot_general | solution.py:31
  359.7 9.6 %fusion.40 = f32[1024,1792]{1,0:T(8,128)} fusion(f32[256,1024]{1,0:T(8,128)S(1)} %copy-done.4, f32[256]{0:T(256)S(1)} %add_rsqrt_fusion, f32[1024]{0:T(1024)S(1)} %copy-done.17, f32[256,1792]{1,0:T(8,128)S(1)} %copy-done.7, f32[256,1792]{1,0:T(8,128)S(1)} %copy-done.3, f32[256,1792]{1,0:T(8,128)S(1)} %copy-done.8), kind=kOutput, calls=%fused_computation.41 | convolution fusion | flops 5642715136 | bytes 13898752 | tf_op jit(solution)/shard_map/dot_general | solution.py:31
  369.3 3.2 convolution_bitcast_fusion
  372.5 2.9 copy.36
  (63 shorter events, 0.3 us)
Async XLA Ops:
  7.2 287.8 %copy-start = (f32[512,1024]{1,0:T(8,128)S(1)}, f32[512,1024]{1,0:T(8,128)}, u32[]{:S(2)}) copy-start(f32[512,1024]{1,0:T(8,128)} %param.18) | copy-start | bytes 6291460
  7.2 27.3 %all-gather.5.cloned.1.call-start = ((), (), s32[]{:S(2)}) async-start(), calls=%async_computation.3 | async-start | bytes 1179648 | tf_op jit(solution)/shard_map/all_gather | solution.py:79
  7.9 49.9 %all-gather.7.cloned.1.call-start = ((), (), s32[]{:S(2)}) async-start(), calls=%async_computation.4 | async-start | bytes 1179648 | tf_op jit(solution)/shard_map/all_gather | solution.py:80
  8.7 35.8 %copy-start.17 = (f32[1024]{0:T(1024)S(1)}, f32[1024]{0:T(1024)}, u32[]{:S(2)}) copy-start(f32[1024]{0:T(1024)} %param.14) | copy-start | bytes 12292
  8.7 185.2 %all-reduce.3.cloned.1.call-start = ((), (), s32[]{:S(2)}) async-start(), calls=%async_computation.9 | async-start | bytes 11010048 | tf_op jit(solution)/shard_map/psum | solution.py:83
  34.5 10.0 %copy-start.4 = (f32[256,1024]{1,0:T(8,128)S(1)}, f32[256,1024]{1,0:T(8,128)}, u32[]{:S(2)}) copy-start(f32[256,1024]{1,0:T(8,128)} %all-gather.5.cloned.1.call-done) | copy-start | bytes 3145732
  34.5 10.0 %copy-start.11 = (f32[1024,1792]{1,0:T(8,128)S(1)}, f32[1024,1792]{1,0:T(8,128)}, u32[]{:S(2)}) copy-start(f32[1024,1792]{1,0:T(8,128)} %param.15) | copy-start | bytes 22020100
  67.9 180.8 %reduce-scatter.4.cloned.1.call-start = ((), (), s32[]{:S(2)}) async-start(), calls=%async_computation.5 | async-start | bytes 1179648 | tf_op jit(solution)/shard_map/reduce_scatter | solution.py:105
  193.9 11.9 %copy-start.2 = (f32[256,1792]{1,0:T(8,128)S(1)}, f32[256,1792]{1,0:T(8,128)}, u32[]{:S(2)}) copy-start(f32[256,1792]{1,0:T(8,128)} %get-tuple-element.31) | copy-start | bytes 5505028
  193.9 12.0 %copy-start.5 = (f32[256,1792]{1,0:T(8,128)S(1)}, f32[256,1792]{1,0:T(8,128)}, u32[]{:S(2)}) copy-start(f32[256,1792]{1,0:T(8,128)} %get-tuple-element.30) | copy-start | bytes 5505028
  205.9 42.9 %copy-start.16 = (f32[32,1024]{1,0:T(8,128)S(1)}, f32[32,1024]{1,0:T(8,128)}, u32[]{:S(2)}) copy-start(f32[32,1024]{1,0:T(8,128)} %param.12) | copy-start | bytes 393220
  205.9 55.0 %copy-start.18 = (f32[32,1024]{1,0:T(8,128)S(1)}, f32[32,1024]{1,0:T(8,128)}, u32[]{:S(2)}) copy-start(f32[32,1024]{1,0:T(8,128)} %param.13) | copy-start | bytes 393220
  216.2 46.4 %copy-start.22 = (f32[4,64]{1,0:T(4,128)S(1)}, f32[4,64]{1,0:T(4,128)}, u32[]{:S(2)}) copy-start(f32[4,64]{1,0:T(4,128)} %param.21) | copy-start | bytes 3076
  216.2 53.7 %copy-start.20 = (f32[64,512]{1,0:T(8,128)S(1)}, f32[64,512]{1,0:T(8,128)}, u32[]{:S(2)}) copy-start(f32[64,512]{1,0:T(8,128)} %param.19) | copy-start | bytes 393220
  216.2 78.7 %all-gather.9.cloned.1.call-start = ((), (), s32[]{:S(2)}) async-start(), calls=%async_computation.6 | async-start | bytes 1179648 | tf_op jit(solution)/shard_map/all_gather | solution.py:115
  262.5 22.2 %copy-start.21 = (f32[64,512]{1,0:T(8,128)S(1)}, f32[64,512]{1,0:T(8,128)}, u32[]{:S(2)}) copy-start(f32[64,512]{1,0:T(8,128)} %param.20) | copy-start | bytes 393220
  262.5 58.6 %reduce-scatter.6.cloned.1.call-start = ((), (), s32[]{:S(2)}) async-start(), calls=%async_computation.7 | async-start | bytes 655360 | tf_op jit(solution)/shard_map/reduce_scatter | solution.py:116
  298.9 76.4 %reduce-scatter.8.cloned.1.call-start = ((), (), s32[]{:S(2)}) async-start(), calls=%async_computation.8 | async-start | bytes 655360 | tf_op jit(solution)/shard_map/reduce_scatter | solution.py:179
  299.0 8.7 %copy-start.6 = (f32[256,1792]{1,0:T(8,128)S(1)}, f32[256,1792]{1,0:T(8,128)}, u32[]{:S(2)}) copy-start(f32[256,1792]{1,0:T(8,128)} %get-tuple-element.30) | copy-start | bytes 5505028
  303.4 4.4 %copy-start.3 = (f32[256,1792]{1,0:T(8,128)S(1)}, f32[256,1792]{1,0:T(8,128)}, u32[]{:S(2)}) copy-start(f32[256,1792]{1,0:T(8,128)} %get-tuple-element.31) | copy-start | bytes 5505028
  321.1 10.1 %copy-start.19 = (f32[1,1024,128]{2,1,0:T(8,128)S(1)}, f32[1,1024,128]{2,1,0:T(8,128)}, u32[]{:S(2)}) copy-start(f32[1,1024,128]{2,1,0:T(8,128)} %param.23) | copy-start | bytes 1572868
  334.4 3.1 copy-start.12
  341.8 4.5 %copy-start.9 = (f32[1024,512]{1,0:T(8,128)S(1)}, f32[1024,512]{1,0:T(8,128)}, u32[]{:S(2)}) copy-start(f32[1024,512]{1,0:T(8,128)} %fusion.65) | copy-start | bytes 6291460
  341.8 4.5 %copy-start.10 = (f32[1024,512]{1,0:T(8,128)S(1)}, f32[1024,512]{1,0:T(8,128)}, u32[]{:S(2)}) copy-start(f32[1024,512]{1,0:T(8,128)} %fusion.62) | copy-start | bytes 6291460
  341.9 4.5 %copy-start.15 = (f32[1,1024,128]{2,1,0:T(8,128)S(1)}, f32[1,1024,128]{2,1,0:T(8,128)}, u32[]{:S(2)}) copy-start(f32[1,1024,128]{2,1,0:T(8,128)} %param.22) | copy-start | bytes 1572868
  349.5 10.2 %copy-start.7 = (f32[256,1792]{1,0:T(8,128)S(1)}, f32[256,1792]{1,0:T(8,128)}, u32[]{:S(2)}) copy-start(f32[256,1792]{1,0:T(8,128)} %get-tuple-element.30) | copy-start | bytes 5505028
  349.5 10.2 %copy-start.8 = (f32[256,1792]{1,0:T(8,128)S(1)}, f32[256,1792]{1,0:T(8,128)}, u32[]{:S(2)}) copy-start(f32[256,1792]{1,0:T(8,128)} %get-tuple-element.32) | copy-start | bytes 5505028
  359.7 9.6 %copy-start.13 = (f32[256,512]{1,0:T(8,128)S(1)}, f32[256,512]{1,0:T(8,128)}, u32[]{:S(2)}) copy-start(f32[256,512]{1,0:T(8,128)} %all_gather.24) | copy-start | bytes 1572868
  359.7 9.6 %copy-start.14 = (f32[256,1024]{1,0:T(8,128)S(1)}, f32[256,1024]{1,0:T(8,128)}, u32[]{:S(2)}) copy-start(f32[256,1024]{1,0:T(8,128)} %all-gather.9.cloned.1.call-done) | copy-start | bytes 3145732
  369.3 6.1 %copy-start.1 = (f32[512,1024]{1,0:T(8,128)S(1)}, f32[512,1024]{1,0:T(8,128)}, u32[]{:S(2)}) copy-start(f32[512,1024]{1,0:T(8,128)} %param.18) | copy-start | bytes 6291460
Sparse Core Ops, SparseCore 0:
  9.6 24.7 all-gather.4
  36.0 21.7 all-gather.6
  68.0 125.8 all-reduce.2
  216.4 32.3 reduce-scatter.3
  262.6 18.5 all-gather.8
  299.1 21.9 reduce-scatter.5
  349.7 24.7 reduce-scatter.7
where the time goes:
time: 390 us; the launch traced here: 382 us
  waiting for transfers between devices  186 us (48%)
  matrix products  108 us (28%)
  blocking collectives  58.5 us (15%)
  between operations  14.6 us (4%)
  local copies, waits for them, and re-layouts  10.1 us (3%)
  other arithmetic  5.85 us (2%)
    psum x1, waiting for transfers between devices, shards(): lax.psum((matmul(gained, w_gate), matmul(gained, w_up), matmul_nt(all_gra...  116 us
    dot_general x8, matrix products, matmul_nt(): lax.dot_general(left, right, (((1,), (1,)), ((), ())), precision=highest,...  51.3 us
    reduce_scatter x1, waiting for transfers between devices, shards(): lax.psum_scatter(matmul_nt(d_gate, w_gate) + matmul_nt(d_up, w_up), 'wide...  32.4 us
    dot_general x4, matrix products, matmul_tn(): lax.dot_general(left, right, (((0,), (0,)), ((), ())), precision=highest,...  31.9 us
    all_gather x1, waiting for transfers between devices, shards(): lax.all_gather(residual, 'wide', axis=0, tiled=True)  25.7 us
    dot_general x4, matrix products, matmul(): jnp.dot(left, right, precision=highest, preferred_element_type=jnp.float32)  24.4 us
    all_gather x1, blocking collectives, shards(): lax.all_gather(queries, 'ctx', axis=0, tiled=True)  10.6 us
    psum x1, blocking collectives, shards(): row_dot = lax.psum(jnp.sum(residual * scaled, axis=1), 'ctx')  10.3 us
  transfers between devices with their start and end apart: 7, of which 5 were waited for; matrix products, arithmetic and copies ran while one was open for 17% of the time, Pallas kernels for 0%

commit v1 on v0

--- a/solution.py
+++ b/solution.py
@@ -1,8 +1,11 @@
+import functools
 import math
 
 import jax
 import jax.numpy as jnp
 from jax import lax
+from jax.experimental import pallas as pl
+from jax.experimental.pallas import tpu as pltpu
 from jax.sharding import PartitionSpec as P
 
 KVH = 8
@@ -11,6 +14,776 @@
 
 epsilon = 1e-05
 highest = lax.Precision.HIGHEST
+f32 = jnp.float32
+bf16 = jnp.bfloat16
+LANES = 128
+TILE = 256
+VMEM_LIMIT = 16 * 1024 * 1024
+VMEM_MOST = 60 * 1024 * 1024
+NN = (((1,), (0,)), ((), ()))
+NT = (((1,), (1,)), ((), ()))
+TN = (((0,), (0,)), ((), ()))
+
+
+def flip(block, axis, mask):
+    count = lax.axis_size(axis)
+    return lax.ppermute(block, axis, [(at, at ^ mask) for at in range(count)])
+
+
+def pieces(values):
+    high = values.astype(bf16)
+    return high, (values - high.astype(f32)).astype(bf16)
+
+
+def dot(left, right, dims):
+    return lax.dot_general(left, right, dims, preferred_element_type=f32)
+
+
+def dot3(left, right, dims):
+    left_high, left_low = left
+    right_high, right_low = right
+    return (
+        dot(left_high, right_high, dims)
+        + dot(left_low, right_high, dims)
+        + dot(left_high, right_low, dims)
+    )
+
+
+class Chain:
+    def __init__(self):
+        self.links = []
+
+    def wait(self, *arrays):
+        self.links += arrays
+
+
+def call(
+    name,
+    kernel,
+    grid,
+    in_specs,
+    out_specs,
+    out_shape,
+    scratch=(),
+    flops=0,
+    moved=0,
+    after=None,
+    limit=VMEM_LIMIT,
+):
+    count, waits, outs = len(in_specs), len(after.links), len(out_specs)
+
+    def body(*refs):
+        link = refs[count + waits + outs]
+        link[...] = jnp.zeros_like(link)
+        kernel(*refs[:count], *refs[count + waits : count + waits + outs], *refs[count + waits + outs + 1 :])
+
+    run = pl.pallas_call(
+        body,
+        name=name,
+        grid=grid,
+        in_specs=list(in_specs) + [pl.BlockSpec(memory_space=pl.ANY)] * waits,
+        out_specs=list(out_specs) + [whole((8, LANES))],
+        out_shape=list(out_shape) + [shape_of(8, LANES)],
+        scratch_shapes=list(scratch),
+        compiler_params=pltpu.CompilerParams(vmem_limit_bytes=limit),
+        cost_estimate=pl.CostEstimate(flops=4 * flops, bytes_accessed=4 * moved, transcendentals=0),
+    )
+
+    def apply(*operands):
+        *results, link = run(*operands, *after.links)
+        after.links = [link]
+        return results if len(results) > 1 else results[0]
+
+    return apply
+
+
+def ordered(array, *earlier):
+    anywhere = pl.BlockSpec(memory_space=pl.ANY)
+    return pl.pallas_call(
+        lambda *refs: None,
+        name="ordered",
+        in_specs=[anywhere] * (1 + len(earlier)),
+        out_specs=anywhere,
+        out_shape=jax.ShapeDtypeStruct(array.shape, array.dtype),
+        input_output_aliases={0: 0},
+    )(array, *earlier)
+
+
+def whole(shape):
+    return pl.BlockSpec(shape, lambda *_: (0,) * len(shape))
+
+
+def shape_of(*shape, dtype=f32):
+    return jax.ShapeDtypeStruct(shape, dtype)
+
+
+def partial_kernel(orders, *refs):
+    units = len(orders)
+    sources = refs[: 2 * units]
+    gain, w_gate, w_up, w_down = refs[2 * units : 2 * units + 4]
+    results = refs[2 * units + 4 : -2]
+    x_parts, g_parts = refs[-2:]
+    step = pl.program_id(0)
+    width = gain.shape[1]
+    count = results[2].shape[0]
+    total = units * count
+    hidden = (results[0].shape[1] - LANES) // 3
+
+    @pl.when(step == 0)
+    def _():
+        for unit, order in enumerate(orders):
+            own, far = sources[2 * unit : 2 * unit + 2]
+            keep, send, rows = results[3 * unit : 3 * unit + 3]
+            cut = count // len(order)
+            for at, rel in enumerate(order):
+                piece = pl.ds(rel * cut // 2, cut // 2)
+                rows[pl.ds(at * cut, cut // 2), :] = own[piece, :]
+                rows[pl.ds(at * cut + cut // 2, cut // 2), :] = far[piece, :]
+            resid = rows[:, :width]
+            squares = jnp.broadcast_to(
+                jnp.sum(resid * resid, axis=1, keepdims=True), (count, LANES)
+            )
+            keep[:, pl.ds(3 * hidden, LANES)] = squares[: count // 2]
+            send[:, pl.ds(3 * hidden, LANES)] = squares[count // 2 :]
+            gained = resid * gain[...]
+            rows[:, :width] = gained
+            for parts, values in ((x_parts, gained), (g_parts, rows[:, width:])):
+                high, low = pieces(values)
+                parts[pl.ds(unit * count, count), :] = high
+                parts[pl.ds(total + unit * count, count), :] = low
+
+    at = pl.multiple_of(step * TILE, TILE)
+    for section, parts, weight, dims in (
+        (0, x_parts, w_gate, NN),
+        (1, x_parts, w_up, NN),
+        (2, g_parts, w_down, NT),
+    ):
+        high, low = pieces(weight[...])
+        both = dot(parts[...], high, dims)
+        value = both[:total] + both[total:] + dot(parts[:total, :], low, dims)
+        place = pl.ds(section * hidden + at, TILE)
+        for unit in range(units):
+            keep, send = results[3 * unit : 3 * unit + 2]
+            start = unit * count
+            keep[:, place] = value[start : start + count // 2]
+            send[:, place] = value[start + count // 2 : start + count]
+
+
+def partial_sums(orders, sources, gain, w_gate, w_up, w_down, after):
+    width, hidden = w_gate.shape
+    own_shape = sources[0][0].shape
+    count = 2 * own_shape[0]
+    total = count * len(orders)
+    half = (count // 2, 3 * hidden + LANES)
+    both = (count, 2 * width)
+    flat = [item for pair in sources for item in pair]
+    results = call(
+        "partial",
+        functools.partial(partial_kernel, orders),
+        (hidden // TILE,),
+        [whole(own_shape)] * len(flat)
+        + [
+            whole((1, width)),
+            pl.BlockSpec((width, TILE), lambda j: (0, j)),
+            pl.BlockSpec((width, TILE), lambda j: (0, j)),
+            pl.BlockSpec((TILE, width), lambda j: (j, 0)),
+        ],
+        [whole(half), whole(half), whole(both)] * len(orders),
+        [shape_of(*half), shape_of(*half), shape_of(*both)] * len(orders),
+        [pltpu.VMEM((2 * total, width), bf16), pltpu.VMEM((2 * total, width), bf16)],
+        flops=18 * total * width * hidden,
+        moved=12 * width * hidden,
+        after=after,
+        limit=VMEM_MOST,
+    )(*flat, gain, w_gate, w_up, w_down)
+    return [results[3 * unit : 3 * unit + 3] for unit in range(len(orders))]
+
+
+def fold_kernel(kept, got, keep, send):
+    half = keep.shape[0]
+    keep[...] = kept[:half, :] + got[:half, :]
+    send[...] = kept[half:, :] + got[half:, :]
+
+
+def fold(kept, got, after):
+    rows, columns = kept.shape
+    half = (rows // 2, columns)
+    return call(
+        "fold",
+        fold_kernel,
+        (1,),
+        [whole(kept.shape)] * 2,
+        [whole(half)] * 2,
+        [shape_of(*half)] * 2,
+        flops=rows * columns,
+        moved=12 * rows * columns,
+        after=after,
+    )(kept, got)
+
+
+def join_kernel(one, other, out):
+    out[...] = one[...] + other[...]
+
+
+def join(one, other, after):
+    return call(
+        "join",
+        join_kernel,
+        (1,),
+        [whole(one.shape)] * 2,
+        [whole(one.shape)],
+        [shape_of(*one.shape)],
+        moved=12 * one.size,
+        after=after,
+    )(one, other)
+
+
+def middle_kernel(width, kept, got, out):
+    hidden = (out.shape[1] - LANES) // 3
+    gate_at, up_at, down_at = (pl.ds(part * hidden, hidden) for part in range(3))
+    rest = pl.ds(3 * hidden, LANES)
+    squares = (kept[:, rest] + got[:, rest])[:, :1]
+    inv_rms = lax.rsqrt(squares / width + epsilon)
+    gate_raw = kept[:, gate_at] + got[:, gate_at]
+    up_raw = kept[:, up_at] + got[:, up_at]
+    d_hidden = kept[:, down_at] + got[:, down_at]
+    gate_out = gate_raw * inv_rms
+    up_out = up_raw * inv_rms
+    sigmoid_gate = jax.nn.sigmoid(gate_out)
+    activated = gate_out * sigmoid_gate
+    d_up = d_hidden * activated * inv_rms
+    d_gate = d_hidden * up_out * sigmoid_gate * (1.0 + gate_out * (1.0 - sigmoid_gate)) * inv_rms
+    out[:, gate_at] = d_gate
+    out[:, up_at] = d_up
+    out[:, down_at] = activated * up_out
+    row_sum = jnp.sum(d_gate * gate_raw + d_up * up_raw, axis=1, keepdims=True)
+    out[:, rest] = jnp.broadcast_to(row_sum * (inv_rms * inv_rms / width), (out.shape[0], LANES))
+
+
+def middle(width, kept, got, after):
+    rows, columns = kept.shape
+    return call(
+        "middle",
+        functools.partial(middle_kernel, float(width)),
+        (1,),
+        [whole(kept.shape)] * 2,
+        [whole(kept.shape)],
+        [shape_of(rows, columns)],
+        flops=20 * rows * columns,
+        moved=12 * rows * columns,
+        after=after,
+    )(kept, got)
+
+
+def normed_kernel(order, *refs):
+    blocks = refs[: len(order)]
+    w_gate, w_up, own, far, split, parts = refs[len(order) :]
+    step = pl.program_id(0)
+    cut = blocks[0].shape[0]
+    count = cut * len(order)
+    hidden = w_gate.shape[1]
+    width = own.shape[1] - LANES
+
+    @pl.when(step == 0)
+    def _():
+        for at, block in enumerate(blocks):
+            high, low = pieces(block[:, : 3 * hidden])
+            split[0, pl.ds(at * cut, cut), :] = high
+            split[1, pl.ds(at * cut, cut), :] = low
+            for section in range(2):
+                columns = slice(section * hidden, (section + 1) * hidden)
+                parts[section, pl.ds(at * cut, cut), :] = high[:, columns]
+                parts[section, pl.ds(count + at * cut, cut), :] = low[:, columns]
+            terms = block[:, pl.ds(3 * hidden, LANES)]
+            piece = pl.ds(order[at] * cut // 2, cut // 2)
+            own[piece, pl.ds(width, LANES)] = terms[: cut // 2]
+            far[piece, pl.ds(width, LANES)] = terms[cut // 2 :]
+
+    total = jnp.zeros((count, TILE), f32)
+    for section, weight in ((0, w_gate), (1, w_up)):
+        high, low = pieces(weight[...])
+        both = dot(parts[section], high, NT)
+        total += both[:count] + both[count:] + dot(parts[section, :count, :], low, NT)
+    place = pl.ds(pl.multiple_of(step * TILE, TILE), TILE)
+    for at, rel in enumerate(order):
+        piece = pl.ds(rel * cut // 2, cut // 2)
+        own[piece, place] = total[at * cut : at * cut + cut // 2]
+        far[piece, place] = total[at * cut + cut // 2 : (at + 1) * cut]
+
+
+def normed_sums(order, blocks, w_gate, w_up, after):
+    width, hidden = w_gate.shape
+    cut = blocks[0].shape[0]
+    count = cut * len(order)
+    half = (count // 2, width + LANES)
+    weight = pl.BlockSpec((TILE, hidden), lambda j: (j, 0))
+    return call(
+        "normed",
+        functools.partial(normed_kernel, order),
+        (width // TILE,),
+        [whole(blocks[0].shape)] * len(order) + [weight, weight],
+        [whole(half), whole(half), whole((2, count, 3 * hidden))],
+        [shape_of(*half), shape_of(*half), shape_of(2, count, 3 * hidden, dtype=bf16)],
+        [pltpu.VMEM((2, 2 * count, hidden), bf16)],
+        flops=12 * count * width * hidden,
+        moved=8 * width * hidden,
+        after=after,
+    )(*blocks, w_gate, w_up)
+
+
+def collect_kernel(*refs):
+    rows, left, right = refs[:-2], refs[-2], refs[-1]
+    width = right.shape[2]
+    gained = jnp.concatenate([item[:, :width] for item in rows], axis=0)
+    left[0], left[1] = pieces(gained.T)
+    right[0], right[1] = pieces(jnp.concatenate([item[:, width:] for item in rows], axis=0))
+
+
+def collect(rows, after):
+    total, width = sum(item.shape[0] for item in rows), rows[0].shape[1] // 2
+    return call(
+        "collect",
+        collect_kernel,
+        (1,),
+        [whole(item.shape) for item in rows],
+        [whole((2, width, total)), whole((2, total, width))],
+        [shape_of(2, width, total, dtype=bf16), shape_of(2, total, width, dtype=bf16)],
+        moved=16 * total * width,
+        after=after,
+        limit=VMEM_MOST,
+    )(*rows)
+
+
+def weight_kernel(flipped, rows, *refs):
+    splits, out = refs[:-1], refs[-1]
+    high = jnp.concatenate([split[0] for split in splits], axis=0)
+    low = jnp.concatenate([split[1] for split in splits], axis=0)
+    held = (rows[0], rows[1])
+    out[...] = dot3((high, low), held, TN) if flipped else dot3(held, (high, low), NN)
+
+
+def weight_grad(section, rows, splits, hidden, after):
+    flipped = section == 2
+    width, total = (rows.shape[2], rows.shape[1]) if flipped else rows.shape[1:]
+    tiles = hidden // TILE
+    if flipped:
+        out_spec, out_shape = pl.BlockSpec((TILE, width), lambda j: (j, 0)), (hidden, width)
+    else:
+        out_spec, out_shape = pl.BlockSpec((width, TILE), lambda j: (0, j)), (width, hidden)
+    return call(
+        "weight",
+        functools.partial(weight_kernel, flipped),
+        (tiles,),
+        [whole(rows.shape)]
+        + [
+            pl.BlockSpec((2, split.shape[1], TILE), lambda j: (0, 0, section * tiles + j))
+            for split in splits
+        ],
+        [out_spec],
+        [shape_of(*out_shape)],
+        flops=6 * total * width * hidden,
+        moved=4 * width * hidden,
+        after=after,
+        limit=VMEM_MOST,
+    )(rows, *splits)
+
+
+def by_head(source, heads):
+    return jnp.concatenate([source[:, at * HD : (at + 1) * HD] for at in range(heads)], axis=0)
+
+
+def probs_kernel(heads, scale, place, first, queries, lse, keys, *refs):
+    rest, probs = refs[:-1], refs[-1]
+    rows = queries.shape[0]
+    query_rows = by_head(queries, heads)
+    shift = lse[...]
+    row_at = lax.broadcasted_iota(jnp.int32, (heads * rows, 1), 0)
+    row_pos = lax.rem(row_at, rows) + first[0]
+    for at, source in enumerate((keys,) + rest):
+        key_count = source.shape[0]
+        for begin in range(0, key_count, TILE):
+            scores = lax.dot_general(
+                query_rows,
+                source[pl.ds(begin, TILE), :],
+                NT,
+                precision=highest,
+                preferred_element_type=f32,
+            )
+            key_at = lax.broadcasted_iota(jnp.int32, (1, TILE), 1)
+            key_pos = key_at + (place[at] * key_count + begin)
+            probs[:, pl.ds(at * key_count + begin, TILE)] = jnp.where(
+                key_pos <= row_pos, jnp.exp(scores * scale - shift), 0.0
+            )
+
+
+def probs_of(place, first, queries, lse, keys, key_count, after):
+    rows, columns = queries.shape
+    heads = columns // HD
+    scalar = pl.BlockSpec(memory_space=pltpu.SMEM)
+    total = (heads * rows, key_count * len(keys))
+    return call(
+        "probs",
+        functools.partial(probs_kernel, heads, 1.0 / math.sqrt(HD)),
+        (1,),
+        [scalar, scalar, whole(queries.shape), whole(lse.shape)]
+        + [pl.BlockSpec((key_count, HD), lambda i: (0, 0))] * len(keys),
+        [whole(total)],
+        [shape_of(*total)],
+        flops=12 * rows * columns * total[1],
+        moved=4 * total[0] * total[1],
+        after=after,
+    )(place, first, queries, lse, *keys)
+
+
+def attend_kernel(heads, scale, probs, outs, *refs):
+    out = refs[-1]
+    count = (len(refs) - 1) // 3
+    douts, keys, values = refs[:count], refs[count : 2 * count], refs[2 * count : 3 * count]
+    rows = outs.shape[0]
+    dout = douts[0][...]
+    for other in douts[1:]:
+        dout = dout + other[...]
+    dout_rows = by_head(dout, heads)
+    delta = jnp.sum(dout_rows * by_head(outs, heads), axis=1, keepdims=True)
+    dout_parts = pieces(dout_rows)
+    total = jnp.zeros((heads * rows, HD), f32)
+    for at in range(count):
+        key_count = keys[at].shape[0]
+        for begin in range(0, key_count, TILE):
+            part = pl.ds(begin, TILE)
+            dprobs = dot3(dout_parts, pieces(values[at][part, :]), NT)
+            weights = probs[:, pl.ds(at * key_count + begin, TILE)] * (dprobs - delta)
+            total += dot3(pieces(weights), pieces(keys[at][part, :]), NN)
+    for head in range(heads):
+        out[:, head * HD : (head + 1) * HD] = total[head * rows : (head + 1) * rows] * scale
+
+
+def attend(probs, outs, douts, keys, values, key_count, after):
+    rows, columns = outs.shape
+    block = pl.BlockSpec((key_count, HD), lambda i: (0, 0))
+    return call(
+        "attend",
+        functools.partial(attend_kernel, columns // HD, 1.0 / math.sqrt(HD)),
+        (1,),
+        [whole(probs.shape), whole(outs.shape)]
+        + [whole(outs.shape)] * len(douts)
+        + [block] * (len(keys) + len(values)),
+        [whole(outs.shape)],
+        [shape_of(rows, columns)],
+        flops=12 * rows * columns * key_count * len(keys),
+        moved=4 * (probs.size + 2 * key_count * HD * len(keys)),
+        after=after,
+    )(probs, outs, *douts, *keys, *values)
+
+
+def attn_grad_kernel(blocks, place, weight, *refs):
+    sources, outs = refs[:blocks], refs[blocks:-2]
+    rel_rows, parts = refs[-2:]
+    cut = outs[0].shape[0]
+    total = cut * len(outs)
+    piece = total // blocks
+
+    @pl.when(pl.program_id(0) == 0)
+    def _():
+        for at, source in enumerate(sources):
+            high, low = pieces(source[...])
+            start = pl.multiple_of(place[at] * piece, piece)
+            rel_rows[pl.ds(start, piece), :] = source[...]
+            parts[pl.ds(start, piece), :] = high
+            parts[pl.ds(pl.multiple_of(total + start, piece), piece), :] = low
+
+    high, low = pieces(weight[...])
+    both = dot(parts[...], high, NT)
+    result = both[:total] + both[total:] + dot(parts[:total, :], low, NT)
+    for at, out in enumerate(outs):
+        out[...] = result[at * cut : (at + 1) * cut]
+
+
+def attn_grad(place, sources, weight, count, after):
+    piece, width = sources[0].shape
+    total = piece * len(sources)
+    columns = weight.shape[0]
+    part = (total // count, columns)
+    return call(
+        "attn_grad",
+        functools.partial(attn_grad_kernel, len(sources)),
+        (columns // TILE,),
+        [pl.BlockSpec(memory_space=pltpu.SMEM), pl.BlockSpec((TILE, width), lambda j: (j, 0))]
+        + [whole(source.shape) for source in sources],
+        [pl.BlockSpec((part[0], TILE), lambda j: (0, j))] * count + [whole((total, width))],
+        [shape_of(*part)] * count + [shape_of(total, width)],
+        [pltpu.VMEM((2 * total, width), bf16)],
+        flops=6 * total * width * columns,
+        moved=4 * width * columns,
+        after=after,
+    )(place, weight, *sources)
+
+
+def out_weight_kernel(*refs):
+    outs, (resid, grad) = refs[:-2], refs[-2:]
+    rows = resid.shape[0] // len(outs)
+    head = pl.ds(pl.multiple_of(pl.program_id(0) * rows, rows), rows)
+    left = jnp.concatenate([out[head, :] for out in outs], axis=0)
+    grad[...] = dot3(pieces(left), pieces(resid[...]), TN)
+
+
+def out_weight_grad(outs, resid, heads, after):
+    total, width = resid.shape
+    return call(
+        "out_weight",
+        out_weight_kernel,
+        (heads,),
+        [pl.BlockSpec((heads * total // len(outs), HD), lambda j, at=at: (at, 0)) for _, at in outs]
+        + [whole(resid.shape)],
+        [pl.BlockSpec((HD, width), lambda j: (j, 0))],
+        [shape_of(heads * HD, width)],
+        flops=6 * total * width * heads * HD,
+        moved=4 * width * heads * HD,
+        after=after,
+    )(*[item for item, _ in outs], resid)
+
+
+def arrange_kernel(count, place, resid, grad, out, again):
+    rows, width = resid.shape
+    cut = rows // count
+    for rel in range(count):
+        source = pl.ds(pl.multiple_of(place[rel] * cut, cut), cut)
+        out[pl.ds(rel * cut, cut), :width] = resid[source, :]
+        out[pl.ds(rel * cut, cut), width:] = grad[source, :]
+    again[...] = out[...]
+
+
+def arrange(place, resid, grad, count, after):
+    rows, width = resid.shape
+    return call(
+        "arrange",
+        functools.partial(arrange_kernel, count),
+        (1,),
+        [pl.BlockSpec(memory_space=pltpu.SMEM)] + [whole(resid.shape)] * 2,
+        [whole((rows, 2 * width))] * 2,
+        [shape_of(rows, 2 * width)] * 2,
+        moved=16 * rows * width,
+        after=after,
+        limit=VMEM_MOST,
+    )(place, resid, grad)
+
+
+def finish_kernel(count, place, rows_rel, gain, *refs):
+    parts, out = refs[:-1], refs[-1]
+    rows, width = out.shape
+    cut = rows // count
+    total = parts[0][...]
+    for part in parts[1:]:
+        total = total + part[...]
+    result = (
+        rows_rel[:, width:]
+        + gain[...] * total[:, :width]
+        - rows_rel[:, :width] * total[:, width : width + 1]
+    )
+    for rel in range(count):
+        target = pl.ds(pl.multiple_of(place[rel] * cut, cut), cut)
+        out[target, :] = result[rel * cut : (rel + 1) * cut]
+
+
+def finish(place, rows_rel, gain, parts, count, after):
+    rows, width = rows_rel.shape[0], gain.shape[1]
+    return call(
+        "finish",
+        functools.partial(finish_kernel, count),
+        (1,),
+        [pl.BlockSpec(memory_space=pltpu.SMEM), whole(rows_rel.shape), whole(gain.shape)]
+        + [whole(part.shape) for part in parts],
+        [whole((rows, width))],
+        [shape_of(rows, width)],
+        moved=4 * rows * width * (len(parts) + 3),
+        after=after,
+    )(place, rows_rel, gain, *parts)
+
+
+def save_kernel(heads, keys, values, outs, saved, kept):
+    kept[...] = values[...]
+    count = keys.shape[0]
+    rows = outs.shape[0]
+    saved[pl.ds(0, count), :] = keys[...]
+    for head in range(heads):
+        saved[pl.ds(count + head * rows, rows), :] = outs[:, head * HD : (head + 1) * HD]
+
+
+def save(keys, values, outs, after):
+    count, rows, columns = keys.shape[0], outs.shape[0], outs.shape[1]
+    heads = columns // HD
+    total = (count + heads * rows, HD)
+    return call(
+        "save",
+        functools.partial(save_kernel, heads),
+        (1,),
+        [whole(keys.shape), whole(values.shape), whole(outs.shape)],
+        [whole(total), whole(values.shape)],
+        [shape_of(*total), shape_of(*values.shape)],
+        moved=8 * total[0] * HD,
+        after=after,
+    )(keys, values, outs)
+
+
+def shards_square(
+    residual,
+    grad_out,
+    norm_gain,
+    w_gate,
+    w_up,
+    w_down,
+    w_out,
+    queries,
+    attn_out,
+    log_sum_exp,
+    key_cache,
+    value_cache,
+):
+    square = lax.axis_size("ctx")
+    planes = lax.axis_size("wide") // 2
+    here = lax.axis_index("ctx")
+    local_width, hidden = w_gate.shape
+    width = local_width * square
+    gain = norm_gain[None, :]
+    places = jnp.arange(square, dtype=jnp.int32) ^ here
+    chain = Chain()
+    rows_rel, rows_again = arrange(places, residual, grad_out, square, chain)
+
+    offsets = list(range(planes))
+    orders = [(0, 2, 1, 3) if unit % 2 == 0 else (0, 1, 2, 3) for unit in range(planes)]
+    sources, stacked, kept, sent, folded = {}, {}, {}, {}, {}
+    done, from_second, from_first, from_far = {}, {}, {}, {}
+    splits, own_sums, far_sums, normed_parts = {}, {}, {}, {}
+
+    def begin(*units):
+        results = partial_sums(
+            [orders[unit] for unit in units],
+            [sources[unit] for unit in units],
+            gain,
+            w_gate,
+            w_up,
+            w_down,
+            chain,
+        )
+        for unit, (keep, send, rows) in zip(units, results):
+            kept[unit], stacked[unit] = keep, rows
+            sent[unit] = flip(send, "ctx", orders[unit][2])
+
+    def half(unit):
+        kept[unit], send = fold(kept[unit], sent[unit], chain)
+        folded[unit] = flip(send, "ctx", orders[unit][1])
+
+    def centre(unit):
+        result = middle(width, kept[unit], folded[unit], chain)
+        done[unit] = result
+        from_second[unit] = flip(result, "ctx", orders[unit][1])
+        from_first[unit] = flip(result, "ctx", orders[unit][2])
+        from_far[unit] = flip(from_second[unit], "ctx", orders[unit][2])
+
+    def close(unit):
+        own_sums[unit], far_sum, splits[unit] = normed_sums(
+            orders[unit],
+            (done[unit], from_second[unit], from_first[unit], from_far[unit]),
+            w_gate,
+            w_up,
+            chain,
+        )
+        far_sums[unit] = flip(far_sum, "wide", 1)
+
+    def settle(unit):
+        part = join(own_sums[unit], far_sums[unit], chain)
+        offset = offsets[unit]
+        normed_parts[unit] = flip(part, "wide", offset * 2) if offset else part
+
+    rows, columns = queries.shape
+    heads = columns // HD
+    mine = lax.axis_index("wide")
+    spots = [mine ^ (offset * 2 + far) for offset in offsets for far in range(2)]
+    spots = (jnp.stack(spots) ^ (here * 2)).astype(jnp.int32)
+    keys_own, values_own = key_cache[0], value_cache[0]
+    key_count = keys_own.shape[0]
+    context = key_count * square
+    first_pos = jnp.reshape(context - rows * square + here * rows, (1,)).astype(jnp.int32)
+    lse_rows = log_sum_exp.reshape(heads * rows, 1)
+
+    def wide_rows(unit, own):
+        own = ordered(own, *chain.links)
+        sources[unit] = (own, flip(own, "wide", 1))
+
+    sources[0] = (rows_rel, flip(rows_rel, "wide", 1))
+    own = flip(rows_again, "wide", 2)
+    sources[1] = (own, flip(own, "wide", 1))
+    later = ordered(rows_again, own)
+    arriving = {unit: flip(later, "wide", offsets[unit] * 2) for unit in (2, 3)}
+    begin(0, 1)
+    wide_rows(2, arriving[2])
+    wide_rows(3, arriving[3])
+    begin(2, 3)
+    chain.wait(spots, first_pos, lse_rows)
+    half(0)
+    half(1)
+    centre(0)
+    centre(1)
+    row_parts, grad_parts = collect([stacked[unit] for unit in range(planes)], chain)
+    saved, values_own = save(keys_own, values_own, attn_out, chain)
+    chain.wait(from_second[0], from_second[1])
+    half(2)
+    half(3)
+    centre(2)
+    chain.wait(from_second[2])
+    centre(3)
+    close(0)
+    chain.wait(from_second[3])
+    close(1)
+    settle(0)
+    close(2)
+    settle(1)
+    close(3)
+    settle(2)
+    settle(3)
+    all_splits = [splits[unit] for unit in range(planes)]
+    grad_w_gate = weight_grad(0, row_parts, all_splits, hidden, chain)
+    parts = [normed_parts[unit] for unit in range(planes)]
+    grad_resid = finish(places, rows_rel, gain, parts, square, chain)
+
+    across = [flip(grad_resid, "wide", offset * 2) if offset else grad_resid for offset in offsets]
+    keys_near = flip(saved, "ctx", 1)
+    keys_side = flip(saved, "ctx", 2)
+    values_side = flip(values_own, "ctx", 2)
+    values_near = flip(values_own, "ctx", 1)
+    keys = [saved, keys_near, keys_side, flip(keys_near, "ctx", 2)]
+    values = [values_own, values_near, values_side, flip(values_side, "ctx", 1)]
+    outs = [(item, key_count // (heads * rows)) for item in keys]
+
+    grad_w_up = weight_grad(1, row_parts, all_splits, hidden, chain)
+    blocks = []
+    for own in across:
+        own = ordered(own, *chain.links) if own is not grad_resid else own
+        blocks += [own, flip(own, "wide", 1)]
+    grad_w_down = weight_grad(2, grad_parts, all_splits, hidden, chain)
+    *parts, resid_rows = attn_grad(spots, blocks, w_out, square, chain)
+    d_attn = [flip(part, "ctx", rel) if rel else part for rel, part in enumerate(parts)]
+    probs = probs_of(places, first_pos, queries, lse_rows, keys, key_count, chain)
+    grad_w_out = out_weight_grad(outs, resid_rows, heads, chain)
+    grad_queries = attend(probs, attn_out, d_attn, keys, values, key_count, chain)
+    return (grad_w_gate, grad_w_up, grad_w_down, grad_w_out, grad_resid, grad_queries)
+
+
+def shards(*arrays):
+    residual, queries, key_cache, w_gate = arrays[0], arrays[7], arrays[10], arrays[3]
+    wide, ctx = lax.axis_size("wide"), lax.axis_size("ctx")
+    planes = wide // 2
+    heads = queries.shape[1] // HD
+    fits = (
+        ctx == 4
+        and wide == KVH
+        and planes == ctx
+        and residual.shape[0] % 32 == 0
+        and queries.shape[0] % 16 == 0
+        and all(extent % TILE == 0 for extent in w_gate.shape + (queries.shape[1],))
+        and key_cache.shape[1] % (heads * queries.shape[0]) == 0
+    )
+    return shards_square(*arrays) if fits else shards_general(*arrays)
 
 
 def swapped(block, axis, bit):
@@ -60,7 +833,7 @@
     return partial_sums
 
 
-def shards(
+def shards_general(
     residual,
     grad_out,
     norm_gain,

time: 390 us -> 253 us (0.65); the launches traced: 382 us -> 251 us
  waiting for transfers between devices: 186 us -> 60.3 us
  matrix products: 108 us -> 0 us
  Pallas kernels: 0 us -> 107 us
  starting transfers between devices: 0.28 us -> 59.7 us
  blocking collectives: 58.5 us -> 0 us
  between operations: 14.6 us -> 1.07 us
  local copies, waits for them, and re-layouts: 10.1 us -> 22.5 us
  other arithmetic: 5.85 us -> 0.55 us
    psum x1 -> x0, waiting for transfers between devices: 116 us -> none  [shards(): lax.psum((matmul(gained, w_gate), matmul(gained, w_up), matmul_nt(all_gra...]
    dot_general x16 -> x0, matrix products: 108 us -> none  [the longest x8 51.3 us: matmul_nt(): lax.dot_general(left, right, (((1,), (1,)), ((), ())), precision=highest,...]
    pallas_call x0 -> x35, Pallas kernels: none -> 107 us  [the longest x29 107 us: apply(): *results, link = run(*operands, *after.links)]
    ppermute x0 -> x50, waiting for transfers between devices: none -> 60.3 us  [flip(): return lax.ppermute(block, axis, [(at, at ^ mask) for at in range(count)])]
    ppermute x0 -> x50, starting transfers between devices: none -> 59.7 us  [flip(): return lax.ppermute(block, axis, [(at, at ^ mask) for at in range(count)])]
    all_gather x4 -> x0, blocking collectives: 38.2 us -> none  [the longest x1 10.6 us: shards(): lax.all_gather(queries, 'ctx', axis=0, tiled=True)]
    reduce_scatter x3 -> x0, waiting for transfers between devices: 36.8 us -> none  [the longest x1 32.4 us: shards(): lax.psum_scatter(matmul_nt(d_gate, w_gate) + matmul_nt(d_up, w_up), 'wide...]
    all_gather x3 -> x0, waiting for transfers between devices: 31.4 us -> none  [the longest x1 25.7 us: shards(): lax.all_gather(residual, 'wide', axis=0, tiled=True)]
  transfers between devices with their start and end apart: 7 -> 50, of which waited for: 5 -> 15; matrix products, arithmetic and copies ran while one was open for 17% -> 0% of each run, Pallas kernels for 0% -> 39%
where the time goes in v1:
time: 253 us; the launch traced here: 251 us
  Pallas kernels  107 us (42%)
  waiting for transfers between devices  60.3 us (24%)
  starting transfers between devices  59.7 us (24%)
  local copies, waits for them, and re-layouts  22.5 us (9%)
    pallas_call x29, Pallas kernels, apply(): *results, link = run(*operands, *after.links)  107 us
    ppermute x50, waiting for transfers between devices, flip(): return lax.ppermute(block, axis, [(at, at ^ mask) for at in range(count)])  60.3 us
    ppermute x50, starting transfers between devices, flip(): return lax.ppermute(block, axis, [(at, at ^ mask) for at in range(count)])  59.7 us
    unnamed x92, local copies, waits for them, and re-layouts  21.6 us
  transfers between devices with their start and end apart: 50, of which 15 were waited for; matrix products, arithmetic and copies ran while one was open for 0% of the time, Pallas kernels for 39%

profile of v1, /device:TPU:0, one launch (start us, length us, event | category | flops | bytes accessed | tf_op | source)
XLA Modules:
  0.0 250.9 jit_solution(8034365568293544026)
XLA Ops:
  1.2 1.9 arrange.1
  3.0 3.0 %collective-permute-start.1 = (f32[32,2048]{1,0:T(8,128)}, f32[32,2048]{1,0:T(8,128)S(1)}, u32[]{:S(2)}, u32[]{:S(2)}) collective-permute-start(f32[32,2048]{1,0:T(8,128)} %get-tuple-element.93.refs_0_), channel_id=1, source_target_pairs={{0,8},{4,12},{8,0},{12,4},{16,24},{20,28},{24,16},{28,20},{1,9},{5... | collective-permute-start | bytes 786440 | tf_op jit(solution)/shard_map/ppermute | solution.py:30
  6.1 6.5 %collective-permute-done.1.refs_2_.refs_1_ = f32[32,2048]{1,0:T(8,128)S(1)} collective-permute-done((f32[32,2048]{1,0:T(8,128)}, f32[32,2048]{1,0:T(8,128)S(1)}, u32[]{:S(2)}, u32[]{:S(2)}) %collective-permute-start.1) | collective-permute-done | bytes 262176 | tf_op jit(solution)/shard_map/ppermute | solution.py:30
  13.3 2.8 %collective-permute-start.3 = (f32[32,2048]{1,0:T(8,128)}, f32[32,2048]{1,0:T(8,128)}, u32[]{:S(2)}, u32[]{:S(2)}) collective-permute-start(f32[32,2048]{1,0:T(8,128)} %ordered.6), channel_id=1, source_target_pairs={{0,16},{4,20},{8,24},{12,28},{16,0},{20,4},{24,8},{28,12},{1,17},{... | collective-permute-start | bytes 786440 | tf_op jit(solution)/shard_map/ppermute | solution.py:30
  18.2 13.9 %partial.2 = (f32[32,5504]{1,0:T(8,128)}, f32[32,5504]{1,0:T(8,128)}, f32[64,2048]{1,0:T(8,128)}, f32[32,5504]{1,0:T(8,128)}, f32[32,5504]{1,0:T(8,128)}, /*index=5*/f32[64,2048]{1,0:T(8,128)}, f32[8,128]{1,0:T(8,128)}) custom-call(f32[32,2048]{1,0:T(8,128)} %get-tuple-element.92.refs_0_.refs_1_, f32[32,2048]{1,0:T(8,128)} %copy-done.42, ...), custom_call_target="tpu_custom_call" | custom-call | flops 16911433728 | bytes 88080384 | tf_op jit(solution)/shard_map/partial/pallas_call | solution.py:93
  32.1 2.8 %collective-permute-done.3.refs_0_ = f32[32,2048]{1,0:T(8,128)} collective-permute-done((f32[32,2048]{1,0:T(8,128)}, f32[32,2048]{1,0:T(8,128)}, u32[]{:S(2)}, u32[]{:S(2)}) %collective-permute-start.3) | collective-permute-done | bytes 262176 | tf_op jit(solution)/shard_map/ppermute | solution.py:30
  36.3 1.7 collective-permute-start.7
  41.0 13.8 %partial.3 = (f32[32,5504]{1,0:T(8,128)}, f32[32,5504]{1,0:T(8,128)}, f32[64,2048]{1,0:T(8,128)}, f32[32,5504]{1,0:T(8,128)}, f32[32,5504]{1,0:T(8,128)}, /*index=5*/f32[64,2048]{1,0:T(8,128)}, f32[8,128]{1,0:T(8,128)}) custom-call(f32[32,2048]{1,0:T(8,128)} %ordered.7.refs_0_, f32[32,2048]{1,0:T(8,128)} %copy-done.40, f32[32,2048]{1,0:T(8,128)} %ordered.8.refs_2_, ...), custom_call_target="tpu_custom_call" | custom-call | flops 16911433728 | bytes 88080384 | tf_op jit(solution)/shard_map/partial/pallas_call | solution.py:93
  57.9 1.7 collective-permute-start.9
  60.0 1.6 collective-permute-start.14
  61.7 7.0 %collective-permute-done.10.refs_1_ = f32[16,5504]{1,0:T(8,128)S(1)} collective-permute-done((f32[16,5504]{1,0:T(8,128)S(1)}, f32[16,5504]{1,0:T(8,128)S(1)}, u32[]{:S(2)}, u32[]{:S(2)}) %collective-permute-start.10) | collective-permute-done | bytes 352288 | tf_op jit(solution)/shard_map/ppermute | solution.py:30
  71.7 1.6 collective-permute-start.16
  73.3 3.2 %collect.1 = (bf16[2,1024,256]{2,1,0:T(8,128)(2,1)}, bf16[2,256,1024]{2,1,0:T(8,128)(2,1)}, f32[8,128]{1,0:T(8,128)}) custom-call(f32[64,2048]{1,0:T(8,128)} %get-tuple-element.95.refs_0_, f32[64,2048]{1,0:T(8,128)} %get-tuple-element.96.refs_1_, f32[64,2048]{1,0:T(8,128)} %get-tuple-element.98.refs_2_, f32[64,2048]{1,0:T(8,128)} %get-tuple-element.99.refs_3_, ...), custom_call_target="tpu_custom_call" | custom-call | bytes 16777216 | tf_op jit(solution)/shard_map/collect/pallas_call | solution.py:93
  80.9 3.4 %collective-permute-done.15.refs_1_ = f32[32,5504]{1,0:T(8,128)S(1)} collective-permute-done((f32[32,5504]{1,0:T(8,128)}, f32[32,5504]{1,0:T(8,128)S(1)}, u32[]{:S(2)}, u32[]{:S(2)}) %collective-permute-start.15) | collective-permute-done | bytes 704544 | tf_op jit(solution)/shard_map/ppermute | solution.py:30
  84.3 5.1 %collective-permute-done.11.refs_3_.refs_1_ = f32[16,5504]{1,0:T(8,128)} collective-permute-done((f32[16,5504]{1,0:T(8,128)}, f32[16,5504]{1,0:T(8,128)}, u32[]{:S(2)}, u32[]{:S(2)}) %collective-permute-start.11) | collective-permute-done | bytes 352288 | tf_op jit(solution)/shard_map/ppermute | solution.py:30
  89.7 1.7 collective-permute-start.18
  93.0 4.9 %collective-permute-done.18.refs_1_ = f32[16,5504]{1,0:T(8,128)S(1)} collective-permute-done((f32[16,5504]{1,0:T(8,128)S(1)}, f32[16,5504]{1,0:T(8,128)S(1)}, u32[]{:S(2)}, u32[]{:S(2)}) %collective-permute-start.18) | collective-permute-done | bytes 352288 | tf_op jit(solution)/shard_map/ppermute | solution.py:30
  98.2 1.6 collective-permute-start.19
  102.2 1.6 collective-permute-start.21
  103.8 5.5 %collective-permute-done.19.refs_3_.refs_1_ = f32[16,5504]{1,0:T(8,128)S(1)} collective-permute-done((f32[16,5504]{1,0:T(8,128)S(1)}, f32[16,5504]{1,0:T(8,128)S(1)}, u32[]{:S(2)}, u32[]{:S(2)}) %collective-permute-start.19) | collective-permute-done | bytes 352288 | tf_op jit(solution)/shard_map/ppermute | solution.py:30
  109.4 1.5 collective-permute-start.23
  112.6 6.1 %collective-permute-done.13.refs_3_ = f32[16,5504]{1,0:T(8,128)S(1)} collective-permute-done((f32[16,5504]{1,0:T(8,128)}, f32[16,5504]{1,0:T(8,128)S(1)}, u32[]{:S(2)}, u32[]{:S(2)}) %collective-permute-start.13) | collective-permute-done | bytes 352288 | tf_op jit(solution)/shard_map/ppermute | solution.py:30
  119.1 3.1 %copy-done.22 = f32[1024,1792]{1,0:T(8,128)S(1)} copy-done((f32[1024,1792]{1,0:T(8,128)S(1)}, f32[1024,1792]{1,0:T(8,128)}, u32[]{:S(2)}) %copy-start.22) | copy-done | bytes 7340056
  122.2 3.1 %copy-done.23 = f32[1024,1792]{1,0:T(8,128)S(1)} copy-done((f32[1024,1792]{1,0:T(8,128)S(1)}, f32[1024,1792]{1,0:T(8,128)}, u32[]{:S(2)}) %copy-start.23) | copy-done | bytes 7340056
  125.3 6.6 %normed.4 = (f32[32,1152]{1,0:T(8,128)S(1)}, f32[32,1152]{1,0:T(8,128)S(1)}, bf16[2,64,5376]{2,1,0:T(8,128)(2,1)S(1)}, f32[8,128]{1,0:T(8,128)S(1)}) custom-call(f32[16,5504]{1,0:T(8,128)} %get-tuple-element.114.refs_0_, f32[16,5504]{1,0:T(8,128)} %collective-permute-done.11.refs_3_.refs_1_, f32[16,5504]{1,0:T(8,128)S(1)} %collective-permute-done.12.refs_2_, ...), custom_call_target="tpu_custom_call" | custom-call | flops 5637144576 | bytes 58720256 | tf_op jit(solution)/shard_map/normed/pallas_call | solution.py:93
  133.0 1.6 collective-permute-start.24
  134.6 6.6 %normed.5 = (f32[32,1152]{1,0:T(8,128)S(1)}, f32[32,1152]{1,0:T(8,128)S(1)}, bf16[2,64,5376]{2,1,0:T(8,128)(2,1)S(1)}, f32[8,128]{1,0:T(8,128)S(1)}) custom-call(f32[16,5504]{1,0:T(8,128)} %get-tuple-element.121.refs_0_, f32[16,5504]{1,0:T(8,128)} %collective-permute-done.16.refs_4_.refs_1_, f32[16,5504]{1,0:T(8,128)S(1)} %collective-permute-done.20.refs_2_, ...), custom_call_target="tpu_custom_call" | custom-call | flops 5637144576 | bytes 58720256 | tf_op jit(solution)/shard_map/normed/pallas_call | solution.py:93
  142.5 1.5 collective-permute-start.27
  144.1 5.6 %normed.6 = (f32[32,1152]{1,0:T(8,128)S(1)}, f32[32,1152]{1,0:T(8,128)S(1)}, bf16[2,64,5376]{2,1,0:T(8,128)(2,1)S(1)}, f32[8,128]{1,0:T(8,128)S(1)}) custom-call(f32[16,5504]{1,0:T(8,128)S(1)} %get-tuple-element.129.refs_0_, f32[16,5504]{1,0:T(8,128)S(1)} %collective-permute-done.19.refs_3_.refs_1_, f32[16,5504]{1,0:T(8,128)S(1)} %collective-permute-done.23.refs_2_, ...), custom_call_target="tpu_custom_call" | custom-call | flops 5637144576 | bytes 58720256 | tf_op jit(solution)/shard_map/normed/pallas_call | solution.py:93
  150.9 2.1 collective-permute-done.27.refs_3_
  153.0 5.6 %normed.7 = (f32[32,1152]{1,0:T(8,128)S(1)}, f32[32,1152]{1,0:T(8,128)S(1)}, bf16[2,64,5376]{2,1,0:T(8,128)(2,1)S(1)}, f32[8,128]{1,0:T(8,128)S(1)}) custom-call(f32[16,5504]{1,0:T(8,128)S(1)} %get-tuple-element.133.refs_0_, f32[16,5504]{1,0:T(8,128)S(1)} %collective-permute-done.22.refs_7_.refs_1_, f32[16,5504]{1,0:T(8,128)S(1)} %collective-permute-done.26.refs_2_, ...), custom_call_target="tpu_custom_call" | custom-call | flops 5637144576 | bytes 58720256 | tf_op jit(solution)/shard_map/normed/pallas_call | solution.py:93
  159.8 5.8 %collective-permute-start.31 = (f32[32,1152]{1,0:T(8,128)S(1)}, f32[32,1152]{1,0:T(8,128)S(1)}, u32[]{:S(2)}, u32[]{:S(2)}) collective-permute-start(f32[32,1152]{1,0:T(8,128)S(1)} %get-tuple-element.154), channel_id=1, source_target_pairs={{0,8},{4,12},{8,0},{12,4},{16,24},{20,28},{24,16},{28,20},{1,9},{5... | collective-permute-start | bytes 442376 | tf_op jit(solution)/shard_map/ppermute | solution.py:30
  165.6 2.0 collective-permute-start.32
  167.6 1.5 collective-permute-start.33
  169.2 8.7 %weight.3 = (f32[1024,1792]{1,0:T(8,128)}, f32[8,128]{1,0:T(8,128)}) custom-call(bf16[2,1024,256]{2,1,0:T(8,128)(2,1)} %get-tuple-element.113.refs_0_, bf16[2,64,5376]{2,1,0:T(8,128)(2,1)} %copy-done.34, bf16[2,64,5376]{2,1,0:T(8,128)(2,1)} %copy-done.33, bf16[2,64,5376]{2,1,0:T(8,128)(2,1)} %copy-done.35, bf16[2,64,5376]{2,1,0:T(8,128)(2,1)} %copy-done.36, ...), custom_call_target="tpu_custom_call" | custom-call | flops 11274289152 | bytes 29360128 | tf_op jit(solution)/shard_map/weight/pallas_call | solution.py:93
  177.9 1.7 collective-permute-done.33.refs_6_
  181.6 3.0 %collective-permute-start.38 = (f32[32,1024]{1,0:T(8,128)}, f32[32,1024]{1,0:T(8,128)S(1)}, u32[]{:S(2)}, u32[]{:S(2)}) collective-permute-start(f32[32,1024]{1,0:T(8,128)} %get-tuple-element.90.refs_2_), channel_id=1, source_target_pairs={{0,8},{4,12},{8,0},{12,4},{16,24},{20,28},{24,16},{28,20},{1,9},{5... | collective-permute-start | bytes 393224 | tf_op jit(solution)/shard_map/ppermute | solution.py:30
  185.1 1.5 collective-permute-start.48
  186.7 1.9 collective-permute-start.40
  188.5 2.8 %collective-permute-start.42 = (f32[32,1024]{1,0:T(8,128)}, f32[32,1024]{1,0:T(8,128)S(1)}, u32[]{:S(2)}, u32[]{:S(2)}) collective-permute-start(f32[32,1024]{1,0:T(8,128)} %get-tuple-element.90.refs_2_), channel_id=1, source_target_pairs={{0,24},{4,28},{8,16},{12,20},{16,8},{20,12},{24,0},{28,4},{1,25},{... | collective-permute-start | bytes 393224 | tf_op jit(solution)/shard_map/ppermute | solution.py:30
  191.4 8.5 %weight.4 = (f32[1024,1792]{1,0:T(8,128)}, f32[8,128]{1,0:T(8,128)}) custom-call(bf16[2,1024,256]{2,1,0:T(8,128)(2,1)} %get-tuple-element.113.refs_0_, bf16[2,64,5376]{2,1,0:T(8,128)(2,1)} %copy-done.34, bf16[2,64,5376]{2,1,0:T(8,128)(2,1)} %copy-done.33, bf16[2,64,5376]{2,1,0:T(8,128)(2,1)} %copy-done.35, bf16[2,64,5376]{2,1,0:T(8,128)(2,1)} %copy-done.36, ...), custom_call_target="tpu_custom_call" | custom-call | flops 11274289152 | bytes 29360128 | tf_op jit(solution)/shard_map/weight/pallas_call | solution.py:93
  204.4 8.7 %weight.5 = (f32[1792,1024]{1,0:T(8,128)}, f32[8,128]{1,0:T(8,128)}) custom-call(bf16[2,256,1024]{2,1,0:T(8,128)(2,1)} %get-tuple-element.160.refs_0_, bf16[2,64,5376]{2,1,0:T(8,128)(2,1)} %copy-done.34, bf16[2,64,5376]{2,1,0:T(8,128)(2,1)} %copy-done.33, bf16[2,64,5376]{2,1,0:T(8,128)(2,1)} %copy-done.35, bf16[2,64,5376]{2,1,0:T(8,128)(2,1)} %copy-done.36, ...), custom_call_target="tpu_custom_call" | custom-call | flops 11274289152 | bytes 29360128 | tf_op jit(solution)/shard_map/weight/pallas_call | solution.py:93
  216.0 2.7 %attn_grad.1 = (f32[64,512]{1,0:T(8,128)S(1)}, f32[64,512]{1,0:T(8,128)S(1)}, f32[64,512]{1,0:T(8,128)S(1)}, f32[64,512]{1,0:T(8,128)S(1)}, f32[256,1024]{1,0:T(8,128)S(1)}, /*index=5*/f32[8,128]{1,0:T(8,128)S(1)}) custom-call(s32[8]{0:T(128)S(1)} %broadcast_xor_fusion.refs_3_.refs_0_, f32[512,1024]{1,0:T(8,128)S(1)} %copy-done.24, ...), custom_call_target="tpu_custom_call" | custom-call | flops 3221225472 | bytes 8388608 | tf_op jit(solution)/shard_map/attn_grad/pallas_call | solution.py:93
  220.7 10.8 %collective-permute-done.36.refs_7_.refs_3_.refs_9_ = f32[1280,128]{1,0:T(8,128)} collective-permute-done((f32[1280,128]{1,0:T(8,128)}, f32[1280,128]{1,0:T(8,128)}, u32[]{:S(2)}, u32[]{:S(2)}) %collective-permute-start.36) | collective-permute-done | bytes 655392 | tf_op jit(solution)/shard_map/ppermute | solution.py:30
  233.0 5.2 %probs.1 = (f32[256,4096]{1,0:T(8,128)S(1)}, f32[8,128]{1,0:T(8,128)S(1)}) custom-call(s32[4]{0:T(128)S(1)} %copy-done.21, s32[1]{0:T(128)} %bitcast.9.refs_4_.refs_1_, f32[64,512]{1,0:T(8,128)S(1)} %copy-done.29, f32[256,1]{1,0:T(8,128)S(1)} %copy-done.7, f32[1280,128]{1,0:T(8,128)} %get-tuple-element.163.refs_4_.refs_0_.refs_6_, ...), custom_call_target="tpu_custom_call" | custom-call | flops 6442450944 | bytes 16777216 | tf_op jit(solution)/shard_map/probs/pallas_call | solution.py:93
  238.2 4.0 %out_weight.1 = (f32[512,1024]{1,0:T(8,128)}, f32[8,128]{1,0:T(8,128)S(1)}) custom-call(f32[1280,128]{1,0:T(8,128)} %get-tuple-element.163.refs_4_.refs_0_.refs_6_, f32[1280,128]{1,0:T(8,128)} %collective-permute-done.34.refs_5_.refs_1_.refs_7_, f32[1280,128]{1,0:T(8,128)} %collective-permute-done.35.refs_6_.refs_2_.refs_8_, ...), custom_call_target="tpu_custom_call" | custom-call | flops 3221225472 | bytes 8388608 | tf_op jit(solution)/shard_map/out_weight/pallas_call | solution.py:93
  242.3 2.3 collective-permute-done.46.refs_5_
  244.6 6.2 %attend.1 = (f32[64,512]{1,0:T(8,128)}, f32[8,128]{1,0:T(8,128)}) custom-call(f32[256,4096]{1,0:T(8,128)S(1)} %get-tuple-element.170.refs_0_, f32[64,512]{1,0:T(8,128)S(1)} %copy-done.9, f32[64,512]{1,0:T(8,128)S(1)} %get-tuple-element.171.refs_2_, f32[64,512]{1,0:T(8,128)S(1)} %collective-permute-done.44.refs_3_, ...), custom_call_target="tpu_custom_call" | custom-call | flops 6442450944 | bytes 33554432 | tf_op jit(solution)/shard_map/attend/pallas_call | solution.py:93
  (184 shorter events, 43.6 us)
Async XLA Ops:
  3.0 9.5 %collective-permute-start.1 = (f32[32,2048]{1,0:T(8,128)}, f32[32,2048]{1,0:T(8,128)S(1)}, u32[]{:S(2)}, u32[]{:S(2)}) collective-permute-start(f32[32,2048]{1,0:T(8,128)} %get-tuple-element.93.refs_0_), channel_id=1, source_target_pairs={{0,8},{4,12},{8,0},{12,4},{16,24},{20,28},{24,16},{28,20},{1,9},{5... | collective-permute-start | bytes 786440 | tf_op jit(solution)/shard_map/ppermute | solution.py:30
  6.1 11.3 %collective-permute-start = (f32[32,2048]{1,0:T(8,128)}, f32[32,2048]{1,0:T(8,128)S(1)}, u32[]{:S(2)}, u32[]{:S(2)}) collective-permute-start(f32[32,2048]{1,0:T(8,128)} %get-tuple-element.92.refs_0_.refs_1_), channel_id=1, source_target_pairs={{0,4},{4,0},{8,12},{12,8},{16,20},{20,16},{24,28},{28,24},{1,5},{5... | collective-permute-start | bytes 786440 | tf_op jit(solution)/shard_map/ppermute | solution.py:30
  12.6 4.8 %collective-permute-start.2 = (f32[32,2048]{1,0:T(8,128)S(1)}, f32[32,2048]{1,0:T(8,128)S(1)}, u32[]{:S(2)}, u32[]{:S(2)}) collective-permute-start(f32[32,2048]{1,0:T(8,128)S(1)} %collective-permute-done.1.refs_2_.refs_1_), channel_id=1, source_target_pairs={{0,4},{4,0},{8,12},{12,8},{16,20},{20,16},{24,28},{28,24},{1,5},{5... | collective-permute-start | bytes 786440 | tf_op jit(solution)/shard_map/ppermute | solution.py:30
  13.3 21.6 %collective-permute-start.3 = (f32[32,2048]{1,0:T(8,128)}, f32[32,2048]{1,0:T(8,128)}, u32[]{:S(2)}, u32[]{:S(2)}) collective-permute-start(f32[32,2048]{1,0:T(8,128)} %ordered.6), channel_id=1, source_target_pairs={{0,16},{4,20},{8,24},{12,28},{16,0},{20,4},{24,8},{28,12},{1,17},{... | collective-permute-start | bytes 786440 | tf_op jit(solution)/shard_map/ppermute | solution.py:30
  16.0 18.9 %collective-permute-start.5 = (f32[32,2048]{1,0:T(8,128)}, f32[32,2048]{1,0:T(8,128)}, u32[]{:S(2)}, u32[]{:S(2)}) collective-permute-start(f32[32,2048]{1,0:T(8,128)} %ordered.6), channel_id=1, source_target_pairs={{0,24},{4,28},{8,16},{12,20},{16,8},{20,12},{24,0},{28,4},{1,25},{... | collective-permute-start | bytes 786440 | tf_op jit(solution)/shard_map/ppermute | solution.py:30
  36.3 21.5 %collective-permute-start.7 = (f32[32,5504]{1,0:T(8,128)}, f32[32,5504]{1,0:T(8,128)S(1)}, u32[]{:S(2)}, u32[]{:S(2)}) collective-permute-start(f32[32,5504]{1,0:T(8,128)} %get-tuple-element.101), channel_id=1, source_target_pairs={{0,2},{1,3},{2,0},{3,1},{4,6},{5,7},{6,4},{7,5},{8,10},{9,11},{10,... | collective-permute-start | bytes 2113544 | tf_op jit(solution)/shard_map/ppermute | solution.py:30
  38.0 17.7 %collective-permute-start.8 = (f32[32,5504]{1,0:T(8,128)}, f32[32,5504]{1,0:T(8,128)S(1)}, u32[]{:S(2)}, u32[]{:S(2)}) collective-permute-start(f32[32,5504]{1,0:T(8,128)} %get-tuple-element.103), channel_id=1, source_target_pairs={{0,1},{1,0},{2,3},{3,2},{4,5},{5,4},{6,7},{7,6},{8,9},{9,8},{10,11... | collective-permute-start | bytes 2113544 | tf_op jit(solution)/shard_map/ppermute | solution.py:30
  57.4 11.2 %collective-permute-start.10 = (f32[16,5504]{1,0:T(8,128)S(1)}, f32[16,5504]{1,0:T(8,128)S(1)}, u32[]{:S(2)}, u32[]{:S(2)}) collective-permute-start(f32[16,5504]{1,0:T(8,128)S(1)} %get-tuple-element.109), channel_id=1, source_target_pairs={{0,2},{1,3},{2,0},{3,1},{4,6},{5,7},{6,4},{7,5},{8,10},{9,11},{10,... | collective-permute-start | bytes 1056776 | tf_op jit(solution)/shard_map/ppermute | solution.py:30
  57.9 12.1 %collective-permute-start.9 = (f32[16,5504]{1,0:T(8,128)S(1)}, f32[16,5504]{1,0:T(8,128)S(1)}, u32[]{:S(2)}, u32[]{:S(2)}) collective-permute-start(f32[16,5504]{1,0:T(8,128)S(1)} %get-tuple-element.107), channel_id=1, source_target_pairs={{0,1},{1,0},{2,3},{3,2},{4,5},{5,4},{6,7},{7,6},{8,9},{9,8},{10,11... | collective-permute-start | bytes 1056776 | tf_op jit(solution)/shard_map/ppermute | solution.py:30
  59.6 24.7 %collective-permute-start.15 = (f32[32,5504]{1,0:T(8,128)}, f32[32,5504]{1,0:T(8,128)S(1)}, u32[]{:S(2)}, u32[]{:S(2)}) collective-permute-start(f32[32,5504]{1,0:T(8,128)} %get-tuple-element.118), channel_id=1, source_target_pairs={{0,1},{1,0},{2,3},{3,2},{4,5},{5,4},{6,7},{7,6},{8,9},{9,8},{10,11... | collective-permute-start | bytes 2113544 | tf_op jit(solution)/shard_map/ppermute | solution.py:30
  60.0 31.3 %collective-permute-start.14 = (f32[32,5504]{1,0:T(8,128)}, f32[32,5504]{1,0:T(8,128)S(1)}, u32[]{:S(2)}, u32[]{:S(2)}) collective-permute-start(f32[32,5504]{1,0:T(8,128)} %get-tuple-element.116), channel_id=1, source_target_pairs={{0,2},{1,3},{2,0},{3,1},{4,6},{5,7},{6,4},{7,5},{8,10},{9,11},{10,... | collective-permute-start | bytes 2113544 | tf_op jit(solution)/shard_map/ppermute | solution.py:30
  69.7 19.6 %collective-permute-start.11 = (f32[16,5504]{1,0:T(8,128)}, f32[16,5504]{1,0:T(8,128)}, u32[]{:S(2)}, u32[]{:S(2)}) collective-permute-start(f32[16,5504]{1,0:T(8,128)} %get-tuple-element.114.refs_0_), channel_id=1, source_target_pairs={{0,2},{1,3},{2,0},{3,1},{4,6},{5,7},{6,4},{7,5},{8,10},{9,11},{10,... | collective-permute-start | bytes 1056776 | tf_op jit(solution)/shard_map/ppermute | solution.py:30
  71.7 17.9 %collective-permute-start.16 = (f32[16,5504]{1,0:T(8,128)}, f32[16,5504]{1,0:T(8,128)}, u32[]{:S(2)}, u32[]{:S(2)}) collective-permute-start(f32[16,5504]{1,0:T(8,128)} %get-tuple-element.121.refs_0_), channel_id=1, source_target_pairs={{0,1},{1,0},{2,3},{3,2},{4,5},{5,4},{6,7},{7,6},{8,9},{9,8},{10,11... | collective-permute-start | bytes 1056776 | tf_op jit(solution)/shard_map/ppermute | solution.py:30
  89.7 8.2 %collective-permute-start.18 = (f32[16,5504]{1,0:T(8,128)S(1)}, f32[16,5504]{1,0:T(8,128)S(1)}, u32[]{:S(2)}, u32[]{:S(2)}) collective-permute-start(f32[16,5504]{1,0:T(8,128)S(1)} %get-tuple-element.126), channel_id=1, source_target_pairs={{0,2},{1,3},{2,0},{3,1},{4,6},{5,7},{6,4},{7,5},{8,10},{9,11},{10,... | collective-permute-start | bytes 1056776 | tf_op jit(solution)/shard_map/ppermute | solution.py:30
  91.5 10.8 %collective-permute-start.17 = (f32[16,5504]{1,0:T(8,128)S(1)}, f32[16,5504]{1,0:T(8,128)S(1)}, u32[]{:S(2)}, u32[]{:S(2)}) collective-permute-start(f32[16,5504]{1,0:T(8,128)S(1)} %get-tuple-element.124), channel_id=1, source_target_pairs={{0,1},{1,0},{2,3},{3,2},{4,5},{5,4},{6,7},{7,6},{8,9},{9,8},{10,11... | collective-permute-start | bytes 1056776 | tf_op jit(solution)/shard_map/ppermute | solution.py:30
  98.2 11.2 %collective-permute-start.19 = (f32[16,5504]{1,0:T(8,128)S(1)}, f32[16,5504]{1,0:T(8,128)S(1)}, u32[]{:S(2)}, u32[]{:S(2)}) collective-permute-start(f32[16,5504]{1,0:T(8,128)S(1)} %get-tuple-element.129.refs_0_), channel_id=1, source_target_pairs={{0,2},{1,3},{2,0},{3,1},{4,6},{5,7},{6,4},{7,5},{8,10},{9,11},{10,... | collective-permute-start | bytes 1056776 | tf_op jit(solution)/shard_map/ppermute | solution.py:30
  99.8 11.4 %collective-permute-start.12 = (f32[16,5504]{1,0:T(8,128)}, f32[16,5504]{1,0:T(8,128)S(1)}, u32[]{:S(2)}, u32[]{:S(2)}) collective-permute-start(f32[16,5504]{1,0:T(8,128)} %get-tuple-element.114.refs_0_), channel_id=1, source_target_pairs={{0,1},{1,0},{2,3},{3,2},{4,5},{5,4},{6,7},{7,6},{8,9},{9,8},{10,11... | collective-permute-start | bytes 1056776 | tf_op jit(solution)/shard_map/ppermute | solution.py:30
  101.2 17.5 %collective-permute-start.13 = (f32[16,5504]{1,0:T(8,128)}, f32[16,5504]{1,0:T(8,128)S(1)}, u32[]{:S(2)}, u32[]{:S(2)}) collective-permute-start(f32[16,5504]{1,0:T(8,128)} %collective-permute-done.11.refs_3_.refs_1_), channel_id=1, source_target_pairs={{0,1},{1,0},{2,3},{3,2},{4,5},{5,4},{6,7},{7,6},{8,9},{9,8},{10,11... | collective-permute-start | bytes 1056776 | tf_op jit(solution)/shard_map/ppermute | solution.py:30
  101.8 31.2 %collective-permute-start.20 = (f32[16,5504]{1,0:T(8,128)}, f32[16,5504]{1,0:T(8,128)S(1)}, u32[]{:S(2)}, u32[]{:S(2)}) collective-permute-start(f32[16,5504]{1,0:T(8,128)} %get-tuple-element.121.refs_0_), channel_id=1, source_target_pairs={{0,2},{1,3},{2,0},{3,1},{4,6},{5,7},{6,4},{7,5},{8,10},{9,11},{10,... | collective-permute-start | bytes 1056776 | tf_op jit(solution)/shard_map/ppermute | solution.py:30
  102.2 30.8 %collective-permute-start.21 = (f32[16,5504]{1,0:T(8,128)}, f32[16,5504]{1,0:T(8,128)S(1)}, u32[]{:S(2)}, u32[]{:S(2)}) collective-permute-start(f32[16,5504]{1,0:T(8,128)} %collective-permute-done.16.refs_4_.refs_1_), channel_id=1, source_target_pairs={{0,2},{1,3},{2,0},{3,1},{4,6},{5,7},{6,4},{7,5},{8,10},{9,11},{10,... | collective-permute-start | bytes 1056776 | tf_op jit(solution)/shard_map/ppermute | solution.py:30
  109.4 34.7 %collective-permute-start.23 = (f32[16,5504]{1,0:T(8,128)S(1)}, f32[16,5504]{1,0:T(8,128)S(1)}, u32[]{:S(2)}, u32[]{:S(2)}) collective-permute-start(f32[16,5504]{1,0:T(8,128)S(1)} %get-tuple-element.129.refs_0_), channel_id=1, source_target_pairs={{0,1},{1,0},{2,3},{3,2},{4,5},{5,4},{6,7},{7,6},{8,9},{9,8},{10,11... | collective-permute-start | bytes 1056776 | tf_op jit(solution)/shard_map/ppermute | solution.py:30
  111.2 23.4 %collective-permute-start.22 = (f32[16,5504]{1,0:T(8,128)S(1)}, f32[16,5504]{1,0:T(8,128)S(1)}, u32[]{:S(2)}, u32[]{:S(2)}) collective-permute-start(f32[16,5504]{1,0:T(8,128)S(1)} %get-tuple-element.133.refs_0_), channel_id=1, source_target_pairs={{0,1},{1,0},{2,3},{3,2},{4,5},{5,4},{6,7},{7,6},{8,9},{9,8},{10,11... | collective-permute-start | bytes 1056776 | tf_op jit(solution)/shard_map/ppermute | solution.py:30
  118.7 32.2 %collective-permute-start.26 = (f32[16,5504]{1,0:T(8,128)S(1)}, f32[16,5504]{1,0:T(8,128)S(1)}, u32[]{:S(2)}, u32[]{:S(2)}) collective-permute-start(f32[16,5504]{1,0:T(8,128)S(1)} %get-tuple-element.133.refs_0_), channel_id=1, source_target_pairs={{0,2},{1,3},{2,0},{3,1},{4,6},{5,7},{6,4},{7,5},{8,10},{9,11},{10,... | collective-permute-start | bytes 1056776 | tf_op jit(solution)/shard_map/ppermute | solution.py:30
  133.0 9.5 %collective-permute-start.25 = (f32[32,1152]{1,0:T(8,128)S(1)}, f32[32,1152]{1,0:T(8,128)S(1)}, u32[]{:S(2)}, u32[]{:S(2)}) collective-permute-start(f32[32,1152]{1,0:T(8,128)S(1)} %get-tuple-element.136), channel_id=1, source_target_pairs={{0,4},{4,0},{8,12},{12,8},{16,20},{20,16},{24,28},{28,24},{1,5},{5... | collective-permute-start | bytes 442376 | tf_op jit(solution)/shard_map/ppermute | solution.py:30
  133.0 11.0 %collective-permute-start.24 = (f32[16,5504]{1,0:T(8,128)S(1)}, f32[16,5504]{1,0:T(8,128)S(1)}, u32[]{:S(2)}, u32[]{:S(2)}) collective-permute-start(f32[16,5504]{1,0:T(8,128)S(1)} %collective-permute-done.19.refs_3_.refs_1_), channel_id=1, source_target_pairs={{0,1},{1,0},{2,3},{3,2},{4,5},{5,4},{6,7},{7,6},{8,9},{9,8},{10,11... | collective-permute-start | bytes 1056776 | tf_op jit(solution)/shard_map/ppermute | solution.py:30
  142.3 8.6 %collective-permute-start.28 = (f32[32,1152]{1,0:T(8,128)S(1)}, f32[32,1152]{1,0:T(8,128)S(1)}, u32[]{:S(2)}, u32[]{:S(2)}) collective-permute-start(f32[32,1152]{1,0:T(8,128)S(1)} %get-tuple-element.141), channel_id=1, source_target_pairs={{0,4},{4,0},{8,12},{12,8},{16,20},{20,16},{24,28},{28,24},{1,5},{5... | collective-permute-start | bytes 442376 | tf_op jit(solution)/shard_map/ppermute | solution.py:30
  142.5 10.5 %collective-permute-start.27 = (f32[16,5504]{1,0:T(8,128)S(1)}, f32[16,5504]{1,0:T(8,128)S(1)}, u32[]{:S(2)}, u32[]{:S(2)}) collective-permute-start(f32[16,5504]{1,0:T(8,128)S(1)} %collective-permute-done.22.refs_7_.refs_1_), channel_id=1, source_target_pairs={{0,2},{1,3},{2,0},{3,1},{4,6},{5,7},{6,4},{7,5},{8,10},{9,11},{10,... | collective-permute-start | bytes 1056776 | tf_op jit(solution)/shard_map/ppermute | solution.py:30
  150.8 14.7 %collective-permute-start.30 = (f32[32,1152]{1,0:T(8,128)S(1)}, f32[32,1152]{1,0:T(8,128)S(1)}, u32[]{:S(2)}, u32[]{:S(2)}) collective-permute-start(f32[32,1152]{1,0:T(8,128)S(1)} %get-tuple-element.148), channel_id=1, source_target_pairs={{0,4},{4,0},{8,12},{12,8},{16,20},{20,16},{24,28},{28,24},{1,5},{5... | collective-permute-start | bytes 442376 | tf_op jit(solution)/shard_map/ppermute | solution.py:30
  159.8 7.8 %collective-permute-start.29 = (f32[32,1152]{1,0:T(8,128)S(1)}, f32[32,1152]{1,0:T(8,128)S(1)}, u32[]{:S(2)}, u32[]{:S(2)}) collective-permute-start(f32[32,1152]{1,0:T(8,128)S(1)} %get-tuple-element.146), channel_id=1, source_target_pairs={{0,4},{4,0},{8,12},{12,8},{16,20},{20,16},{24,28},{28,24},{1,5},{5... | collective-permute-start | bytes 442376 | tf_op jit(solution)/shard_map/ppermute | solution.py:30
  159.8 18.1 %collective-permute-start.31 = (f32[32,1152]{1,0:T(8,128)S(1)}, f32[32,1152]{1,0:T(8,128)S(1)}, u32[]{:S(2)}, u32[]{:S(2)}) collective-permute-start(f32[32,1152]{1,0:T(8,128)S(1)} %get-tuple-element.154), channel_id=1, source_target_pairs={{0,8},{4,12},{8,0},{12,4},{16,24},{20,28},{24,16},{28,20},{1,9},{5... | collective-permute-start | bytes 442376 | tf_op jit(solution)/shard_map/ppermute | solution.py:30
  165.6 12.3 %collective-permute-start.32 = (f32[32,1152]{1,0:T(8,128)S(1)}, f32[32,1152]{1,0:T(8,128)S(1)}, u32[]{:S(2)}, u32[]{:S(2)}) collective-permute-start(f32[32,1152]{1,0:T(8,128)S(1)} %get-tuple-element.155), channel_id=1, source_target_pairs={{0,16},{4,20},{8,24},{12,28},{16,0},{20,4},{24,8},{28,12},{1,17},{... | collective-permute-start | bytes 442376 | tf_op jit(solution)/shard_map/ppermute | solution.py:30
  167.6 12.0 %collective-permute-start.33 = (f32[32,1152]{1,0:T(8,128)S(1)}, f32[32,1152]{1,0:T(8,128)S(1)}, u32[]{:S(2)}, u32[]{:S(2)}) collective-permute-start(f32[32,1152]{1,0:T(8,128)S(1)} %get-tuple-element.156), channel_id=1, source_target_pairs={{0,24},{4,28},{8,16},{12,20},{16,8},{20,12},{24,0},{28,4},{1,25},{... | collective-permute-start | bytes 442376 | tf_op jit(solution)/shard_map/ppermute | solution.py:30
  181.6 7.0 %collective-permute-start.38 = (f32[32,1024]{1,0:T(8,128)}, f32[32,1024]{1,0:T(8,128)S(1)}, u32[]{:S(2)}, u32[]{:S(2)}) collective-permute-start(f32[32,1024]{1,0:T(8,128)} %get-tuple-element.90.refs_2_), channel_id=1, source_target_pairs={{0,8},{4,12},{8,0},{12,4},{16,24},{20,28},{24,16},{28,20},{1,9},{5... | collective-permute-start | bytes 393224 | tf_op jit(solution)/shard_map/ppermute | solution.py:30
  184.6 16.2 %collective-permute-start.34 = (f32[1280,128]{1,0:T(8,128)}, f32[1280,128]{1,0:T(8,128)}, u32[]{:S(2)}, u32[]{:S(2)}) collective-permute-start(f32[1280,128]{1,0:T(8,128)} %get-tuple-element.163.refs_4_.refs_0_.refs_6_), channel_id=1, source_target_pairs={{0,1},{1,0},{2,3},{3,2},{4,5},{5,4},{6,7},{7,6},{8,9},{9,8},{10,11... | collective-permute-start | bytes 1966088 | tf_op jit(solution)/shard_map/ppermute | solution.py:30
  185.1 18.5 %collective-permute-start.48 = (f32[1024,128]{1,0:T(8,128)S(1)}, f32[1024,128]{1,0:T(8,128)S(1)}, u32[]{:S(2)}, u32[]{:S(2)}) collective-permute-start(f32[1024,128]{1,0:T(8,128)S(1)} %copy-done.26), channel_id=1, source_target_pairs={{0,2},{1,3},{2,0},{3,1},{4,6},{5,7},{6,4},{7,5},{8,10},{9,11},{10,... | collective-permute-start | bytes 1572872 | tf_op jit(solution)/shard_map/ppermute | solution.py:30
  186.6 17.0 %collective-permute-start.37 = (f32[32,1024]{1,0:T(8,128)}, f32[32,1024]{1,0:T(8,128)S(1)}, u32[]{:S(2)}, u32[]{:S(2)}) collective-permute-start(f32[32,1024]{1,0:T(8,128)} %get-tuple-element.90.refs_2_), channel_id=1, source_target_pairs={{0,4},{4,0},{8,12},{12,8},{16,20},{20,16},{24,28},{28,24},{1,5},{5... | collective-permute-start | bytes 393224 | tf_op jit(solution)/shard_map/ppermute | solution.py:30
  186.7 15.6 %collective-permute-start.40 = (f32[32,1024]{1,0:T(8,128)}, f32[32,1024]{1,0:T(8,128)S(1)}, u32[]{:S(2)}, u32[]{:S(2)}) collective-permute-start(f32[32,1024]{1,0:T(8,128)} %get-tuple-element.90.refs_2_), channel_id=1, source_target_pairs={{0,16},{4,20},{8,24},{12,28},{16,0},{20,4},{24,8},{28,12},{1,17},{... | collective-permute-start | bytes 393224 | tf_op jit(solution)/shard_map/ppermute | solution.py:30
  188.5 14.4 %collective-permute-start.42 = (f32[32,1024]{1,0:T(8,128)}, f32[32,1024]{1,0:T(8,128)S(1)}, u32[]{:S(2)}, u32[]{:S(2)}) collective-permute-start(f32[32,1024]{1,0:T(8,128)} %get-tuple-element.90.refs_2_), channel_id=1, source_target_pairs={{0,24},{4,28},{8,16},{12,20},{16,8},{20,12},{24,0},{28,4},{1,25},{... | collective-permute-start | bytes 393224 | tf_op jit(solution)/shard_map/ppermute | solution.py:30
  200.8 18.5 %collective-permute-start.35 = (f32[1280,128]{1,0:T(8,128)}, f32[1280,128]{1,0:T(8,128)}, u32[]{:S(2)}, u32[]{:S(2)}) collective-permute-start(f32[1280,128]{1,0:T(8,128)} %get-tuple-element.163.refs_4_.refs_0_.refs_6_), channel_id=1, source_target_pairs={{0,2},{1,3},{2,0},{3,1},{4,6},{5,7},{6,4},{7,5},{8,10},{9,11},{10,... | collective-permute-start | bytes 1966088 | tf_op jit(solution)/shard_map/ppermute | solution.py:30
  202.3 29.2 %collective-permute-start.36 = (f32[1280,128]{1,0:T(8,128)}, f32[1280,128]{1,0:T(8,128)}, u32[]{:S(2)}, u32[]{:S(2)}) collective-permute-start(f32[1280,128]{1,0:T(8,128)} %collective-permute-done.34.refs_5_.refs_1_.refs_7_), channel_id=1, source_target_pairs={{0,2},{1,3},{2,0},{3,1},{4,6},{5,7},{6,4},{7,5},{8,10},{9,11},{10,... | collective-permute-start | bytes 1966088 | tf_op jit(solution)/shard_map/ppermute | solution.py:30
  202.9 10.2 %collective-permute-start.39 = (f32[32,1024]{1,0:T(8,128)}, f32[32,1024]{1,0:T(8,128)}, u32[]{:S(2)}, u32[]{:S(2)}) collective-permute-start(f32[32,1024]{1,0:T(8,128)} %ordered.9.refs_4_), channel_id=1, source_target_pairs={{0,4},{4,0},{8,12},{12,8},{16,20},{20,16},{24,28},{28,24},{1,5},{5... | collective-permute-start | bytes 393224 | tf_op jit(solution)/shard_map/ppermute | solution.py:30
  203.6 10.2 %collective-permute-start.41 = (f32[32,1024]{1,0:T(8,128)}, f32[32,1024]{1,0:T(8,128)}, u32[]{:S(2)}, u32[]{:S(2)}) collective-permute-start(f32[32,1024]{1,0:T(8,128)} %ordered.10.refs_6_), channel_id=1, source_target_pairs={{0,4},{4,0},{8,12},{12,8},{16,20},{20,16},{24,28},{28,24},{1,5},{5... | collective-permute-start | bytes 393224 | tf_op jit(solution)/shard_map/ppermute | solution.py:30
  203.6 11.6 %collective-permute-start.43 = (f32[32,1024]{1,0:T(8,128)}, f32[32,1024]{1,0:T(8,128)}, u32[]{:S(2)}, u32[]{:S(2)}) collective-permute-start(f32[32,1024]{1,0:T(8,128)} %ordered.11.refs_8_), channel_id=1, source_target_pairs={{0,4},{4,0},{8,12},{12,8},{16,20},{20,16},{24,28},{28,24},{1,5},{5... | collective-permute-start | bytes 393224 | tf_op jit(solution)/shard_map/ppermute | solution.py:30
  213.2 29.1 %collective-permute-start.47 = (f32[1024,128]{1,0:T(8,128)S(1)}, f32[1024,128]{1,0:T(8,128)S(1)}, u32[]{:S(2)}, u32[]{:S(2)}) collective-permute-start(f32[1024,128]{1,0:T(8,128)S(1)} %copy-done.26), channel_id=1, source_target_pairs={{0,1},{1,0},{2,3},{3,2},{4,5},{5,4},{6,7},{7,6},{8,9},{9,8},{10,11... | collective-permute-start | bytes 1572872 | tf_op jit(solution)/shard_map/ppermute | solution.py:30
  213.8 28.5 %collective-permute-start.49 = (f32[1024,128]{1,0:T(8,128)S(1)}, f32[1024,128]{1,0:T(8,128)S(1)}, u32[]{:S(2)}, u32[]{:S(2)}) collective-permute-start(f32[1024,128]{1,0:T(8,128)S(1)} %copy-done.28), channel_id=1, source_target_pairs={{0,1},{1,0},{2,3},{3,2},{4,5},{5,4},{6,7},{7,6},{8,9},{9,8},{10,11... | collective-permute-start | bytes 1572872 | tf_op jit(solution)/shard_map/ppermute | solution.py:30
  218.7 23.6 %collective-permute-start.44 = (f32[64,512]{1,0:T(8,128)S(1)}, f32[64,512]{1,0:T(8,128)S(1)}, u32[]{:S(2)}, u32[]{:S(2)}) collective-permute-start(f32[64,512]{1,0:T(8,128)S(1)} %get-tuple-element.172), channel_id=1, source_target_pairs={{0,1},{1,0},{2,3},{3,2},{4,5},{5,4},{6,7},{7,6},{8,9},{9,8},{10,11... | collective-permute-start | bytes 393224 | tf_op jit(solution)/shard_map/ppermute | solution.py:30
  219.3 23.0 %collective-permute-start.45 = (f32[64,512]{1,0:T(8,128)S(1)}, f32[64,512]{1,0:T(8,128)S(1)}, u32[]{:S(2)}, u32[]{:S(2)}) collective-permute-start(f32[64,512]{1,0:T(8,128)S(1)} %get-tuple-element.173), channel_id=1, source_target_pairs={{0,2},{1,3},{2,0},{3,1},{4,6},{5,7},{6,4},{7,5},{8,10},{9,11},{10,... | collective-permute-start | bytes 393224 | tf_op jit(solution)/shard_map/ppermute | solution.py:30
  231.5 13.1 %collective-permute-start.46 = (f32[64,512]{1,0:T(8,128)S(1)}, f32[64,512]{1,0:T(8,128)S(1)}, u32[]{:S(2)}, u32[]{:S(2)}) collective-permute-start(f32[64,512]{1,0:T(8,128)S(1)} %get-tuple-element.174), channel_id=1, source_target_pairs={{0,3},{1,2},{2,1},{3,0},{4,7},{5,6},{6,5},{7,4},{8,11},{9,10},{10,... | collective-permute-start | bytes 393224 | tf_op jit(solution)/shard_map/ppermute | solution.py:30
  (48 other events, 370.8 us)

commit v2 on v1

--- a/solution.py
+++ b/solution.py
@@ -333,10 +333,17 @@
 
 def collect_kernel(*refs):
     rows, left, right = refs[:-2], refs[-2], refs[-1]
-    width = right.shape[2]
+    width = right.shape[1]
     gained = jnp.concatenate([item[:, :width] for item in rows], axis=0)
-    left[0], left[1] = pieces(gained.T)
-    right[0], right[1] = pieces(jnp.concatenate([item[:, width:] for item in rows], axis=0))
+    total = gained.shape[0]
+    high, low = pieces(gained.T)
+    left[:, :total] = high
+    left[:, total : 2 * total] = low
+    left[:, 2 * total :] = high
+    high, low = pieces(jnp.concatenate([item[:, width:] for item in rows], axis=0))
+    right[:total, :] = high
+    right[total : 2 * total, :] = high
+    right[2 * total :, :] = low
 
 
 def collect(rows, after):
@@ -346,8 +353,8 @@
         collect_kernel,
         (1,),
         [whole(item.shape) for item in rows],
-        [whole((2, width, total)), whole((2, total, width))],
-        [shape_of(2, width, total, dtype=bf16), shape_of(2, total, width, dtype=bf16)],
+        [whole((width, 3 * total)), whole((3 * total, width))],
+        [shape_of(width, 3 * total, dtype=bf16), shape_of(3 * total, width, dtype=bf16)],
         moved=16 * total * width,
         after=after,
         limit=VMEM_MOST,
@@ -355,33 +362,47 @@
 
 
 def weight_kernel(flipped, rows, *refs):
-    splits, out = refs[:-1], refs[-1]
-    high = jnp.concatenate([split[0] for split in splits], axis=0)
-    low = jnp.concatenate([split[1] for split in splits], axis=0)
-    held = (rows[0], rows[1])
-    out[...] = dot3((high, low), held, TN) if flipped else dot3(held, (high, low), NN)
+    splits, out, whole_split = refs[:-2], refs[-2], refs[-1]
+    count = splits[0].shape[1]
+    total = count * len(splits)
+
+    @pl.when(pl.program_id(0) == 0)
+    def _():
+        for at, split in enumerate(splits):
+            for place, part in enumerate((0, 1, 0) if flipped else (0, 0, 1)):
+                whole_split[pl.ds(place * total + at * count, count), :] = split[part]
+
+    if flipped:
+        begin = pl.multiple_of(pl.program_id(0) * out.shape[0], TILE)
+        out[...] = dot(whole_split[:, pl.ds(begin, out.shape[0])], rows[...], TN)
+    else:
+        out[...] = dot(rows[...], whole_split[...], NN)
 
 
 def weight_grad(section, rows, splits, hidden, after):
     flipped = section == 2
-    width, total = (rows.shape[2], rows.shape[1]) if flipped else rows.shape[1:]
-    tiles = hidden // TILE
+    total, width = rows.shape if flipped else rows.shape[::-1]
     if flipped:
-        out_spec, out_shape = pl.BlockSpec((TILE, width), lambda j: (j, 0)), (hidden, width)
+        block = TILE
+        out_shape = (hidden, width)
+        row_spec = whole(rows.shape)
     else:
-        out_spec, out_shape = pl.BlockSpec((width, TILE), lambda j: (0, j)), (width, hidden)
+        block = 2 * TILE if width % (2 * TILE) == 0 else TILE
+        out_shape = (width, hidden)
+        row_spec = pl.BlockSpec((block, total), lambda j: (j, 0))
     return call(
         "weight",
         functools.partial(weight_kernel, flipped),
-        (tiles,),
-        [whole(rows.shape)]
+        (out_shape[0] // block,),
+        [row_spec]
         + [
-            pl.BlockSpec((2, split.shape[1], TILE), lambda j: (0, 0, section * tiles + j))
+            pl.BlockSpec((2, split.shape[1], hidden), lambda j: (0, 0, section))
             for split in splits
         ],
-        [out_spec],
+        [pl.BlockSpec((block, out_shape[1]), lambda j: (j, 0))],
         [shape_of(*out_shape)],
-        flops=6 * total * width * hidden,
+        [pltpu.VMEM((total, hidden), bf16)],
+        flops=2 * total * width * hidden,
         moved=4 * width * hidden,
         after=after,
         limit=VMEM_MOST,
@@ -435,7 +456,7 @@
     )(place, first, queries, lse, *keys)
 
 
-def attend_kernel(heads, scale, probs, outs, *refs):
+def attend_kernel(heads, scale, probs, last_probs, outs, *refs):
     out = refs[-1]
     count = (len(refs) - 1) // 3
     douts, keys, values = refs[:count], refs[count : 2 * count], refs[2 * count : 3 * count]
@@ -452,20 +473,24 @@
         for begin in range(0, key_count, TILE):
             part = pl.ds(begin, TILE)
             dprobs = dot3(dout_parts, pieces(values[at][part, :]), NT)
-            weights = probs[:, pl.ds(at * key_count + begin, TILE)] * (dprobs - delta)
+            if at < count - 1:
+                seen = probs[:, pl.ds(at * key_count + begin, TILE)]
+            else:
+                seen = last_probs[:, part]
+            weights = seen * (dprobs - delta)
             total += dot3(pieces(weights), pieces(keys[at][part, :]), NN)
     for head in range(heads):
         out[:, head * HD : (head + 1) * HD] = total[head * rows : (head + 1) * rows] * scale
 
 
-def attend(probs, outs, douts, keys, values, key_count, after):
+def attend(probs, last_probs, outs, douts, keys, values, key_count, after):
     rows, columns = outs.shape
     block = pl.BlockSpec((key_count, HD), lambda i: (0, 0))
     return call(
         "attend",
         functools.partial(attend_kernel, columns // HD, 1.0 / math.sqrt(HD)),
         (1,),
-        [whole(probs.shape), whole(outs.shape)]
+        [whole(probs.shape), whole(last_probs.shape), whole(outs.shape)]
         + [whole(outs.shape)] * len(douts)
         + [block] * (len(keys) + len(values)),
         [whole(outs.shape)],
@@ -473,7 +498,7 @@
         flops=12 * rows * columns * key_count * len(keys),
         moved=4 * (probs.size + 2 * key_count * HD * len(keys)),
         after=after,
-    )(probs, outs, *douts, *keys, *values)
+    )(probs, last_probs, outs, *douts, *keys, *values)
 
 
 def attn_grad_kernel(blocks, place, weight, *refs):
@@ -600,8 +625,7 @@
     )(place, rows_rel, gain, *parts)
 
 
-def save_kernel(heads, keys, values, outs, saved, kept):
-    kept[...] = values[...]
+def save_kernel(heads, keys, outs, saved):
     count = keys.shape[0]
     rows = outs.shape[0]
     saved[pl.ds(0, count), :] = keys[...]
@@ -609,7 +633,7 @@
         saved[pl.ds(count + head * rows, rows), :] = outs[:, head * HD : (head + 1) * HD]
 
 
-def save(keys, values, outs, after):
+def save(keys, outs, after):
     count, rows, columns = keys.shape[0], outs.shape[0], outs.shape[1]
     heads = columns // HD
     total = (count + heads * rows, HD)
@@ -617,12 +641,13 @@
         "save",
         functools.partial(save_kernel, heads),
         (1,),
-        [whole(keys.shape), whole(values.shape), whole(outs.shape)],
-        [whole(total), whole(values.shape)],
-        [shape_of(*total), shape_of(*values.shape)],
+        [whole(keys.shape), whole(outs.shape)],
+        [whole(total)],
+        [shape_of(*total)],
         moved=8 * total[0] * HD,
         after=after,
-    )(keys, values, outs)
+        limit=VMEM_MOST,
+    )(keys, outs)
 
 
 def shards_square(
@@ -715,20 +740,28 @@
     sources[1] = (own, flip(own, "wide", 1))
     later = ordered(rows_again, own)
     arriving = {unit: flip(later, "wide", offsets[unit] * 2) for unit in (2, 3)}
+    saved = save(keys_own, attn_out, chain)
+    keys_near = flip(saved, "ctx", 1)
+    keys_side = flip(saved, "ctx", 2)
+    keys = [saved, keys_near, keys_side, flip(keys_near, "ctx", 2)]
+    outs = [(item, key_count // (heads * rows)) for item in keys]
     begin(0, 1)
+    chain.wait(keys_near, keys_side)
     wide_rows(2, arriving[2])
     wide_rows(3, arriving[3])
     begin(2, 3)
     chain.wait(spots, first_pos, lse_rows)
     half(0)
     half(1)
+    row_parts, grad_parts = collect([stacked[unit] for unit in range(planes)], chain)
     centre(0)
     centre(1)
-    row_parts, grad_parts = collect([stacked[unit] for unit in range(planes)], chain)
-    saved, values_own = save(keys_own, values_own, attn_out, chain)
-    chain.wait(from_second[0], from_second[1])
     half(2)
     half(3)
+    probs = probs_of(
+        places[:-1], first_pos, queries, lse_rows, keys[:-1], key_count, chain
+    )
+    chain.wait(from_second[0], from_second[1])
     centre(2)
     chain.wait(from_second[2])
     centre(3)
@@ -741,31 +774,30 @@
     close(3)
     settle(2)
     settle(3)
+    values_side = flip(values_own, "ctx", 2)
+    values_near = flip(values_own, "ctx", 1)
+    values = [values_own, values_near, values_side, flip(values_side, "ctx", 1)]
     all_splits = [splits[unit] for unit in range(planes)]
     grad_w_gate = weight_grad(0, row_parts, all_splits, hidden, chain)
     parts = [normed_parts[unit] for unit in range(planes)]
     grad_resid = finish(places, rows_rel, gain, parts, square, chain)
 
     across = [flip(grad_resid, "wide", offset * 2) if offset else grad_resid for offset in offsets]
-    keys_near = flip(saved, "ctx", 1)
-    keys_side = flip(saved, "ctx", 2)
-    values_side = flip(values_own, "ctx", 2)
-    values_near = flip(values_own, "ctx", 1)
-    keys = [saved, keys_near, keys_side, flip(keys_near, "ctx", 2)]
-    values = [values_own, values_near, values_side, flip(values_side, "ctx", 1)]
-    outs = [(item, key_count // (heads * rows)) for item in keys]
-
+    chain.wait(values_near, values_side)
     grad_w_up = weight_grad(1, row_parts, all_splits, hidden, chain)
     blocks = []
     for own in across:
         own = ordered(own, *chain.links) if own is not grad_resid else own
         blocks += [own, flip(own, "wide", 1)]
     grad_w_down = weight_grad(2, grad_parts, all_splits, hidden, chain)
+    chain.wait(values[3], keys[3])
     *parts, resid_rows = attn_grad(spots, blocks, w_out, square, chain)
     d_attn = [flip(part, "ctx", rel) if rel else part for rel, part in enumerate(parts)]
-    probs = probs_of(places, first_pos, queries, lse_rows, keys, key_count, chain)
+    last_probs = probs_of(
+        places[-1:], first_pos, queries, lse_rows, keys[-1:], key_count, chain
+    )
     grad_w_out = out_weight_grad(outs, resid_rows, heads, chain)
-    grad_queries = attend(probs, attn_out, d_attn, keys, values, key_count, chain)
+    grad_queries = attend(probs, last_probs, attn_out, d_attn, keys, values, key_count, chain)
     return (grad_w_gate, grad_w_up, grad_w_down, grad_w_out, grad_resid, grad_queries)
 
 

time: 253 us -> 238 us (0.941)
  starting transfers between devices: 59.7 us -> 51.9 us
  waiting for transfers between devices: 60.3 us -> 56 us
  local copies, waits for them, and re-layouts: 22.5 us -> 19.4 us
    ppermute x50, starting transfers between devices: 59.7 us -> 51.9 us  [flip(): return lax.ppermute(block, axis, [(at, at ^ mask) for at in range(count)])]
    ppermute x50, waiting for transfers between devices: 60.3 us -> 56 us  [flip(): return lax.ppermute(block, axis, [(at, at ^ mask) for at in range(count)])]
    unnamed x92 -> x120, local copies, waits for them, and re-layouts: 21.6 us -> 18.5 us
    pallas_call x29 -> x30, Pallas kernels: 107 us -> 108 us  [apply(): *results, link = run(*operands, *after.links)]
  transfers between devices with their start and end apart: 50 -> 50, of which waited for: 15 -> 14; matrix products, arithmetic and copies ran while one was open for 0% -> 0% of each run, Pallas kernels for 39% -> 41%
where the time goes in v2:
time: 238 us; the launch traced here: 237 us
  Pallas kernels  108 us (45%)
  waiting for transfers between devices  56 us (24%)
  starting transfers between devices  51.9 us (22%)
  local copies, waits for them, and re-layouts  19.4 us (8%)
    pallas_call x30, Pallas kernels, apply(): *results, link = run(*operands, *after.links)  108 us
    ppermute x50, waiting for transfers between devices, flip(): return lax.ppermute(block, axis, [(at, at ^ mask) for at in range(count)])  56 us
    ppermute x50, starting transfers between devices, flip(): return lax.ppermute(block, axis, [(at, at ^ mask) for at in range(count)])  51.9 us
    unnamed x120, local copies, waits for them, and re-layouts  18.5 us
  transfers between devices with their start and end apart: 50, of which 14 were waited for; matrix products, arithmetic and copies ran while one was open for 0% of the time, Pallas kernels for 41%

profile of v2, /device:TPU:0, one launch (start us, length us, event | category | flops | bytes accessed | tf_op | source)
XLA Modules:
  0.0 237.3 jit_solution(7596588625365609789)
XLA Ops:
  1.2 1.8 arrange.1
  3.0 3.0 %collective-permute-start.1 = (f32[32,2048]{1,0:T(8,128)}, f32[32,2048]{1,0:T(8,128)S(1)}, u32[]{:S(2)}, u32[]{:S(2)}) collective-permute-start(f32[32,2048]{1,0:T(8,128)} %get-tuple-element.94.refs_0_), channel_id=1, source_target_pairs={{0,8},{4,12},{8,0},{12,4},{16,24},{20,28},{24,16},{28,20},{1,9},{5... | collective-permute-start | bytes 786440 | tf_op jit(solution)/shard_map/ppermute | solution.py:30
  6.0 6.5 %collective-permute-done.1.refs_2_.refs_1_ = f32[32,2048]{1,0:T(8,128)S(1)} collective-permute-done((f32[32,2048]{1,0:T(8,128)}, f32[32,2048]{1,0:T(8,128)S(1)}, u32[]{:S(2)}, u32[]{:S(2)}) %collective-permute-start.1) | collective-permute-done | bytes 262176 | tf_op jit(solution)/shard_map/ppermute | solution.py:30
  12.6 2.1 save.1
  14.6 1.7 collective-permute-start.4
  16.3 1.5 collective-permute-start.5
  17.8 2.6 %collective-permute-start.3 = (f32[32,2048]{1,0:T(8,128)}, f32[32,2048]{1,0:T(8,128)S(1)}, u32[]{:S(2)}, u32[]{:S(2)}) collective-permute-start(f32[32,2048]{1,0:T(8,128)} %ordered.6), channel_id=1, source_target_pairs={{0,16},{4,20},{8,24},{12,28},{16,0},{20,4},{24,8},{28,12},{1,17},{... | collective-permute-start | bytes 786440 | tf_op jit(solution)/shard_map/ppermute | solution.py:30
  22.5 13.9 %partial.2 = (f32[32,5504]{1,0:T(8,128)}, f32[32,5504]{1,0:T(8,128)}, f32[64,2048]{1,0:T(8,128)}, f32[32,5504]{1,0:T(8,128)}, f32[32,5504]{1,0:T(8,128)}, /*index=5*/f32[64,2048]{1,0:T(8,128)}, f32[8,128]{1,0:T(8,128)}) custom-call(f32[32,2048]{1,0:T(8,128)} %get-tuple-element.93.refs_0_.refs_1_, f32[32,2048]{1,0:T(8,128)} %copy-done.52, ...), custom_call_target="tpu_custom_call" | custom-call | flops 16911433728 | bytes 88080384 | tf_op jit(solution)/shard_map/partial/pallas_call | solution.py:93
  36.4 3.0 %collective-permute-done.3.refs_0_ = f32[32,2048]{1,0:T(8,128)S(1)} collective-permute-done((f32[32,2048]{1,0:T(8,128)}, f32[32,2048]{1,0:T(8,128)S(1)}, u32[]{:S(2)}, u32[]{:S(2)}) %collective-permute-start.3) | collective-permute-done | bytes 262176 | tf_op jit(solution)/shard_map/ppermute | solution.py:30
  44.1 13.9 %partial.3 = (f32[32,5504]{1,0:T(8,128)}, f32[32,5504]{1,0:T(8,128)}, f32[64,2048]{1,0:T(8,128)}, f32[32,5504]{1,0:T(8,128)}, f32[32,5504]{1,0:T(8,128)}, /*index=5*/f32[64,2048]{1,0:T(8,128)}, f32[8,128]{1,0:T(8,128)}) custom-call(f32[32,2048]{1,0:T(8,128)} %ordered.7.refs_0_, f32[32,2048]{1,0:T(8,128)} %copy-done.54, f32[32,2048]{1,0:T(8,128)} %ordered.8.refs_2_, ...), custom_call_target="tpu_custom_call" | custom-call | flops 16911433728 | bytes 88080384 | tf_op jit(solution)/shard_map/partial/pallas_call | solution.py:93
  58.0 1.7 collective-permute-start.16
  59.7 1.5 collective-permute-start.15
  62.2 1.9 fold.4
  66.8 3.7 %collect.1 = (bf16[1024,768]{1,0:T(8,128)(2,1)}, bf16[768,1024]{1,0:T(8,128)(2,1)}, f32[8,128]{1,0:T(8,128)}) custom-call(f32[64,2048]{1,0:T(8,128)} %get-tuple-element.97.refs_0_, f32[64,2048]{1,0:T(8,128)} %get-tuple-element.98.refs_1_, f32[64,2048]{1,0:T(8,128)} %get-tuple-element.101.refs_2_, f32[64,2048]{1,0:T(8,128)} %get-tuple-element.102.refs_3_, ...), custom_call_target="tpu_custom_call" | custom-call | bytes 16777216 | tf_op jit(solution)/shard_map/collect/pallas_call | solution.py:93
  70.4 14.0 %collective-permute-done.11.refs_1_ = f32[16,5504]{1,0:T(8,128)} collective-permute-done((f32[16,5504]{1,0:T(8,128)}, f32[16,5504]{1,0:T(8,128)}, u32[]{:S(2)}, u32[]{:S(2)}) %collective-permute-start.11) | collective-permute-done | bytes 352288 | tf_op jit(solution)/shard_map/ppermute | solution.py:30
  87.6 1.5 collective-permute-start.12
  92.4 1.6 collective-permute-start.18
  94.5 3.4 %probs.2 = (f32[256,3072]{1,0:T(8,128)S(1)}, f32[8,128]{1,0:T(8,128)S(1)}) custom-call(s32[3]{0:T(128)S(1)} %bitcast.16, s32[1]{0:T(128)} %bitcast.10.refs_4_.refs_1_, f32[64,512]{1,0:T(8,128)S(1)} %copy-done.35, f32[256,1]{1,0:T(8,128)S(1)} %reshape.20.refs_5_.refs_3_, f32[1280,128]{1,0:T(8,128)S(1)} %copy-done.27, f32[1280,128]{1,0:T(8,128)S(1)} %copy-done.1, ...), custom_call_target="tpu_custom_call" | custom-call | flops 4831838208 | bytes 12582912 | tf_op jit(solution)/shard_map/probs/pallas_call | solution.py:93
  97.9 1.7 copy-done.45
  99.6 2.0 collective-permute-done.20.refs_4_.refs_1_
  101.6 1.9 collective-permute-done.19.refs_1_
  109.4 5.6 %collective-permute-done.21.refs_3_.refs_1_ = f32[16,5504]{1,0:T(8,128)S(1)} collective-permute-done((f32[16,5504]{1,0:T(8,128)S(1)}, f32[16,5504]{1,0:T(8,128)S(1)}, u32[]{:S(2)}, u32[]{:S(2)}) %collective-permute-start.21) | collective-permute-done | bytes 352288 | tf_op jit(solution)/shard_map/ppermute | solution.py:30
  117.5 6.6 %collective-permute-done.14.refs_3_ = f32[16,5504]{1,0:T(8,128)S(1)} collective-permute-done((f32[16,5504]{1,0:T(8,128)S(1)}, f32[16,5504]{1,0:T(8,128)S(1)}, u32[]{:S(2)}, u32[]{:S(2)}) %collective-permute-start.14) | collective-permute-done | bytes 352288 | tf_op jit(solution)/shard_map/ppermute | solution.py:30
  124.7 5.4 %normed.4 = (f32[32,1152]{1,0:T(8,128)S(1)}, f32[32,1152]{1,0:T(8,128)S(1)}, bf16[2,64,5376]{2,1,0:T(8,128)(2,1)S(1)}, f32[8,128]{1,0:T(8,128)S(1)}) custom-call(f32[16,5504]{1,0:T(8,128)S(1)} %get-tuple-element.114.refs_0_, f32[16,5504]{1,0:T(8,128)S(1)} %collective-permute-done.12.refs_3_.refs_1_, f32[16,5504]{1,0:T(8,128)S(1)} %collective-permute-done.13.refs_2_, ...), custom_call_target="tpu_custom_call" | custom-call | flops 5637144576 | bytes 58720256 | tf_op jit(solution)/shard_map/normed/pallas_call | solution.py:93
  131.2 2.6 %collective-permute-done.22.refs_2_ = f32[16,5504]{1,0:T(8,128)S(1)} collective-permute-done((f32[16,5504]{1,0:T(8,128)S(1)}, f32[16,5504]{1,0:T(8,128)S(1)}, u32[]{:S(2)}, u32[]{:S(2)}) %collective-permute-start.22) | collective-permute-done | bytes 352288 | tf_op jit(solution)/shard_map/ppermute | solution.py:30
  135.3 6.0 %collective-permute-done.23.refs_3_ = f32[16,5504]{1,0:T(8,128)S(1)} collective-permute-done((f32[16,5504]{1,0:T(8,128)S(1)}, f32[16,5504]{1,0:T(8,128)S(1)}, u32[]{:S(2)}, u32[]{:S(2)}) %collective-permute-start.23) | collective-permute-done | bytes 352288 | tf_op jit(solution)/shard_map/ppermute | solution.py:30
  141.4 1.8 collective-permute-start.26
  143.2 5.4 %normed.5 = (f32[32,1152]{1,0:T(8,128)S(1)}, f32[32,1152]{1,0:T(8,128)S(1)}, bf16[2,64,5376]{2,1,0:T(8,128)(2,1)S(1)}, f32[8,128]{1,0:T(8,128)S(1)}) custom-call(f32[16,5504]{1,0:T(8,128)S(1)} %get-tuple-element.130.refs_0_, f32[16,5504]{1,0:T(8,128)S(1)} %collective-permute-done.20.refs_4_.refs_1_, f32[16,5504]{1,0:T(8,128)S(1)} %collective-permute-done.22.refs_2_, ...), custom_call_target="tpu_custom_call" | custom-call | flops 5637144576 | bytes 58720256 | tf_op jit(solution)/shard_map/normed/pallas_call | solution.py:93
  150.4 1.7 collective-permute-done.26.refs_3_
  152.1 5.4 %normed.6 = (f32[32,1152]{1,0:T(8,128)S(1)}, f32[32,1152]{1,0:T(8,128)S(1)}, bf16[2,64,5376]{2,1,0:T(8,128)(2,1)S(1)}, f32[8,128]{1,0:T(8,128)S(1)}) custom-call(f32[16,5504]{1,0:T(8,128)S(1)} %get-tuple-element.132.refs_0_, f32[16,5504]{1,0:T(8,128)S(1)} %collective-permute-done.21.refs_3_.refs_1_, f32[16,5504]{1,0:T(8,128)S(1)} %collective-permute-done.25.refs_2_, ...), custom_call_target="tpu_custom_call" | custom-call | flops 5637144576 | bytes 58720256 | tf_op jit(solution)/shard_map/normed/pallas_call | solution.py:93
  160.5 5.4 %normed.7 = (f32[32,1152]{1,0:T(8,128)S(1)}, f32[32,1152]{1,0:T(8,128)S(1)}, bf16[2,64,5376]{2,1,0:T(8,128)(2,1)S(1)}, f32[8,128]{1,0:T(8,128)S(1)}) custom-call(f32[16,5504]{1,0:T(8,128)S(1)} %get-tuple-element.136.refs_0_, f32[16,5504]{1,0:T(8,128)S(1)} %collective-permute-done.24.refs_7_.refs_1_, f32[16,5504]{1,0:T(8,128)S(1)} %collective-permute-done.28.refs_2_, ...), custom_call_target="tpu_custom_call" | custom-call | flops 5637144576 | bytes 58720256 | tf_op jit(solution)/shard_map/normed/pallas_call | solution.py:93
  169.7 3.7 %collective-permute-start.33 = (f32[32,1152]{1,0:T(8,128)}, f32[32,1152]{1,0:T(8,128)S(1)}, u32[]{:S(2)}, u32[]{:S(2)}) collective-permute-start(f32[32,1152]{1,0:T(8,128)} %get-tuple-element.157), channel_id=1, source_target_pairs={{0,8},{4,12},{8,0},{12,4},{16,24},{20,28},{24,16},{28,20},{1,9},{5... | collective-permute-start | bytes 442376 | tf_op jit(solution)/shard_map/ppermute | solution.py:30
  174.1 1.8 collective-permute-start.34
  176.0 1.5 collective-permute-start.35
  177.5 7.0 %weight.3 = (f32[1024,1792]{1,0:T(8,128)}, f32[8,128]{1,0:T(8,128)}) custom-call(bf16[1024,768]{1,0:T(8,128)(2,1)} %get-tuple-element.110.refs_0_, bf16[2,64,5376]{2,1,0:T(8,128)(2,1)} %copy-done.42, bf16[2,64,5376]{2,1,0:T(8,128)(2,1)} %copy-done.41, bf16[2,64,5376]{2,1,0:T(8,128)(2,1)} %copy-done.43, bf16[2,64,5376]{2,1,0:T(8,128)(2,1)} %copy-done.44, ...), custom_call_target="tpu_custom_call" | custom-call | flops 11274289152 | bytes 29360128 | tf_op jit(solution)/shard_map/weight/pallas_call | solution.py:93
  184.5 1.6 collective-permute-start.38
  186.0 2.1 collective-permute-done.34.refs_5_
  190.7 2.5 %collective-permute-start.40 = (f32[32,1024]{1,0:T(8,128)}, f32[32,1024]{1,0:T(8,128)S(1)}, u32[]{:S(2)}, u32[]{:S(2)}) collective-permute-start(f32[32,1024]{1,0:T(8,128)} %get-tuple-element.91.refs_2_), channel_id=1, source_target_pairs={{0,8},{4,12},{8,0},{12,4},{16,24},{20,28},{24,16},{28,20},{1,9},{5... | collective-permute-start | bytes 393224 | tf_op jit(solution)/shard_map/ppermute | solution.py:30
  193.1 1.7 collective-permute-start.42
  194.8 1.5 collective-permute-start.44
  196.3 6.9 %weight.4 = (f32[1024,1792]{1,0:T(8,128)}, f32[8,128]{1,0:T(8,128)}) custom-call(bf16[1024,768]{1,0:T(8,128)(2,1)} %get-tuple-element.110.refs_0_, bf16[2,64,5376]{2,1,0:T(8,128)(2,1)} %copy-done.42, bf16[2,64,5376]{2,1,0:T(8,128)(2,1)} %copy-done.41, bf16[2,64,5376]{2,1,0:T(8,128)(2,1)} %copy-done.43, bf16[2,64,5376]{2,1,0:T(8,128)(2,1)} %copy-done.44, ...), custom_call_target="tpu_custom_call" | custom-call | flops 11274289152 | bytes 29360128 | tf_op jit(solution)/shard_map/weight/pallas_call | solution.py:93
  203.9 2.1 collective-permute-done.42.refs_0_
  207.3 8.6 %weight.5 = (f32[1792,1024]{1,0:T(8,128)}, f32[8,128]{1,0:T(8,128)}) custom-call(bf16[768,1024]{1,0:T(8,128)(2,1)} %get-tuple-element.163.refs_0_, bf16[2,64,5376]{2,1,0:T(8,128)(2,1)} %copy-done.42, bf16[2,64,5376]{2,1,0:T(8,128)(2,1)} %copy-done.41, bf16[2,64,5376]{2,1,0:T(8,128)(2,1)} %copy-done.43, bf16[2,64,5376]{2,1,0:T(8,128)(2,1)} %copy-done.44, ...), custom_call_target="tpu_custom_call" | custom-call | flops 11274289152 | bytes 29360128 | tf_op jit(solution)/shard_map/weight/pallas_call | solution.py:93
  218.3 2.7 %attn_grad.1 = (f32[64,512]{1,0:T(8,128)S(1)}, f32[64,512]{1,0:T(8,128)S(1)}, f32[64,512]{1,0:T(8,128)S(1)}, f32[64,512]{1,0:T(8,128)S(1)}, f32[256,1024]{1,0:T(8,128)S(1)}, /*index=5*/f32[8,128]{1,0:T(8,128)S(1)}) custom-call(s32[8]{0:T(128)S(1)} %copy-done.25, f32[512,1024]{1,0:T(8,128)S(1)} %copy-done.26, f32[32,1024]{1,0:T(8,128)} %get-tuple-element.91.refs_2_, ...), custom_call_target="tpu_custom_call" | custom-call | flops 3221225472 | bytes 8388608 | tf_op jit(solution)/shard_map/attn_grad/pallas_call | solution.py:93
  222.1 1.5 collective-permute-start.48
  224.5 2.9 %probs.3 = (f32[256,1024]{1,0:T(8,128)S(1)}, f32[8,128]{1,0:T(8,128)S(1)}) custom-call(s32[1]{0:T(128)} %slice.7.refs_0_, s32[1]{0:T(128)} %bitcast.10.refs_4_.refs_1_, f32[64,512]{1,0:T(8,128)S(1)} %copy-done.36, f32[256,1]{1,0:T(8,128)S(1)} %reshape.20.refs_5_.refs_3_, f32[1280,128]{1,0:T(8,128)} %collective-permute-done.38.refs_12_.refs_4_.refs_3_.refs_10_, ...), custom_call_target="tpu_custom_call" | custom-call | flops 1610612736 | bytes 4194304 | tf_op jit(solution)/shard_map/probs/pallas_call | solution.py:93
  227.5 3.9 %out_weight.1 = (f32[512,1024]{1,0:T(8,128)}, f32[8,128]{1,0:T(8,128)S(1)}) custom-call(f32[1280,128]{1,0:T(8,128)S(1)} %copy-done.28, f32[1280,128]{1,0:T(8,128)S(1)} %copy-done.1, f32[1280,128]{1,0:T(8,128)S(1)} %copy-done.3, f32[1280,128]{1,0:T(8,128)} %collective-permute-done.38.refs_12_.refs_4_.refs_3_.refs_10_, ...), custom_call_target="tpu_custom_call" | custom-call | flops 3221225472 | bytes 8388608 | tf_op jit(solution)/shard_map/out_weight/pallas_call | solution.py:93
  231.5 5.8 %attend.1 = (f32[64,512]{1,0:T(8,128)}, f32[8,128]{1,0:T(8,128)}) custom-call(f32[256,3072]{1,0:T(8,128)S(1)} %copy-done.46, f32[256,1024]{1,0:T(8,128)S(1)} %get-tuple-element.173.refs_1_, f32[64,512]{1,0:T(8,128)S(1)} %copy-done.11, f32[64,512]{1,0:T(8,128)S(1)} %get-tuple-element.174.refs_3_, f32[64,512]{1,0:T(8,128)S(1)} %collective-permute-done.47.refs_4_, ...), custom_call_target="tpu_custom_call" | custom-call | flops 6442450944 | bytes 29360128 | tf_op jit(solution)/shard_map/attend/pallas_call | solution.py:93
  (215 shorter events, 47.4 us)
Async XLA Ops:
  3.0 9.5 %collective-permute-start.1 = (f32[32,2048]{1,0:T(8,128)}, f32[32,2048]{1,0:T(8,128)S(1)}, u32[]{:S(2)}, u32[]{:S(2)}) collective-permute-start(f32[32,2048]{1,0:T(8,128)} %get-tuple-element.94.refs_0_), channel_id=1, source_target_pairs={{0,8},{4,12},{8,0},{12,4},{16,24},{20,28},{24,16},{28,20},{1,9},{5... | collective-permute-start | bytes 786440 | tf_op jit(solution)/shard_map/ppermute | solution.py:30
  6.0 14.4 %collective-permute-start = (f32[32,2048]{1,0:T(8,128)}, f32[32,2048]{1,0:T(8,128)S(1)}, u32[]{:S(2)}, u32[]{:S(2)}) collective-permute-start(f32[32,2048]{1,0:T(8,128)} %get-tuple-element.93.refs_0_.refs_1_), channel_id=1, source_target_pairs={{0,4},{4,0},{8,12},{12,8},{16,20},{20,16},{24,28},{28,24},{1,5},{5... | collective-permute-start | bytes 786440 | tf_op jit(solution)/shard_map/ppermute | solution.py:30
  12.6 9.2 %collective-permute-start.2 = (f32[32,2048]{1,0:T(8,128)S(1)}, f32[32,2048]{1,0:T(8,128)S(1)}, u32[]{:S(2)}, u32[]{:S(2)}) collective-permute-start(f32[32,2048]{1,0:T(8,128)S(1)} %collective-permute-done.1.refs_2_.refs_1_), channel_id=1, source_target_pairs={{0,4},{4,0},{8,12},{12,8},{16,20},{20,16},{24,28},{28,24},{1,5},{5... | collective-permute-start | bytes 786440 | tf_op jit(solution)/shard_map/ppermute | solution.py:30
  14.6 24.7 %collective-permute-start.4 = (f32[1280,128]{1,0:T(8,128)}, f32[1280,128]{1,0:T(8,128)S(1)}, u32[]{:S(2)}, u32[]{:S(2)}) collective-permute-start(f32[1280,128]{1,0:T(8,128)} %get-tuple-element.100.refs_4_.refs_0_.refs_7_), channel_id=1, source_target_pairs={{0,1},{1,0},{2,3},{3,2},{4,5},{5,4},{6,7},{7,6},{8,9},{9,8},{10,11... | collective-permute-start | bytes 1966088 | tf_op jit(solution)/shard_map/ppermute | solution.py:30
  16.3 23.1 %collective-permute-start.5 = (f32[1280,128]{1,0:T(8,128)}, f32[1280,128]{1,0:T(8,128)S(1)}, u32[]{:S(2)}, u32[]{:S(2)}) collective-permute-start(f32[1280,128]{1,0:T(8,128)} %get-tuple-element.100.refs_4_.refs_0_.refs_7_), channel_id=1, source_target_pairs={{0,2},{1,3},{2,0},{3,1},{4,6},{5,7},{6,4},{7,5},{8,10},{9,11},{10,... | collective-permute-start | bytes 1966088 | tf_op jit(solution)/shard_map/ppermute | solution.py:30
  17.8 21.5 %collective-permute-start.3 = (f32[32,2048]{1,0:T(8,128)}, f32[32,2048]{1,0:T(8,128)S(1)}, u32[]{:S(2)}, u32[]{:S(2)}) collective-permute-start(f32[32,2048]{1,0:T(8,128)} %ordered.6), channel_id=1, source_target_pairs={{0,16},{4,20},{8,24},{12,28},{16,0},{20,4},{24,8},{28,12},{1,17},{... | collective-permute-start | bytes 786440 | tf_op jit(solution)/shard_map/ppermute | solution.py:30
  20.4 20.2 %collective-permute-start.7 = (f32[32,2048]{1,0:T(8,128)}, f32[32,2048]{1,0:T(8,128)S(1)}, u32[]{:S(2)}, u32[]{:S(2)}) collective-permute-start(f32[32,2048]{1,0:T(8,128)} %ordered.6), channel_id=1, source_target_pairs={{0,24},{4,28},{8,16},{12,20},{16,8},{20,12},{24,0},{28,4},{1,25},{... | collective-permute-start | bytes 786440 | tf_op jit(solution)/shard_map/ppermute | solution.py:30
  41.8 23.5 %collective-permute-start.9 = (f32[32,5504]{1,0:T(8,128)}, f32[32,5504]{1,0:T(8,128)S(1)}, u32[]{:S(2)}, u32[]{:S(2)}) collective-permute-start(f32[32,5504]{1,0:T(8,128)} %get-tuple-element.104), channel_id=1, source_target_pairs={{0,2},{1,3},{2,0},{3,1},{4,6},{5,7},{6,4},{7,5},{8,10},{9,11},{10,... | collective-permute-start | bytes 2113544 | tf_op jit(solution)/shard_map/ppermute | solution.py:30
  42.3 19.2 %collective-permute-start.10 = (f32[32,5504]{1,0:T(8,128)}, f32[32,5504]{1,0:T(8,128)}, u32[]{:S(2)}, u32[]{:S(2)}) collective-permute-start(f32[32,5504]{1,0:T(8,128)} %get-tuple-element.106), channel_id=1, source_target_pairs={{0,1},{1,0},{2,3},{3,2},{4,5},{5,4},{6,7},{7,6},{8,9},{9,8},{10,11... | collective-permute-start | bytes 2113544 | tf_op jit(solution)/shard_map/ppermute | solution.py:30
  58.0 32.9 %collective-permute-start.16 = (f32[32,5504]{1,0:T(8,128)}, f32[32,5504]{1,0:T(8,128)}, u32[]{:S(2)}, u32[]{:S(2)}) collective-permute-start(f32[32,5504]{1,0:T(8,128)} %get-tuple-element.118), channel_id=1, source_target_pairs={{0,1},{1,0},{2,3},{3,2},{4,5},{5,4},{6,7},{7,6},{8,9},{9,8},{10,11... | collective-permute-start | bytes 2113544 | tf_op jit(solution)/shard_map/ppermute | solution.py:30
  59.7 32.6 %collective-permute-start.15 = (f32[32,5504]{1,0:T(8,128)}, f32[32,5504]{1,0:T(8,128)S(1)}, u32[]{:S(2)}, u32[]{:S(2)}) collective-permute-start(f32[32,5504]{1,0:T(8,128)} %get-tuple-element.116), channel_id=1, source_target_pairs={{0,2},{1,3},{2,0},{3,1},{4,6},{5,7},{6,4},{7,5},{8,10},{9,11},{10,... | collective-permute-start | bytes 2113544 | tf_op jit(solution)/shard_map/ppermute | solution.py:30
  64.9 19.6 %collective-permute-start.11 = (f32[16,5504]{1,0:T(8,128)}, f32[16,5504]{1,0:T(8,128)}, u32[]{:S(2)}, u32[]{:S(2)}) collective-permute-start(f32[16,5504]{1,0:T(8,128)} %get-tuple-element.112), channel_id=1, source_target_pairs={{0,2},{1,3},{2,0},{3,1},{4,6},{5,7},{6,4},{7,5},{8,10},{9,11},{10,... | collective-permute-start | bytes 1056776 | tf_op jit(solution)/shard_map/ppermute | solution.py:30
  66.2 22.9 %collective-permute-start.17 = (f32[16,5504]{1,0:T(8,128)}, f32[16,5504]{1,0:T(8,128)}, u32[]{:S(2)}, u32[]{:S(2)}) collective-permute-start(f32[16,5504]{1,0:T(8,128)} %get-tuple-element.120), channel_id=1, source_target_pairs={{0,1},{1,0},{2,3},{3,2},{4,5},{5,4},{6,7},{7,6},{8,9},{9,8},{10,11... | collective-permute-start | bytes 1056776 | tf_op jit(solution)/shard_map/ppermute | solution.py:30
  87.6 12.0 %collective-permute-start.12 = (f32[16,5504]{1,0:T(8,128)S(1)}, f32[16,5504]{1,0:T(8,128)S(1)}, u32[]{:S(2)}, u32[]{:S(2)}) collective-permute-start(f32[16,5504]{1,0:T(8,128)S(1)} %get-tuple-element.114.refs_0_), channel_id=1, source_target_pairs={{0,2},{1,3},{2,0},{3,1},{4,6},{5,7},{6,4},{7,5},{8,10},{9,11},{10,... | collective-permute-start | bytes 1056776 | tf_op jit(solution)/shard_map/ppermute | solution.py:30
  90.4 11.2 %collective-permute-start.20 = (f32[16,5504]{1,0:T(8,128)S(1)}, f32[16,5504]{1,0:T(8,128)S(1)}, u32[]{:S(2)}, u32[]{:S(2)}) collective-permute-start(f32[16,5504]{1,0:T(8,128)S(1)} %get-tuple-element.130.refs_0_), channel_id=1, source_target_pairs={{0,1},{1,0},{2,3},{3,2},{4,5},{5,4},{6,7},{7,6},{8,9},{9,8},{10,11... | collective-permute-start | bytes 1056776 | tf_op jit(solution)/shard_map/ppermute | solution.py:30
  92.4 15.5 %collective-permute-start.18 = (f32[16,5504]{1,0:T(8,128)S(1)}, f32[16,5504]{1,0:T(8,128)S(1)}, u32[]{:S(2)}, u32[]{:S(2)}) collective-permute-start(f32[16,5504]{1,0:T(8,128)S(1)} %get-tuple-element.125), channel_id=1, source_target_pairs={{0,1},{1,0},{2,3},{3,2},{4,5},{5,4},{6,7},{7,6},{8,9},{9,8},{10,11... | collective-permute-start | bytes 1056776 | tf_op jit(solution)/shard_map/ppermute | solution.py:30
  93.9 9.6 %collective-permute-start.19 = (f32[16,5504]{1,0:T(8,128)S(1)}, f32[16,5504]{1,0:T(8,128)S(1)}, u32[]{:S(2)}, u32[]{:S(2)}) collective-permute-start(f32[16,5504]{1,0:T(8,128)S(1)} %get-tuple-element.127), channel_id=1, source_target_pairs={{0,2},{1,3},{2,0},{3,1},{4,6},{5,7},{6,4},{7,5},{8,10},{9,11},{10,... | collective-permute-start | bytes 1056776 | tf_op jit(solution)/shard_map/ppermute | solution.py:30
  103.8 11.2 %collective-permute-start.21 = (f32[16,5504]{1,0:T(8,128)S(1)}, f32[16,5504]{1,0:T(8,128)S(1)}, u32[]{:S(2)}, u32[]{:S(2)}) collective-permute-start(f32[16,5504]{1,0:T(8,128)S(1)} %get-tuple-element.132.refs_0_), channel_id=1, source_target_pairs={{0,2},{1,3},{2,0},{3,1},{4,6},{5,7},{6,4},{7,5},{8,10},{9,11},{10,... | collective-permute-start | bytes 1056776 | tf_op jit(solution)/shard_map/ppermute | solution.py:30
  105.4 11.5 %collective-permute-start.13 = (f32[16,5504]{1,0:T(8,128)S(1)}, f32[16,5504]{1,0:T(8,128)S(1)}, u32[]{:S(2)}, u32[]{:S(2)}) collective-permute-start(f32[16,5504]{1,0:T(8,128)S(1)} %get-tuple-element.114.refs_0_), channel_id=1, source_target_pairs={{0,1},{1,0},{2,3},{3,2},{4,5},{5,4},{6,7},{7,6},{8,9},{9,8},{10,11... | collective-permute-start | bytes 1056776 | tf_op jit(solution)/shard_map/ppermute | solution.py:30
  106.0 18.1 %collective-permute-start.14 = (f32[16,5504]{1,0:T(8,128)S(1)}, f32[16,5504]{1,0:T(8,128)S(1)}, u32[]{:S(2)}, u32[]{:S(2)}) collective-permute-start(f32[16,5504]{1,0:T(8,128)S(1)} %collective-permute-done.12.refs_3_.refs_1_), channel_id=1, source_target_pairs={{0,1},{1,0},{2,3},{3,2},{4,5},{5,4},{6,7},{7,6},{8,9},{9,8},{10,11... | collective-permute-start | bytes 1056776 | tf_op jit(solution)/shard_map/ppermute | solution.py:30
  107.4 61.3 %collective-permute-start.37 = (f32[1024,128]{1,0:T(8,128)S(1)}, f32[1024,128]{1,0:T(8,128)S(1)}, u32[]{:S(2)}, u32[]{:S(2)}) collective-permute-start(f32[1024,128]{1,0:T(8,128)S(1)} %bitcast.21), channel_id=1, source_target_pairs={{0,2},{1,3},{2,0},{3,1},{4,6},{5,7},{6,4},{7,5},{8,10},{9,11},{10,... | collective-permute-start | bytes 1572872 | tf_op jit(solution)/shard_map/ppermute | solution.py:30
  107.9 25.9 %collective-permute-start.22 = (f32[16,5504]{1,0:T(8,128)S(1)}, f32[16,5504]{1,0:T(8,128)S(1)}, u32[]{:S(2)}, u32[]{:S(2)}) collective-permute-start(f32[16,5504]{1,0:T(8,128)S(1)} %get-tuple-element.130.refs_0_), channel_id=1, source_target_pairs={{0,2},{1,3},{2,0},{3,1},{4,6},{5,7},{6,4},{7,5},{8,10},{9,11},{10,... | collective-permute-start | bytes 1056776 | tf_op jit(solution)/shard_map/ppermute | solution.py:30
  115.0 26.3 %collective-permute-start.23 = (f32[16,5504]{1,0:T(8,128)S(1)}, f32[16,5504]{1,0:T(8,128)S(1)}, u32[]{:S(2)}, u32[]{:S(2)}) collective-permute-start(f32[16,5504]{1,0:T(8,128)S(1)} %collective-permute-done.20.refs_4_.refs_1_), channel_id=1, source_target_pairs={{0,2},{1,3},{2,0},{3,1},{4,6},{5,7},{6,4},{7,5},{8,10},{9,11},{10,... | collective-permute-start | bytes 1056776 | tf_op jit(solution)/shard_map/ppermute | solution.py:30
  116.9 33.2 %collective-permute-start.25 = (f32[16,5504]{1,0:T(8,128)S(1)}, f32[16,5504]{1,0:T(8,128)S(1)}, u32[]{:S(2)}, u32[]{:S(2)}) collective-permute-start(f32[16,5504]{1,0:T(8,128)S(1)} %get-tuple-element.132.refs_0_), channel_id=1, source_target_pairs={{0,1},{1,0},{2,3},{3,2},{4,5},{5,4},{6,7},{7,6},{8,9},{9,8},{10,11... | collective-permute-start | bytes 1056776 | tf_op jit(solution)/shard_map/ppermute | solution.py:30
  124.1 17.3 %collective-permute-start.24 = (f32[16,5504]{1,0:T(8,128)S(1)}, f32[16,5504]{1,0:T(8,128)S(1)}, u32[]{:S(2)}, u32[]{:S(2)}) collective-permute-start(f32[16,5504]{1,0:T(8,128)S(1)} %get-tuple-element.136.refs_0_), channel_id=1, source_target_pairs={{0,1},{1,0},{2,3},{3,2},{4,5},{5,4},{6,7},{7,6},{8,9},{9,8},{10,11... | collective-permute-start | bytes 1056776 | tf_op jit(solution)/shard_map/ppermute | solution.py:30
  133.8 25.5 %collective-permute-start.28 = (f32[16,5504]{1,0:T(8,128)S(1)}, f32[16,5504]{1,0:T(8,128)S(1)}, u32[]{:S(2)}, u32[]{:S(2)}) collective-permute-start(f32[16,5504]{1,0:T(8,128)S(1)} %get-tuple-element.136.refs_0_), channel_id=1, source_target_pairs={{0,2},{1,3},{2,0},{3,1},{4,6},{5,7},{6,4},{7,5},{8,10},{9,11},{10,... | collective-permute-start | bytes 1056776 | tf_op jit(solution)/shard_map/ppermute | solution.py:30
  141.4 8.4 %collective-permute-start.27 = (f32[32,1152]{1,0:T(8,128)S(1)}, f32[32,1152]{1,0:T(8,128)S(1)}, u32[]{:S(2)}, u32[]{:S(2)}) collective-permute-start(f32[32,1152]{1,0:T(8,128)S(1)} %get-tuple-element.139), channel_id=1, source_target_pairs={{0,4},{4,0},{8,12},{12,8},{16,20},{20,16},{24,28},{28,24},{1,5},{5... | collective-permute-start | bytes 442376 | tf_op jit(solution)/shard_map/ppermute | solution.py:30
  141.4 10.7 %collective-permute-start.26 = (f32[16,5504]{1,0:T(8,128)S(1)}, f32[16,5504]{1,0:T(8,128)S(1)}, u32[]{:S(2)}, u32[]{:S(2)}) collective-permute-start(f32[16,5504]{1,0:T(8,128)S(1)} %collective-permute-done.21.refs_3_.refs_1_), channel_id=1, source_target_pairs={{0,1},{1,0},{2,3},{3,2},{4,5},{5,4},{6,7},{7,6},{8,9},{9,8},{10,11... | collective-permute-start | bytes 1056776 | tf_op jit(solution)/shard_map/ppermute | solution.py:30
  149.8 8.8 %collective-permute-start.30 = (f32[32,1152]{1,0:T(8,128)S(1)}, f32[32,1152]{1,0:T(8,128)S(1)}, u32[]{:S(2)}, u32[]{:S(2)}) collective-permute-start(f32[32,1152]{1,0:T(8,128)S(1)} %get-tuple-element.144), channel_id=1, source_target_pairs={{0,4},{4,0},{8,12},{12,8},{16,20},{20,16},{24,28},{28,24},{1,5},{5... | collective-permute-start | bytes 442376 | tf_op jit(solution)/shard_map/ppermute | solution.py:30
  150.0 10.5 %collective-permute-start.29 = (f32[16,5504]{1,0:T(8,128)S(1)}, f32[16,5504]{1,0:T(8,128)S(1)}, u32[]{:S(2)}, u32[]{:S(2)}) collective-permute-start(f32[16,5504]{1,0:T(8,128)S(1)} %collective-permute-done.24.refs_7_.refs_1_), channel_id=1, source_target_pairs={{0,2},{1,3},{2,0},{3,1},{4,6},{5,7},{6,4},{7,5},{8,10},{9,11},{10,... | collective-permute-start | bytes 1056776 | tf_op jit(solution)/shard_map/ppermute | solution.py:30
  158.6 14.8 %collective-permute-start.32 = (f32[32,1152]{1,0:T(8,128)S(1)}, f32[32,1152]{1,0:T(8,128)S(1)}, u32[]{:S(2)}, u32[]{:S(2)}) collective-permute-start(f32[32,1152]{1,0:T(8,128)S(1)} %get-tuple-element.151), channel_id=1, source_target_pairs={{0,4},{4,0},{8,12},{12,8},{16,20},{20,16},{24,28},{28,24},{1,5},{5... | collective-permute-start | bytes 442376 | tf_op jit(solution)/shard_map/ppermute | solution.py:30
  167.0 8.9 %collective-permute-start.31 = (f32[32,1152]{1,0:T(8,128)S(1)}, f32[32,1152]{1,0:T(8,128)S(1)}, u32[]{:S(2)}, u32[]{:S(2)}) collective-permute-start(f32[32,1152]{1,0:T(8,128)S(1)} %get-tuple-element.149), channel_id=1, source_target_pairs={{0,4},{4,0},{8,12},{12,8},{16,20},{20,16},{24,28},{28,24},{1,5},{5... | collective-permute-start | bytes 442376 | tf_op jit(solution)/shard_map/ppermute | solution.py:30
  167.0 27.8 %collective-permute-start.36 = (f32[1024,128]{1,0:T(8,128)S(1)}, f32[1024,128]{1,0:T(8,128)S(1)}, u32[]{:S(2)}, u32[]{:S(2)}) collective-permute-start(f32[1024,128]{1,0:T(8,128)S(1)} %bitcast.22), channel_id=1, source_target_pairs={{0,1},{1,0},{2,3},{3,2},{4,5},{5,4},{6,7},{7,6},{8,9},{9,8},{10,11... | collective-permute-start | bytes 1572872 | tf_op jit(solution)/shard_map/ppermute | solution.py:30
  168.7 38.6 %collective-permute-start.46 = (f32[1024,128]{1,0:T(8,128)S(1)}, f32[1024,128]{1,0:T(8,128)}, u32[]{:S(2)}, u32[]{:S(2)}) collective-permute-start(f32[1024,128]{1,0:T(8,128)S(1)} %collective-permute-done.37.refs_7_.refs_13_), channel_id=1, source_target_pairs={{0,1},{1,0},{2,3},{3,2},{4,5},{5,4},{6,7},{7,6},{8,9},{9,8},{10,11... | collective-permute-start | bytes 1572872 | tf_op jit(solution)/shard_map/ppermute | solution.py:30
  169.7 14.8 %collective-permute-start.33 = (f32[32,1152]{1,0:T(8,128)}, f32[32,1152]{1,0:T(8,128)S(1)}, u32[]{:S(2)}, u32[]{:S(2)}) collective-permute-start(f32[32,1152]{1,0:T(8,128)} %get-tuple-element.157), channel_id=1, source_target_pairs={{0,8},{4,12},{8,0},{12,4},{16,24},{20,28},{24,16},{28,20},{1,9},{5... | collective-permute-start | bytes 442376 | tf_op jit(solution)/shard_map/ppermute | solution.py:30
  174.1 14.0 %collective-permute-start.34 = (f32[32,1152]{1,0:T(8,128)}, f32[32,1152]{1,0:T(8,128)S(1)}, u32[]{:S(2)}, u32[]{:S(2)}) collective-permute-start(f32[32,1152]{1,0:T(8,128)} %get-tuple-element.158), channel_id=1, source_target_pairs={{0,16},{4,20},{8,24},{12,28},{16,0},{20,4},{24,8},{28,12},{1,17},{... | collective-permute-start | bytes 442376 | tf_op jit(solution)/shard_map/ppermute | solution.py:30
  176.0 12.1 %collective-permute-start.35 = (f32[32,1152]{1,0:T(8,128)S(1)}, f32[32,1152]{1,0:T(8,128)S(1)}, u32[]{:S(2)}, u32[]{:S(2)}) collective-permute-start(f32[32,1152]{1,0:T(8,128)S(1)} %get-tuple-element.159), channel_id=1, source_target_pairs={{0,24},{4,28},{8,16},{12,20},{16,8},{20,12},{24,0},{28,4},{1,25},{... | collective-permute-start | bytes 442376 | tf_op jit(solution)/shard_map/ppermute | solution.py:30
  184.5 31.5 %collective-permute-start.38 = (f32[1280,128]{1,0:T(8,128)S(1)}, f32[1280,128]{1,0:T(8,128)}, u32[]{:S(2)}, u32[]{:S(2)}) collective-permute-start(f32[1280,128]{1,0:T(8,128)S(1)} %copy-done.1), channel_id=1, source_target_pairs={{0,2},{1,3},{2,0},{3,1},{4,6},{5,7},{6,4},{7,5},{8,10},{9,11},{10,... | collective-permute-start | bytes 1966088 | tf_op jit(solution)/shard_map/ppermute | solution.py:30
  190.7 12.6 %collective-permute-start.40 = (f32[32,1024]{1,0:T(8,128)}, f32[32,1024]{1,0:T(8,128)S(1)}, u32[]{:S(2)}, u32[]{:S(2)}) collective-permute-start(f32[32,1024]{1,0:T(8,128)} %get-tuple-element.91.refs_2_), channel_id=1, source_target_pairs={{0,8},{4,12},{8,0},{12,4},{16,24},{20,28},{24,16},{28,20},{1,9},{5... | collective-permute-start | bytes 393224 | tf_op jit(solution)/shard_map/ppermute | solution.py:30
  193.1 12.8 %collective-permute-start.42 = (f32[32,1024]{1,0:T(8,128)}, f32[32,1024]{1,0:T(8,128)S(1)}, u32[]{:S(2)}, u32[]{:S(2)}) collective-permute-start(f32[32,1024]{1,0:T(8,128)} %get-tuple-element.91.refs_2_), channel_id=1, source_target_pairs={{0,16},{4,20},{8,24},{12,28},{16,0},{20,4},{24,8},{28,12},{1,17},{... | collective-permute-start | bytes 393224 | tf_op jit(solution)/shard_map/ppermute | solution.py:30
  194.8 11.8 %collective-permute-start.44 = (f32[32,1024]{1,0:T(8,128)}, f32[32,1024]{1,0:T(8,128)S(1)}, u32[]{:S(2)}, u32[]{:S(2)}) collective-permute-start(f32[32,1024]{1,0:T(8,128)} %get-tuple-element.91.refs_2_), channel_id=1, source_target_pairs={{0,24},{4,28},{8,16},{12,20},{16,8},{20,12},{24,0},{28,4},{1,25},{... | collective-permute-start | bytes 393224 | tf_op jit(solution)/shard_map/ppermute | solution.py:30
  203.2 12.7 %collective-permute-start.39 = (f32[32,1024]{1,0:T(8,128)}, f32[32,1024]{1,0:T(8,128)}, u32[]{:S(2)}, u32[]{:S(2)}) collective-permute-start(f32[32,1024]{1,0:T(8,128)} %get-tuple-element.91.refs_2_), channel_id=1, source_target_pairs={{0,4},{4,0},{8,12},{12,8},{16,20},{20,16},{24,28},{28,24},{1,5},{5... | collective-permute-start | bytes 393224 | tf_op jit(solution)/shard_map/ppermute | solution.py:30
  206.0 10.0 %collective-permute-start.41 = (f32[32,1024]{1,0:T(8,128)}, f32[32,1024]{1,0:T(8,128)}, u32[]{:S(2)}, u32[]{:S(2)}) collective-permute-start(f32[32,1024]{1,0:T(8,128)} %ordered.9.refs_4_), channel_id=1, source_target_pairs={{0,4},{4,0},{8,12},{12,8},{16,20},{20,16},{24,28},{28,24},{1,5},{5... | collective-permute-start | bytes 393224 | tf_op jit(solution)/shard_map/ppermute | solution.py:30
  206.6 9.3 %collective-permute-start.43 = (f32[32,1024]{1,0:T(8,128)}, f32[32,1024]{1,0:T(8,128)}, u32[]{:S(2)}, u32[]{:S(2)}) collective-permute-start(f32[32,1024]{1,0:T(8,128)} %ordered.10.refs_6_), channel_id=1, source_target_pairs={{0,4},{4,0},{8,12},{12,8},{16,20},{20,16},{24,28},{28,24},{1,5},{5... | collective-permute-start | bytes 393224 | tf_op jit(solution)/shard_map/ppermute | solution.py:30
  207.3 8.7 %collective-permute-start.45 = (f32[32,1024]{1,0:T(8,128)}, f32[32,1024]{1,0:T(8,128)S(1)}, u32[]{:S(2)}, u32[]{:S(2)}) collective-permute-start(f32[32,1024]{1,0:T(8,128)} %ordered.11.refs_8_), channel_id=1, source_target_pairs={{0,4},{4,0},{8,12},{12,8},{16,20},{20,16},{24,28},{28,24},{1,5},{5... | collective-permute-start | bytes 393224 | tf_op jit(solution)/shard_map/ppermute | solution.py:30
  221.0 10.4 %collective-permute-start.47 = (f32[64,512]{1,0:T(8,128)S(1)}, f32[64,512]{1,0:T(8,128)S(1)}, u32[]{:S(2)}, u32[]{:S(2)}) collective-permute-start(f32[64,512]{1,0:T(8,128)S(1)} %get-tuple-element.175), channel_id=1, source_target_pairs={{0,1},{1,0},{2,3},{3,2},{4,5},{5,4},{6,7},{7,6},{8,9},{9,8},{10,11... | collective-permute-start | bytes 393224 | tf_op jit(solution)/shard_map/ppermute | solution.py:30
  222.1 9.3 %collective-permute-start.48 = (f32[64,512]{1,0:T(8,128)S(1)}, f32[64,512]{1,0:T(8,128)S(1)}, u32[]{:S(2)}, u32[]{:S(2)}) collective-permute-start(f32[64,512]{1,0:T(8,128)S(1)} %get-tuple-element.176), channel_id=1, source_target_pairs={{0,2},{1,3},{2,0},{3,1},{4,6},{5,7},{6,4},{7,5},{8,10},{9,11},{10,... | collective-permute-start | bytes 393224 | tf_op jit(solution)/shard_map/ppermute | solution.py:30
  223.7 7.7 %collective-permute-start.49 = (f32[64,512]{1,0:T(8,128)S(1)}, f32[64,512]{1,0:T(8,128)S(1)}, u32[]{:S(2)}, u32[]{:S(2)}) collective-permute-start(f32[64,512]{1,0:T(8,128)S(1)} %get-tuple-element.177), channel_id=1, source_target_pairs={{0,3},{1,2},{2,1},{3,0},{4,7},{5,6},{6,5},{7,4},{8,11},{9,10},{10,... | collective-permute-start | bytes 393224 | tf_op jit(solution)/shard_map/ppermute | solution.py:30
  (62 other events, 427.3 us)

commit v3 on v2

--- a/solution.py
+++ b/solution.py
@@ -373,7 +373,7 @@
                 whole_split[pl.ds(place * total + at * count, count), :] = split[part]
 
     if flipped:
-        begin = pl.multiple_of(pl.program_id(0) * out.shape[0], TILE)
+        begin = pl.multiple_of(pl.program_id(0) * out.shape[0], LANES)
         out[...] = dot(whole_split[:, pl.ds(begin, out.shape[0])], rows[...], TN)
     else:
         out[...] = dot(rows[...], whole_split[...], NN)
@@ -383,7 +383,7 @@
     flipped = section == 2
     total, width = rows.shape if flipped else rows.shape[::-1]
     if flipped:
-        block = TILE
+        block = hidden // 2 if hidden % (2 * LANES) == 0 else TILE
         out_shape = (hidden, width)
         row_spec = whole(rows.shape)
     else:
@@ -541,6 +541,7 @@
         flops=6 * total * width * columns,
         moved=4 * width * columns,
         after=after,
+        limit=VMEM_MOST,
     )(place, weight, *sources)
 
 
@@ -622,6 +623,7 @@
         [shape_of(rows, width)],
         moved=4 * rows * width * (len(parts) + 3),
         after=after,
+        limit=VMEM_MOST,
     )(place, rows_rel, gain, *parts)
 
 
@@ -736,11 +738,11 @@
         sources[unit] = (own, flip(own, "wide", 1))
 
     sources[0] = (rows_rel, flip(rows_rel, "wide", 1))
-    own = flip(rows_again, "wide", 2)
+    saved = save(keys_own, attn_out, chain)
+    own = ordered(flip(rows_again, "wide", 2), *chain.links)
     sources[1] = (own, flip(own, "wide", 1))
     later = ordered(rows_again, own)
     arriving = {unit: flip(later, "wide", offsets[unit] * 2) for unit in (2, 3)}
-    saved = save(keys_own, attn_out, chain)
     keys_near = flip(saved, "ctx", 1)
     keys_side = flip(saved, "ctx", 2)
     keys = [saved, keys_near, keys_side, flip(keys_near, "ctx", 2)]
@@ -750,7 +752,8 @@
     wide_rows(2, arriving[2])
     wide_rows(3, arriving[3])
     begin(2, 3)
-    chain.wait(spots, first_pos, lse_rows)
+    near_places, last_places = places[:-1], places[-1:]
+    chain.wait(spots, first_pos, lse_rows, near_places, last_places)
     half(0)
     half(1)
     row_parts, grad_parts = collect([stacked[unit] for unit in range(planes)], chain)
@@ -759,7 +762,7 @@
     half(2)
     half(3)
     probs = probs_of(
-        places[:-1], first_pos, queries, lse_rows, keys[:-1], key_count, chain
+        near_places, first_pos, queries, lse_rows, keys[:-1], key_count, chain
     )
     chain.wait(from_second[0], from_second[1])
     centre(2)
@@ -794,7 +797,7 @@
     *parts, resid_rows = attn_grad(spots, blocks, w_out, square, chain)
     d_attn = [flip(part, "ctx", rel) if rel else part for rel, part in enumerate(parts)]
     last_probs = probs_of(
-        places[-1:], first_pos, queries, lse_rows, keys[-1:], key_count, chain
+        last_places, first_pos, queries, lse_rows, keys[-1:], key_count, chain
     )
     grad_w_out = out_weight_grad(outs, resid_rows, heads, chain)
     grad_queries = attend(probs, last_probs, attn_out, d_attn, keys, values, key_count, chain)

time: 238 us -> 233 us (0.979)
  waiting for transfers between devices: 56 us -> 52.7 us
    ppermute x50, waiting for transfers between devices: 56 us -> 52.7 us  [flip(): return lax.ppermute(block, axis, [(at, at ^ mask) for at in range(count)])]
    pallas_call x30, Pallas kernels: 108 us -> 106 us  [apply(): *results, link = run(*operands, *after.links)]
    unnamed x120 -> x118, local copies, waits for them, and re-layouts: 18.5 us -> 19.8 us
  transfers between devices with their start and end apart: 50 -> 50, of which waited for: 14 -> 15; matrix products, arithmetic and copies ran while one was open for 0% -> 0% of each run, Pallas kernels for 41% -> 40%
where the time goes in v3:
time: 233 us
  Pallas kernels  106 us (45%)
  waiting for transfers between devices  52.7 us (23%)
  starting transfers between devices  51.8 us (22%)
  local copies, waits for them, and re-layouts  20.6 us (9%)
    pallas_call x30, Pallas kernels, apply(): *results, link = run(*operands, *after.links)  106 us
    ppermute x50, waiting for transfers between devices, flip(): return lax.ppermute(block, axis, [(at, at ^ mask) for at in range(count)])  52.7 us
    ppermute x50, starting transfers between devices, flip(): return lax.ppermute(block, axis, [(at, at ^ mask) for at in range(count)])  51.8 us
    unnamed x118, local copies, waits for them, and re-layouts  19.8 us
  transfers between devices with their start and end apart: 50, of which 15 were waited for; matrix products, arithmetic and copies ran while one was open for 0% of the time, Pallas kernels for 40%

profile of v3, /device:TPU:0, one launch (start us, length us, event | category | flops | bytes accessed | tf_op | source)
XLA Modules:
  0.0 232.7 jit_solution(3307190928240345826)
XLA Ops:
  1.2 1.8 arrange.1
  3.0 3.0 %collective-permute-start.1 = (f32[32,2048]{1,0:T(8,128)}, f32[32,2048]{1,0:T(8,128)}, u32[]{:S(2)}, u32[]{:S(2)}) collective-permute-start(f32[32,2048]{1,0:T(8,128)} %get-tuple-element.94.refs_0_), channel_id=1, source_target_pairs={{0,8},{4,12},{8,0},{12,4},{16,24},{20,28},{24,16},{28,20},{1,9},{5... | collective-permute-start | bytes 786440 | tf_op jit(solution)/shard_map/ppermute | solution.py:30
  6.1 2.0 save.1
  8.0 4.6 %collective-permute-done.1.refs_0_ = f32[32,2048]{1,0:T(8,128)} collective-permute-done((f32[32,2048]{1,0:T(8,128)}, f32[32,2048]{1,0:T(8,128)}, u32[]{:S(2)}, u32[]{:S(2)}) %collective-permute-start.1) | collective-permute-done | bytes 262176 | tf_op jit(solution)/shard_map/ppermute | solution.py:30
  12.7 1.7 collective-permute-start.4
  14.3 1.5 collective-permute-start.5
  15.9 2.6 %collective-permute-start.3 = (f32[32,2048]{1,0:T(8,128)}, f32[32,2048]{1,0:T(8,128)}, u32[]{:S(2)}, u32[]{:S(2)}) collective-permute-start(f32[32,2048]{1,0:T(8,128)} %ordered.8), channel_id=1, source_target_pairs={{0,16},{4,20},{8,24},{12,28},{16,0},{20,4},{24,8},{28,12},{1,17},{... | collective-permute-start | bytes 786440 | tf_op jit(solution)/shard_map/ppermute | solution.py:30
  20.5 13.9 %partial.2 = (f32[32,5504]{1,0:T(8,128)}, f32[32,5504]{1,0:T(8,128)}, f32[64,2048]{1,0:T(8,128)}, f32[32,5504]{1,0:T(8,128)}, f32[32,5504]{1,0:T(8,128)}, /*index=5*/f32[64,2048]{1,0:T(8,128)}, f32[8,128]{1,0:T(8,128)}) custom-call(f32[32,2048]{1,0:T(8,128)} %get-tuple-element.93.refs_0_.refs_1_, f32[32,2048]{1,0:T(8,128)} %copy-done.46, ...), custom_call_target="tpu_custom_call" | custom-call | flops 16911433728 | bytes 88080384 | tf_op jit(solution)/shard_map/partial/pallas_call | solution.py:93
  34.4 3.1 %collective-permute-done.3.refs_0_ = f32[32,2048]{1,0:T(8,128)} collective-permute-done((f32[32,2048]{1,0:T(8,128)}, f32[32,2048]{1,0:T(8,128)}, u32[]{:S(2)}, u32[]{:S(2)}) %collective-permute-start.3) | collective-permute-done | bytes 262176 | tf_op jit(solution)/shard_map/ppermute | solution.py:30
  41.8 13.9 %partial.3 = (f32[32,5504]{1,0:T(8,128)}, f32[32,5504]{1,0:T(8,128)}, f32[64,2048]{1,0:T(8,128)}, f32[32,5504]{1,0:T(8,128)}, f32[32,5504]{1,0:T(8,128)}, /*index=5*/f32[64,2048]{1,0:T(8,128)}, f32[8,128]{1,0:T(8,128)}) custom-call(f32[32,2048]{1,0:T(8,128)} %ordered.9.refs_0_, f32[32,2048]{1,0:T(8,128)} %copy-done.48, f32[32,2048]{1,0:T(8,128)} %ordered.10.refs_2_, ...), custom_call_target="tpu_custom_call" | custom-call | flops 16911433728 | bytes 88080384 | tf_op jit(solution)/shard_map/partial/pallas_call | solution.py:93
  57.1 1.5 collective-permute-start.15
  60.2 2.6 %fold.4 = (f32[16,5504]{1,0:T(8,128)S(1)}, f32[16,5504]{1,0:T(8,128)}, f32[8,128]{1,0:T(8,128)S(1)}) custom-call(f32[32,5504]{1,0:T(8,128)S(1)} %copy-done.7, f32[32,5504]{1,0:T(8,128)} %collective-permute-done.10.refs_1_, f32[8,128]{1,0:T(8,128)S(1)} %copy-done.16, s32[8]{0:T(128)S(1)} %broadcast_xor_fusion.refs_3_.refs_0_, s32[1]{0:T(128)} %bitcast.10.refs_4_.refs_1_, ...), custom_call_target="tpu_custom_call" | custom-call | flops 704512 | bytes 8454144 | tf_op jit(solution)/shard_map/fold/pallas_call | solution.py:93
  65.6 3.7 %collect.1 = (bf16[1024,768]{1,0:T(8,128)(2,1)}, bf16[768,1024]{1,0:T(8,128)(2,1)}, f32[8,128]{1,0:T(8,128)}) custom-call(f32[64,2048]{1,0:T(8,128)} %get-tuple-element.97.refs_0_, f32[64,2048]{1,0:T(8,128)} %get-tuple-element.98.refs_1_, f32[64,2048]{1,0:T(8,128)} %get-tuple-element.101.refs_2_, f32[64,2048]{1,0:T(8,128)} %get-tuple-element.102.refs_3_, ...), custom_call_target="tpu_custom_call" | custom-call | bytes 16777216 | tf_op jit(solution)/shard_map/collect/pallas_call | solution.py:93
  69.3 12.5 %collective-permute-done.11.refs_1_ = f32[16,5504]{1,0:T(8,128)S(1)} collective-permute-done((f32[16,5504]{1,0:T(8,128)}, f32[16,5504]{1,0:T(8,128)S(1)}, u32[]{:S(2)}, u32[]{:S(2)}) %collective-permute-start.11) | collective-permute-done | bytes 352288 | tf_op jit(solution)/shard_map/ppermute | solution.py:30
  85.5 1.5 collective-permute-start.12
  90.3 1.6 collective-permute-start.18
  92.4 3.4 %probs.2 = (f32[256,3072]{1,0:T(8,128)S(1)}, f32[8,128]{1,0:T(8,128)S(1)}) custom-call(s32[3]{0:T(128)S(1)} %bitcast.14, s32[1]{0:T(128)} %bitcast.10.refs_4_.refs_1_, f32[64,512]{1,0:T(8,128)S(1)} %copy-done.28, f32[256,1]{1,0:T(8,128)S(1)} %reshape.20.refs_5_.refs_3_, f32[1280,128]{1,0:T(8,128)S(1)} %copy-done.20, f32[1280,128]{1,0:T(8,128)S(1)} %copy-done.1, ...), custom_call_target="tpu_custom_call" | custom-call | flops 4831838208 | bytes 12582912 | tf_op jit(solution)/shard_map/probs/pallas_call | solution.py:93
  95.8 1.7 copy-done.36
  97.5 2.0 collective-permute-done.20.refs_4_.refs_1_
  99.5 2.1 collective-permute-done.19.refs_1_
  107.5 5.6 %collective-permute-done.21.refs_3_.refs_1_ = f32[16,5504]{1,0:T(8,128)S(1)} collective-permute-done((f32[16,5504]{1,0:T(8,128)S(1)}, f32[16,5504]{1,0:T(8,128)S(1)}, u32[]{:S(2)}, u32[]{:S(2)}) %collective-permute-start.21) | collective-permute-done | bytes 352288 | tf_op jit(solution)/shard_map/ppermute | solution.py:30
  115.7 6.5 %collective-permute-done.14.refs_3_ = f32[16,5504]{1,0:T(8,128)S(1)} collective-permute-done((f32[16,5504]{1,0:T(8,128)S(1)}, f32[16,5504]{1,0:T(8,128)S(1)}, u32[]{:S(2)}, u32[]{:S(2)}) %collective-permute-start.14) | collective-permute-done | bytes 352288 | tf_op jit(solution)/shard_map/ppermute | solution.py:30
  123.0 5.6 %normed.4 = (f32[32,1152]{1,0:T(8,128)S(1)}, f32[32,1152]{1,0:T(8,128)S(1)}, bf16[2,64,5376]{2,1,0:T(8,128)(2,1)S(1)}, f32[8,128]{1,0:T(8,128)S(1)}) custom-call(f32[16,5504]{1,0:T(8,128)S(1)} %get-tuple-element.114.refs_0_, f32[16,5504]{1,0:T(8,128)S(1)} %collective-permute-done.12.refs_3_.refs_1_, f32[16,5504]{1,0:T(8,128)S(1)} %collective-permute-done.13.refs_2_, ...), custom_call_target="tpu_custom_call" | custom-call | flops 5637144576 | bytes 58720256 | tf_op jit(solution)/shard_map/normed/pallas_call | solution.py:93
  129.7 2.2 collective-permute-done.22.refs_2_
  133.4 6.0 %collective-permute-done.23.refs_3_ = f32[16,5504]{1,0:T(8,128)S(1)} collective-permute-done((f32[16,5504]{1,0:T(8,128)S(1)}, f32[16,5504]{1,0:T(8,128)S(1)}, u32[]{:S(2)}, u32[]{:S(2)}) %collective-permute-start.23) | collective-permute-done | bytes 352288 | tf_op jit(solution)/shard_map/ppermute | solution.py:30
  139.4 2.0 collective-permute-start.26
  141.4 5.6 %normed.5 = (f32[32,1152]{1,0:T(8,128)S(1)}, f32[32,1152]{1,0:T(8,128)S(1)}, bf16[2,64,5376]{2,1,0:T(8,128)(2,1)S(1)}, f32[8,128]{1,0:T(8,128)S(1)}) custom-call(f32[16,5504]{1,0:T(8,128)S(1)} %get-tuple-element.130.refs_0_, f32[16,5504]{1,0:T(8,128)S(1)} %collective-permute-done.20.refs_4_.refs_1_, f32[16,5504]{1,0:T(8,128)S(1)} %collective-permute-done.22.refs_2_, ...), custom_call_target="tpu_custom_call" | custom-call | flops 5637144576 | bytes 58720256 | tf_op jit(solution)/shard_map/normed/pallas_call | solution.py:93
  150.3 5.6 %normed.6 = (f32[32,1152]{1,0:T(8,128)S(1)}, f32[32,1152]{1,0:T(8,128)S(1)}, bf16[2,64,5376]{2,1,0:T(8,128)(2,1)S(1)}, f32[8,128]{1,0:T(8,128)S(1)}) custom-call(f32[16,5504]{1,0:T(8,128)S(1)} %get-tuple-element.132.refs_0_, f32[16,5504]{1,0:T(8,128)S(1)} %collective-permute-done.21.refs_3_.refs_1_, f32[16,5504]{1,0:T(8,128)S(1)} %collective-permute-done.25.refs_2_, ...), custom_call_target="tpu_custom_call" | custom-call | flops 5637144576 | bytes 58720256 | tf_op jit(solution)/shard_map/normed/pallas_call | solution.py:93
  157.1 2.5 %collective-permute-done.29.refs_3_ = f32[16,5504]{1,0:T(8,128)S(1)} collective-permute-done((f32[16,5504]{1,0:T(8,128)S(1)}, f32[16,5504]{1,0:T(8,128)S(1)}, u32[]{:S(2)}, u32[]{:S(2)}) %collective-permute-start.29) | collective-permute-done | bytes 352288 | tf_op jit(solution)/shard_map/ppermute | solution.py:30
  159.5 5.6 %normed.7 = (f32[32,1152]{1,0:T(8,128)S(1)}, f32[32,1152]{1,0:T(8,128)S(1)}, bf16[2,64,5376]{2,1,0:T(8,128)(2,1)S(1)}, f32[8,128]{1,0:T(8,128)S(1)}) custom-call(f32[16,5504]{1,0:T(8,128)S(1)} %get-tuple-element.136.refs_0_, f32[16,5504]{1,0:T(8,128)S(1)} %collective-permute-done.24.refs_7_.refs_1_, f32[16,5504]{1,0:T(8,128)S(1)} %collective-permute-done.28.refs_2_, ...), custom_call_target="tpu_custom_call" | custom-call | flops 5637144576 | bytes 58720256 | tf_op jit(solution)/shard_map/normed/pallas_call | solution.py:93
  166.3 2.0 collective-permute-start.46
  168.2 3.4 %collective-permute-start.33 = (f32[32,1152]{1,0:T(8,128)S(1)}, f32[32,1152]{1,0:T(8,128)S(1)}, u32[]{:S(2)}, u32[]{:S(2)}) collective-permute-start(f32[32,1152]{1,0:T(8,128)S(1)} %get-tuple-element.157), channel_id=1, source_target_pairs={{0,8},{4,12},{8,0},{12,4},{16,24},{20,28},{24,16},{28,20},{1,9},{5... | collective-permute-start | bytes 442376 | tf_op jit(solution)/shard_map/ppermute | solution.py:30
  171.7 2.0 collective-permute-start.34
  173.7 1.6 collective-permute-start.35
  175.2 6.9 %weight.3 = (f32[1024,1792]{1,0:T(8,128)}, f32[8,128]{1,0:T(8,128)}) custom-call(bf16[1024,768]{1,0:T(8,128)(2,1)} %get-tuple-element.110.refs_0_, bf16[2,64,5376]{2,1,0:T(8,128)(2,1)} %copy-done.32, bf16[2,64,5376]{2,1,0:T(8,128)(2,1)} %copy-done.31, bf16[2,64,5376]{2,1,0:T(8,128)(2,1)} %copy-done.33, bf16[2,64,5376]{2,1,0:T(8,128)(2,1)} %copy-done.34, ...), custom_call_target="tpu_custom_call" | custom-call | flops 11274289152 | bytes 29360128 | tf_op jit(solution)/shard_map/weight/pallas_call | solution.py:93
  183.4 1.9 collective-permute-done.34.refs_5_
  186.0 1.9 finish.1
  187.9 2.3 collective-permute-start.40
  190.2 1.8 collective-permute-start.42
  192.0 1.5 collective-permute-start.44
  193.5 7.0 %weight.4 = (f32[1024,1792]{1,0:T(8,128)}, f32[8,128]{1,0:T(8,128)}) custom-call(bf16[1024,768]{1,0:T(8,128)(2,1)} %get-tuple-element.110.refs_0_, bf16[2,64,5376]{2,1,0:T(8,128)(2,1)} %copy-done.32, bf16[2,64,5376]{2,1,0:T(8,128)(2,1)} %copy-done.31, bf16[2,64,5376]{2,1,0:T(8,128)(2,1)} %copy-done.33, bf16[2,64,5376]{2,1,0:T(8,128)(2,1)} %copy-done.34, ...), custom_call_target="tpu_custom_call" | custom-call | flops 11274289152 | bytes 29360128 | tf_op jit(solution)/shard_map/weight/pallas_call | solution.py:93
  201.2 1.9 collective-permute-done.42.refs_0_
  204.4 7.2 %weight.5 = (f32[1792,1024]{1,0:T(8,128)}, f32[8,128]{1,0:T(8,128)}) custom-call(bf16[768,1024]{1,0:T(8,128)(2,1)} %get-tuple-element.163.refs_0_, bf16[2,64,5376]{2,1,0:T(8,128)(2,1)} %copy-done.32, bf16[2,64,5376]{2,1,0:T(8,128)(2,1)} %copy-done.31, bf16[2,64,5376]{2,1,0:T(8,128)(2,1)} %copy-done.33, bf16[2,64,5376]{2,1,0:T(8,128)(2,1)} %copy-done.34, ...), custom_call_target="tpu_custom_call" | custom-call | flops 11274289152 | bytes 29360128 | tf_op jit(solution)/shard_map/weight/pallas_call | solution.py:93
  212.6 3.9 %attn_grad.1 = (f32[64,512]{1,0:T(8,128)}, f32[64,512]{1,0:T(8,128)}, f32[64,512]{1,0:T(8,128)}, f32[64,512]{1,0:T(8,128)}, f32[256,1024]{1,0:T(8,128)}, /*index=5*/f32[8,128]{1,0:T(8,128)}) custom-call(s32[8]{0:T(128)} %copy-done.19, f32[512,1024]{1,0:T(8,128)} %refs_1_.5, f32[32,1024]{1,0:T(8,128)} %get-tuple-element.91.refs_2_, f32[32,1024]{1,0:T(8,128)} %copy-done.51, ...), custom_call_target="tpu_custom_call" | custom-call | flops 3221225472 | bytes 8388608 | tf_op jit(solution)/shard_map/attn_grad/pallas_call | solution.py:93
  217.7 1.5 collective-permute-start.48
  221.8 1.9 probs.3
  223.8 2.9 %out_weight.1 = (f32[512,1024]{1,0:T(8,128)}, f32[8,128]{1,0:T(8,128)S(1)}) custom-call(f32[1280,128]{1,0:T(8,128)S(1)} %copy-done.21, f32[1280,128]{1,0:T(8,128)S(1)} %copy-done.1, f32[1280,128]{1,0:T(8,128)S(1)} %copy-done.3, f32[1280,128]{1,0:T(8,128)S(1)} %copy-done.24, f32[256,1024]{1,0:T(8,128)S(1)} %copy-done.35, f32[8,128]{1,0:T(8,128)S(1)} %get-tuple-element.170.refs_5_), custom_call_target="tpu_custom_call" | custom-call | flops 3221225472 | bytes 8388608 | tf_op jit(solution)/shard_map/out_weight/pallas_call | solution.py:93
  226.8 5.9 %attend.1 = (f32[64,512]{1,0:T(8,128)}, f32[8,128]{1,0:T(8,128)}) custom-call(f32[256,3072]{1,0:T(8,128)S(1)} %copy-done.37, f32[256,1024]{1,0:T(8,128)S(1)} %get-tuple-element.173.refs_1_, f32[64,512]{1,0:T(8,128)S(1)} %copy-done.13, f32[64,512]{1,0:T(8,128)S(1)} %copy-done.38, f32[64,512]{1,0:T(8,128)S(1)} %collective-permute-done.47.refs_4_, ...), custom_call_target="tpu_custom_call" | custom-call | flops 6442450944 | bytes 29360128 | tf_op jit(solution)/shard_map/attend/pallas_call | solution.py:93
  (214 shorter events, 46.2 us)
Async XLA Ops:
  3.0 9.6 %collective-permute-start.1 = (f32[32,2048]{1,0:T(8,128)}, f32[32,2048]{1,0:T(8,128)}, u32[]{:S(2)}, u32[]{:S(2)}) collective-permute-start(f32[32,2048]{1,0:T(8,128)} %get-tuple-element.94.refs_0_), channel_id=1, source_target_pairs={{0,8},{4,12},{8,0},{12,4},{16,24},{20,28},{24,16},{28,20},{1,9},{5... | collective-permute-start | bytes 786440 | tf_op jit(solution)/shard_map/ppermute | solution.py:30
  6.1 12.4 %collective-permute-start = (f32[32,2048]{1,0:T(8,128)}, f32[32,2048]{1,0:T(8,128)S(1)}, u32[]{:S(2)}, u32[]{:S(2)}) collective-permute-start(f32[32,2048]{1,0:T(8,128)} %get-tuple-element.93.refs_0_.refs_1_), channel_id=1, source_target_pairs={{0,4},{4,0},{8,12},{12,8},{16,20},{20,16},{24,28},{28,24},{1,5},{5... | collective-permute-start | bytes 786440 | tf_op jit(solution)/shard_map/ppermute | solution.py:30
  12.7 7.1 %collective-permute-start.2 = (f32[32,2048]{1,0:T(8,128)}, f32[32,2048]{1,0:T(8,128)S(1)}, u32[]{:S(2)}, u32[]{:S(2)}) collective-permute-start(f32[32,2048]{1,0:T(8,128)} %ordered.7.refs_2_.refs_1_), channel_id=1, source_target_pairs={{0,4},{4,0},{8,12},{12,8},{16,20},{20,16},{24,28},{28,24},{1,5},{5... | collective-permute-start | bytes 786440 | tf_op jit(solution)/shard_map/ppermute | solution.py:30
  12.7 24.8 %collective-permute-start.4 = (f32[1280,128]{1,0:T(8,128)}, f32[1280,128]{1,0:T(8,128)S(1)}, u32[]{:S(2)}, u32[]{:S(2)}) collective-permute-start(f32[1280,128]{1,0:T(8,128)} %get-tuple-element.100.refs_4_.refs_0_.refs_7_), channel_id=1, source_target_pairs={{0,1},{1,0},{2,3},{3,2},{4,5},{5,4},{6,7},{7,6},{8,9},{9,8},{10,11... | collective-permute-start | bytes 1966088 | tf_op jit(solution)/shard_map/ppermute | solution.py:30
  14.3 23.1 %collective-permute-start.5 = (f32[1280,128]{1,0:T(8,128)}, f32[1280,128]{1,0:T(8,128)S(1)}, u32[]{:S(2)}, u32[]{:S(2)}) collective-permute-start(f32[1280,128]{1,0:T(8,128)} %get-tuple-element.100.refs_4_.refs_0_.refs_7_), channel_id=1, source_target_pairs={{0,2},{1,3},{2,0},{3,1},{4,6},{5,7},{6,4},{7,5},{8,10},{9,11},{10,... | collective-permute-start | bytes 1966088 | tf_op jit(solution)/shard_map/ppermute | solution.py:30
  15.9 21.6 %collective-permute-start.3 = (f32[32,2048]{1,0:T(8,128)}, f32[32,2048]{1,0:T(8,128)}, u32[]{:S(2)}, u32[]{:S(2)}) collective-permute-start(f32[32,2048]{1,0:T(8,128)} %ordered.8), channel_id=1, source_target_pairs={{0,16},{4,20},{8,24},{12,28},{16,0},{20,4},{24,8},{28,12},{1,17},{... | collective-permute-start | bytes 786440 | tf_op jit(solution)/shard_map/ppermute | solution.py:30
  18.5 20.2 %collective-permute-start.7 = (f32[32,2048]{1,0:T(8,128)}, f32[32,2048]{1,0:T(8,128)}, u32[]{:S(2)}, u32[]{:S(2)}) collective-permute-start(f32[32,2048]{1,0:T(8,128)} %ordered.8), channel_id=1, source_target_pairs={{0,24},{4,28},{8,16},{12,20},{16,8},{20,12},{24,0},{28,4},{1,25},{... | collective-permute-start | bytes 786440 | tf_op jit(solution)/shard_map/ppermute | solution.py:30
  39.2 24.9 %collective-permute-start.9 = (f32[32,5504]{1,0:T(8,128)}, f32[32,5504]{1,0:T(8,128)S(1)}, u32[]{:S(2)}, u32[]{:S(2)}) collective-permute-start(f32[32,5504]{1,0:T(8,128)} %get-tuple-element.104), channel_id=1, source_target_pairs={{0,2},{1,3},{2,0},{3,1},{4,6},{5,7},{6,4},{7,5},{8,10},{9,11},{10,... | collective-permute-start | bytes 2113544 | tf_op jit(solution)/shard_map/ppermute | solution.py:30
  39.7 19.8 %collective-permute-start.10 = (f32[32,5504]{1,0:T(8,128)}, f32[32,5504]{1,0:T(8,128)}, u32[]{:S(2)}, u32[]{:S(2)}) collective-permute-start(f32[32,5504]{1,0:T(8,128)} %get-tuple-element.106), channel_id=1, source_target_pairs={{0,1},{1,0},{2,3},{3,2},{4,5},{5,4},{6,7},{7,6},{8,9},{9,8},{10,11... | collective-permute-start | bytes 2113544 | tf_op jit(solution)/shard_map/ppermute | solution.py:30
  55.7 33.1 %collective-permute-start.16 = (f32[32,5504]{1,0:T(8,128)}, f32[32,5504]{1,0:T(8,128)}, u32[]{:S(2)}, u32[]{:S(2)}) collective-permute-start(f32[32,5504]{1,0:T(8,128)} %get-tuple-element.118), channel_id=1, source_target_pairs={{0,1},{1,0},{2,3},{3,2},{4,5},{5,4},{6,7},{7,6},{8,9},{9,8},{10,11... | collective-permute-start | bytes 2113544 | tf_op jit(solution)/shard_map/ppermute | solution.py:30
  57.1 33.1 %collective-permute-start.15 = (f32[32,5504]{1,0:T(8,128)}, f32[32,5504]{1,0:T(8,128)S(1)}, u32[]{:S(2)}, u32[]{:S(2)}) collective-permute-start(f32[32,5504]{1,0:T(8,128)} %get-tuple-element.116), channel_id=1, source_target_pairs={{0,2},{1,3},{2,0},{3,1},{4,6},{5,7},{6,4},{7,5},{8,10},{9,11},{10,... | collective-permute-start | bytes 2113544 | tf_op jit(solution)/shard_map/ppermute | solution.py:30
  63.5 18.2 %collective-permute-start.11 = (f32[16,5504]{1,0:T(8,128)}, f32[16,5504]{1,0:T(8,128)S(1)}, u32[]{:S(2)}, u32[]{:S(2)}) collective-permute-start(f32[16,5504]{1,0:T(8,128)} %get-tuple-element.112), channel_id=1, source_target_pairs={{0,2},{1,3},{2,0},{3,1},{4,6},{5,7},{6,4},{7,5},{8,10},{9,11},{10,... | collective-permute-start | bytes 1056776 | tf_op jit(solution)/shard_map/ppermute | solution.py:30
  64.9 22.2 %collective-permute-start.17 = (f32[16,5504]{1,0:T(8,128)}, f32[16,5504]{1,0:T(8,128)}, u32[]{:S(2)}, u32[]{:S(2)}) collective-permute-start(f32[16,5504]{1,0:T(8,128)} %get-tuple-element.120), channel_id=1, source_target_pairs={{0,1},{1,0},{2,3},{3,2},{4,5},{5,4},{6,7},{7,6},{8,9},{9,8},{10,11... | collective-permute-start | bytes 1056776 | tf_op jit(solution)/shard_map/ppermute | solution.py:30
  85.5 12.0 %collective-permute-start.12 = (f32[16,5504]{1,0:T(8,128)S(1)}, f32[16,5504]{1,0:T(8,128)S(1)}, u32[]{:S(2)}, u32[]{:S(2)}) collective-permute-start(f32[16,5504]{1,0:T(8,128)S(1)} %get-tuple-element.114.refs_0_), channel_id=1, source_target_pairs={{0,2},{1,3},{2,0},{3,1},{4,6},{5,7},{6,4},{7,5},{8,10},{9,11},{10,... | collective-permute-start | bytes 1056776 | tf_op jit(solution)/shard_map/ppermute | solution.py:30
  88.3 11.2 %collective-permute-start.20 = (f32[16,5504]{1,0:T(8,128)S(1)}, f32[16,5504]{1,0:T(8,128)S(1)}, u32[]{:S(2)}, u32[]{:S(2)}) collective-permute-start(f32[16,5504]{1,0:T(8,128)S(1)} %get-tuple-element.130.refs_0_), channel_id=1, source_target_pairs={{0,1},{1,0},{2,3},{3,2},{4,5},{5,4},{6,7},{7,6},{8,9},{9,8},{10,11... | collective-permute-start | bytes 1056776 | tf_op jit(solution)/shard_map/ppermute | solution.py:30
  90.3 15.7 %collective-permute-start.18 = (f32[16,5504]{1,0:T(8,128)S(1)}, f32[16,5504]{1,0:T(8,128)S(1)}, u32[]{:S(2)}, u32[]{:S(2)}) collective-permute-start(f32[16,5504]{1,0:T(8,128)S(1)} %get-tuple-element.125), channel_id=1, source_target_pairs={{0,1},{1,0},{2,3},{3,2},{4,5},{5,4},{6,7},{7,6},{8,9},{9,8},{10,11... | collective-permute-start | bytes 1056776 | tf_op jit(solution)/shard_map/ppermute | solution.py:30
  91.8 9.8 %collective-permute-start.19 = (f32[16,5504]{1,0:T(8,128)S(1)}, f32[16,5504]{1,0:T(8,128)S(1)}, u32[]{:S(2)}, u32[]{:S(2)}) collective-permute-start(f32[16,5504]{1,0:T(8,128)S(1)} %get-tuple-element.127), channel_id=1, source_target_pairs={{0,2},{1,3},{2,0},{3,1},{4,6},{5,7},{6,4},{7,5},{8,10},{9,11},{10,... | collective-permute-start | bytes 1056776 | tf_op jit(solution)/shard_map/ppermute | solution.py:30
  101.9 11.2 %collective-permute-start.21 = (f32[16,5504]{1,0:T(8,128)S(1)}, f32[16,5504]{1,0:T(8,128)S(1)}, u32[]{:S(2)}, u32[]{:S(2)}) collective-permute-start(f32[16,5504]{1,0:T(8,128)S(1)} %get-tuple-element.132.refs_0_), channel_id=1, source_target_pairs={{0,2},{1,3},{2,0},{3,1},{4,6},{5,7},{6,4},{7,5},{8,10},{9,11},{10,... | collective-permute-start | bytes 1056776 | tf_op jit(solution)/shard_map/ppermute | solution.py:30
  103.4 11.5 %collective-permute-start.13 = (f32[16,5504]{1,0:T(8,128)S(1)}, f32[16,5504]{1,0:T(8,128)S(1)}, u32[]{:S(2)}, u32[]{:S(2)}) collective-permute-start(f32[16,5504]{1,0:T(8,128)S(1)} %get-tuple-element.114.refs_0_), channel_id=1, source_target_pairs={{0,1},{1,0},{2,3},{3,2},{4,5},{5,4},{6,7},{7,6},{8,9},{9,8},{10,11... | collective-permute-start | bytes 1056776 | tf_op jit(solution)/shard_map/ppermute | solution.py:30
  104.2 18.0 %collective-permute-start.14 = (f32[16,5504]{1,0:T(8,128)S(1)}, f32[16,5504]{1,0:T(8,128)S(1)}, u32[]{:S(2)}, u32[]{:S(2)}) collective-permute-start(f32[16,5504]{1,0:T(8,128)S(1)} %collective-permute-done.12.refs_3_.refs_1_), channel_id=1, source_target_pairs={{0,1},{1,0},{2,3},{3,2},{4,5},{5,4},{6,7},{7,6},{8,9},{9,8},{10,11... | collective-permute-start | bytes 1056776 | tf_op jit(solution)/shard_map/ppermute | solution.py:30
  105.5 60.8 %collective-permute-start.37 = (f32[1024,128]{1,0:T(8,128)S(1)}, f32[1024,128]{1,0:T(8,128)}, u32[]{:S(2)}, u32[]{:S(2)}) collective-permute-start(f32[1024,128]{1,0:T(8,128)S(1)} %bitcast.19), channel_id=1, source_target_pairs={{0,2},{1,3},{2,0},{3,1},{4,6},{5,7},{6,4},{7,5},{8,10},{9,11},{10,... | collective-permute-start | bytes 1572872 | tf_op jit(solution)/shard_map/ppermute | solution.py:30
  106.0 25.9 %collective-permute-start.22 = (f32[16,5504]{1,0:T(8,128)S(1)}, f32[16,5504]{1,0:T(8,128)S(1)}, u32[]{:S(2)}, u32[]{:S(2)}) collective-permute-start(f32[16,5504]{1,0:T(8,128)S(1)} %get-tuple-element.130.refs_0_), channel_id=1, source_target_pairs={{0,2},{1,3},{2,0},{3,1},{4,6},{5,7},{6,4},{7,5},{8,10},{9,11},{10,... | collective-permute-start | bytes 1056776 | tf_op jit(solution)/shard_map/ppermute | solution.py:30
  113.1 26.3 %collective-permute-start.23 = (f32[16,5504]{1,0:T(8,128)S(1)}, f32[16,5504]{1,0:T(8,128)S(1)}, u32[]{:S(2)}, u32[]{:S(2)}) collective-permute-start(f32[16,5504]{1,0:T(8,128)S(1)} %collective-permute-done.20.refs_4_.refs_1_), channel_id=1, source_target_pairs={{0,2},{1,3},{2,0},{3,1},{4,6},{5,7},{6,4},{7,5},{8,10},{9,11},{10,... | collective-permute-start | bytes 1056776 | tf_op jit(solution)/shard_map/ppermute | solution.py:30
  114.9 34.2 %collective-permute-start.25 = (f32[16,5504]{1,0:T(8,128)S(1)}, f32[16,5504]{1,0:T(8,128)S(1)}, u32[]{:S(2)}, u32[]{:S(2)}) collective-permute-start(f32[16,5504]{1,0:T(8,128)S(1)} %get-tuple-element.132.refs_0_), channel_id=1, source_target_pairs={{0,1},{1,0},{2,3},{3,2},{4,5},{5,4},{6,7},{7,6},{8,9},{9,8},{10,11... | collective-permute-start | bytes 1056776 | tf_op jit(solution)/shard_map/ppermute | solution.py:30
  122.1 17.3 %collective-permute-start.24 = (f32[16,5504]{1,0:T(8,128)S(1)}, f32[16,5504]{1,0:T(8,128)S(1)}, u32[]{:S(2)}, u32[]{:S(2)}) collective-permute-start(f32[16,5504]{1,0:T(8,128)S(1)} %get-tuple-element.136.refs_0_), channel_id=1, source_target_pairs={{0,1},{1,0},{2,3},{3,2},{4,5},{5,4},{6,7},{7,6},{8,9},{9,8},{10,11... | collective-permute-start | bytes 1056776 | tf_op jit(solution)/shard_map/ppermute | solution.py:30
  131.9 25.2 %collective-permute-start.28 = (f32[16,5504]{1,0:T(8,128)S(1)}, f32[16,5504]{1,0:T(8,128)S(1)}, u32[]{:S(2)}, u32[]{:S(2)}) collective-permute-start(f32[16,5504]{1,0:T(8,128)S(1)} %get-tuple-element.136.refs_0_), channel_id=1, source_target_pairs={{0,2},{1,3},{2,0},{3,1},{4,6},{5,7},{6,4},{7,5},{8,10},{9,11},{10,... | collective-permute-start | bytes 1056776 | tf_op jit(solution)/shard_map/ppermute | solution.py:30
  139.4 8.8 %collective-permute-start.27 = (f32[32,1152]{1,0:T(8,128)S(1)}, f32[32,1152]{1,0:T(8,128)S(1)}, u32[]{:S(2)}, u32[]{:S(2)}) collective-permute-start(f32[32,1152]{1,0:T(8,128)S(1)} %get-tuple-element.139), channel_id=1, source_target_pairs={{0,4},{4,0},{8,12},{12,8},{16,20},{20,16},{24,28},{28,24},{1,5},{5... | collective-permute-start | bytes 442376 | tf_op jit(solution)/shard_map/ppermute | solution.py:30
  139.4 10.9 %collective-permute-start.26 = (f32[16,5504]{1,0:T(8,128)S(1)}, f32[16,5504]{1,0:T(8,128)S(1)}, u32[]{:S(2)}, u32[]{:S(2)}) collective-permute-start(f32[16,5504]{1,0:T(8,128)S(1)} %collective-permute-done.21.refs_3_.refs_1_), channel_id=1, source_target_pairs={{0,1},{1,0},{2,3},{3,2},{4,5},{5,4},{6,7},{7,6},{8,9},{9,8},{10,11... | collective-permute-start | bytes 1056776 | tf_op jit(solution)/shard_map/ppermute | solution.py:30
  148.2 8.8 %collective-permute-start.30 = (f32[32,1152]{1,0:T(8,128)S(1)}, f32[32,1152]{1,0:T(8,128)S(1)}, u32[]{:S(2)}, u32[]{:S(2)}) collective-permute-start(f32[32,1152]{1,0:T(8,128)S(1)} %get-tuple-element.144), channel_id=1, source_target_pairs={{0,4},{4,0},{8,12},{12,8},{16,20},{20,16},{24,28},{28,24},{1,5},{5... | collective-permute-start | bytes 442376 | tf_op jit(solution)/shard_map/ppermute | solution.py:30
  149.1 10.4 %collective-permute-start.29 = (f32[16,5504]{1,0:T(8,128)S(1)}, f32[16,5504]{1,0:T(8,128)S(1)}, u32[]{:S(2)}, u32[]{:S(2)}) collective-permute-start(f32[16,5504]{1,0:T(8,128)S(1)} %collective-permute-done.24.refs_7_.refs_1_), channel_id=1, source_target_pairs={{0,2},{1,3},{2,0},{3,1},{4,6},{5,7},{6,4},{7,5},{8,10},{9,11},{10,... | collective-permute-start | bytes 1056776 | tf_op jit(solution)/shard_map/ppermute | solution.py:30
  157.0 14.6 %collective-permute-start.32 = (f32[32,1152]{1,0:T(8,128)S(1)}, f32[32,1152]{1,0:T(8,128)S(1)}, u32[]{:S(2)}, u32[]{:S(2)}) collective-permute-start(f32[32,1152]{1,0:T(8,128)S(1)} %get-tuple-element.151), channel_id=1, source_target_pairs={{0,4},{4,0},{8,12},{12,8},{16,20},{20,16},{24,28},{28,24},{1,5},{5... | collective-permute-start | bytes 442376 | tf_op jit(solution)/shard_map/ppermute | solution.py:30
  166.2 7.4 %collective-permute-start.31 = (f32[32,1152]{1,0:T(8,128)S(1)}, f32[32,1152]{1,0:T(8,128)S(1)}, u32[]{:S(2)}, u32[]{:S(2)}) collective-permute-start(f32[32,1152]{1,0:T(8,128)S(1)} %get-tuple-element.149), channel_id=1, source_target_pairs={{0,4},{4,0},{8,12},{12,8},{16,20},{20,16},{24,28},{28,24},{1,5},{5... | collective-permute-start | bytes 442376 | tf_op jit(solution)/shard_map/ppermute | solution.py:30
  166.2 25.8 %collective-permute-start.36 = (f32[1024,128]{1,0:T(8,128)S(1)}, f32[1024,128]{1,0:T(8,128)S(1)}, u32[]{:S(2)}, u32[]{:S(2)}) collective-permute-start(f32[1024,128]{1,0:T(8,128)S(1)} %bitcast.20), channel_id=1, source_target_pairs={{0,1},{1,0},{2,3},{3,2},{4,5},{5,4},{6,7},{7,6},{8,9},{9,8},{10,11... | collective-permute-start | bytes 1572872 | tf_op jit(solution)/shard_map/ppermute | solution.py:30
  166.3 38.1 %collective-permute-start.46 = (f32[1024,128]{1,0:T(8,128)}, f32[1024,128]{1,0:T(8,128)}, u32[]{:S(2)}, u32[]{:S(2)}) collective-permute-start(f32[1024,128]{1,0:T(8,128)} %collective-permute-done.37.refs_7_.refs_13_), channel_id=1, source_target_pairs={{0,1},{1,0},{2,3},{3,2},{4,5},{5,4},{6,7},{7,6},{8,9},{9,8},{10,11... | collective-permute-start | bytes 1572872 | tf_op jit(solution)/shard_map/ppermute | solution.py:30
  168.2 13.9 %collective-permute-start.33 = (f32[32,1152]{1,0:T(8,128)S(1)}, f32[32,1152]{1,0:T(8,128)S(1)}, u32[]{:S(2)}, u32[]{:S(2)}) collective-permute-start(f32[32,1152]{1,0:T(8,128)S(1)} %get-tuple-element.157), channel_id=1, source_target_pairs={{0,8},{4,12},{8,0},{12,4},{16,24},{20,28},{24,16},{28,20},{1,9},{5... | collective-permute-start | bytes 442376 | tf_op jit(solution)/shard_map/ppermute | solution.py:30
  171.7 13.6 %collective-permute-start.34 = (f32[32,1152]{1,0:T(8,128)S(1)}, f32[32,1152]{1,0:T(8,128)S(1)}, u32[]{:S(2)}, u32[]{:S(2)}) collective-permute-start(f32[32,1152]{1,0:T(8,128)S(1)} %get-tuple-element.158), channel_id=1, source_target_pairs={{0,16},{4,20},{8,24},{12,28},{16,0},{20,4},{24,8},{28,12},{1,17},{... | collective-permute-start | bytes 442376 | tf_op jit(solution)/shard_map/ppermute | solution.py:30
  173.7 11.6 %collective-permute-start.35 = (f32[32,1152]{1,0:T(8,128)S(1)}, f32[32,1152]{1,0:T(8,128)}, u32[]{:S(2)}, u32[]{:S(2)}) collective-permute-start(f32[32,1152]{1,0:T(8,128)S(1)} %get-tuple-element.159), channel_id=1, source_target_pairs={{0,24},{4,28},{8,16},{12,20},{16,8},{20,12},{24,0},{28,4},{1,25},{... | collective-permute-start | bytes 442376 | tf_op jit(solution)/shard_map/ppermute | solution.py:30
  182.2 29.4 %collective-permute-start.38 = (f32[1280,128]{1,0:T(8,128)S(1)}, f32[1280,128]{1,0:T(8,128)S(1)}, u32[]{:S(2)}, u32[]{:S(2)}) collective-permute-start(f32[1280,128]{1,0:T(8,128)S(1)} %copy-done.1), channel_id=1, source_target_pairs={{0,2},{1,3},{2,0},{3,1},{4,6},{5,7},{6,4},{7,5},{8,10},{9,11},{10,... | collective-permute-start | bytes 1966088 | tf_op jit(solution)/shard_map/ppermute | solution.py:30
  187.9 12.6 %collective-permute-start.40 = (f32[32,1024]{1,0:T(8,128)}, f32[32,1024]{1,0:T(8,128)S(1)}, u32[]{:S(2)}, u32[]{:S(2)}) collective-permute-start(f32[32,1024]{1,0:T(8,128)} %get-tuple-element.91.refs_2_), channel_id=1, source_target_pairs={{0,8},{4,12},{8,0},{12,4},{16,24},{20,28},{24,16},{28,20},{1,9},{5... | collective-permute-start | bytes 393224 | tf_op jit(solution)/shard_map/ppermute | solution.py:30
  190.2 12.8 %collective-permute-start.42 = (f32[32,1024]{1,0:T(8,128)}, f32[32,1024]{1,0:T(8,128)S(1)}, u32[]{:S(2)}, u32[]{:S(2)}) collective-permute-start(f32[32,1024]{1,0:T(8,128)} %get-tuple-element.91.refs_2_), channel_id=1, source_target_pairs={{0,16},{4,20},{8,24},{12,28},{16,0},{20,4},{24,8},{28,12},{1,17},{... | collective-permute-start | bytes 393224 | tf_op jit(solution)/shard_map/ppermute | solution.py:30
  192.0 11.7 %collective-permute-start.44 = (f32[32,1024]{1,0:T(8,128)}, f32[32,1024]{1,0:T(8,128)S(1)}, u32[]{:S(2)}, u32[]{:S(2)}) collective-permute-start(f32[32,1024]{1,0:T(8,128)} %get-tuple-element.91.refs_2_), channel_id=1, source_target_pairs={{0,24},{4,28},{8,16},{12,20},{16,8},{20,12},{24,0},{28,4},{1,25},{... | collective-permute-start | bytes 393224 | tf_op jit(solution)/shard_map/ppermute | solution.py:30
  200.5 11.1 %collective-permute-start.39 = (f32[32,1024]{1,0:T(8,128)S(1)}, f32[32,1024]{1,0:T(8,128)S(1)}, u32[]{:S(2)}, u32[]{:S(2)}) collective-permute-start(f32[32,1024]{1,0:T(8,128)S(1)} %copy-done.50), channel_id=1, source_target_pairs={{0,4},{4,0},{8,12},{12,8},{16,20},{20,16},{24,28},{28,24},{1,5},{5... | collective-permute-start | bytes 393224 | tf_op jit(solution)/shard_map/ppermute | solution.py:30
  203.0 8.6 %collective-permute-start.41 = (f32[32,1024]{1,0:T(8,128)}, f32[32,1024]{1,0:T(8,128)S(1)}, u32[]{:S(2)}, u32[]{:S(2)}) collective-permute-start(f32[32,1024]{1,0:T(8,128)} %ordered.11.refs_4_), channel_id=1, source_target_pairs={{0,4},{4,0},{8,12},{12,8},{16,20},{20,16},{24,28},{28,24},{1,5},{5... | collective-permute-start | bytes 393224 | tf_op jit(solution)/shard_map/ppermute | solution.py:30
  203.7 7.9 %collective-permute-start.43 = (f32[32,1024]{1,0:T(8,128)}, f32[32,1024]{1,0:T(8,128)S(1)}, u32[]{:S(2)}, u32[]{:S(2)}) collective-permute-start(f32[32,1024]{1,0:T(8,128)} %ordered.12.refs_6_), channel_id=1, source_target_pairs={{0,4},{4,0},{8,12},{12,8},{16,20},{20,16},{24,28},{28,24},{1,5},{5... | collective-permute-start | bytes 393224 | tf_op jit(solution)/shard_map/ppermute | solution.py:30
  204.4 7.3 %collective-permute-start.45 = (f32[32,1024]{1,0:T(8,128)}, f32[32,1024]{1,0:T(8,128)S(1)}, u32[]{:S(2)}, u32[]{:S(2)}) collective-permute-start(f32[32,1024]{1,0:T(8,128)} %ordered.13.refs_8_), channel_id=1, source_target_pairs={{0,4},{4,0},{8,12},{12,8},{16,20},{20,16},{24,28},{28,24},{1,5},{5... | collective-permute-start | bytes 393224 | tf_op jit(solution)/shard_map/ppermute | solution.py:30
  216.5 10.2 %collective-permute-start.47 = (f32[64,512]{1,0:T(8,128)}, f32[64,512]{1,0:T(8,128)S(1)}, u32[]{:S(2)}, u32[]{:S(2)}) collective-permute-start(f32[64,512]{1,0:T(8,128)} %get-tuple-element.175), channel_id=1, source_target_pairs={{0,1},{1,0},{2,3},{3,2},{4,5},{5,4},{6,7},{7,6},{8,9},{9,8},{10,11... | collective-permute-start | bytes 393224 | tf_op jit(solution)/shard_map/ppermute | solution.py:30
  217.7 9.1 %collective-permute-start.48 = (f32[64,512]{1,0:T(8,128)}, f32[64,512]{1,0:T(8,128)S(1)}, u32[]{:S(2)}, u32[]{:S(2)}) collective-permute-start(f32[64,512]{1,0:T(8,128)} %get-tuple-element.176), channel_id=1, source_target_pairs={{0,2},{1,3},{2,0},{3,1},{4,6},{5,7},{6,4},{7,5},{8,10},{9,11},{10,... | collective-permute-start | bytes 393224 | tf_op jit(solution)/shard_map/ppermute | solution.py:30
  219.2 7.6 %collective-permute-start.49 = (f32[64,512]{1,0:T(8,128)}, f32[64,512]{1,0:T(8,128)S(1)}, u32[]{:S(2)}, u32[]{:S(2)}) collective-permute-start(f32[64,512]{1,0:T(8,128)} %get-tuple-element.177), channel_id=1, source_target_pairs={{0,3},{1,2},{2,1},{3,0},{4,7},{5,6},{6,5},{7,4},{8,11},{9,10},{10,... | collective-permute-start | bytes 393224 | tf_op jit(solution)/shard_map/ppermute | solution.py:30
  (61 other events, 365.0 us)
